TPU v7x, 512 devices: a whole 4x4x16 slice. The times are simulated.
512 devices in a mesh: rep: 16 (over z_lo, x), row: 32 (over z_hi, y, core).
Axes of the slice: x: 4, y: 4, z: 16 (z_hi: 4, z_lo: 4; z = z_hi * 4 + z_lo), core: 2. Of those that a mesh axis runs over, the one named last changes fastest.
Arguments:
- features: bfloat16 [32768, 128], P('row'), may hold values from -6 to 6
- tile_values: bfloat16 [16, 32, 96, 128, 128], P('rep', 'row'), may hold values from 0 to 0.079589844
- tile_counts: int32 [16, 32, 8], P('rep', 'row'), may hold values from 1 to 12, as said below
- tile_columns: int32 [16, 32, 96], P('rep', 'row'), may hold values from 0 to 15, as said below
- weight: bfloat16 [128, 256], replicated, may hold values from -0.5 to 0.5
- node_grad: bfloat16 [32768, 256], P('row'), may hold values from -6 to 6
Outputs:
- output: bfloat16 [32768, 256], P('row')
- weight_grad: float32 [128, 256], replicated
- feature_grad: bfloat16 [32768, 128], P('row')
Inputs may be any that keep to these rules, and one draw needn't show every extreme that they name: `tile_counts`: each entry counts the live tiles of one row block among the 16 column blocks of its replica group; in every draw some node shard of some replica group has 12 in all its 8 row blocks. `tile_columns`: within the live slots of one row block the columns are distinct; slots past a device's total count are not live and hold any column.
All inputs are finite; a program needn't handle non-finite values.
Results may differ from a plain program's by a relative error of at most 0.005.
Values may be sent and summed in bfloat16 or wider, within the bound.
No kernel may reach another device: no remote copies, remote signals or barrier semaphores. Data moves between devices by JAX's collectives and lax.ppermute only.
A program may use at most 64 MiB of HBM per device.

v0:
```python
import math

import jax
import jax.numpy as jnp
from jax import lax
from jax.sharding import PartitionSpec as P


def spread(block, axis, owner):
    block = jnp.where(lax.axis_index(axis) == owner, block, jnp.zeros_like(block))
    return lax.psum(block, axis)


def tile_layout(count_row, slot_total, block_count):
    block_ends = jnp.cumsum(count_row)
    slot_ids = jnp.arange(slot_total, dtype=jnp.int32)
    local_block = jnp.sum((slot_ids[:, None] >= block_ends[None, :]).astype(jnp.int32), axis=1)
    local_block = jnp.minimum(local_block, block_count - 1)
    live_mask = slot_ids < block_ends[block_count - 1]
    return (local_block, live_mask)


def body(features, tile_values, tile_counts, tile_columns, weight, node_grad):
    tile_vals = tile_values[0, 0]
    count_row = tile_counts[0, 0]
    col_row = tile_columns[0, 0]
    rep_size = lax.axis_size("rep")
    row_size = lax.axis_size("row")
    held_count = row_size // rep_size
    rep_index = lax.axis_index("rep")
    row_index = lax.axis_index("row")
    slot_total = tile_vals.shape[0]
    tile_size = tile_vals.shape[1]
    block_count = count_row.shape[0]
    local_rows = features.shape[0]
    feat_width = features.shape[1]
    local_block, live_mask = tile_layout(count_row, slot_total, block_count)
    received = []
    for held_number in range(held_count):
        owner_row = held_number * rep_size + rep_index
        received.append(spread(features, "row", owner_row))
    column_feats = jnp.concatenate(received, axis=0).reshape(
        held_count * block_count, tile_size, feat_width
    )
    picked = column_feats[col_row]
    products = jnp.einsum("tij,tjf->tif", tile_vals, picked, preferred_element_type=jnp.float32)
    row_onehot = (
        (local_block[None, :] == jnp.arange(block_count, dtype=jnp.int32)[:, None])
        & live_mask[None, :]
    ).astype(jnp.float32)
    partial_value = jnp.einsum(
        "bt,tif->bif", row_onehot, products, precision=lax.Precision.HIGHEST
    ).reshape(local_rows, feat_width)
    scaling = 1.0 / math.sqrt(local_rows * row_size)
    aggregate = lax.psum(partial_value, "rep").astype(jnp.bfloat16)
    output = jnp.dot(aggregate, weight, preferred_element_type=jnp.float32).astype(jnp.bfloat16)
    weight_term = jnp.dot(aggregate.T, node_grad, preferred_element_type=jnp.float32)
    weight_grad = lax.psum(weight_term, "row") * scaling
    grad_rows = jnp.dot(node_grad, weight.T, preferred_element_type=jnp.float32).astype(
        jnp.bfloat16
    )
    grad_picked = grad_rows.reshape(block_count, tile_size, feat_width)[local_block]
    backward = jnp.einsum(
        "tji,tjf->tif", tile_vals, grad_picked, preferred_element_type=jnp.float32
    )
    col_onehot = (
        (col_row[None, :] == jnp.arange(held_count * block_count, dtype=jnp.int32)[:, None])
        & live_mask[None, :]
    ).astype(jnp.float32)
    column_terms = jnp.einsum("ct,tif->cif", col_onehot, backward, precision=lax.Precision.HIGHEST)
    column_terms = column_terms.reshape(held_count, local_rows, feat_width)
    owned_part = jnp.zeros((local_rows, feat_width), jnp.bfloat16)
    for held_number in range(held_count):
        owner_row = held_number * rep_size + rep_index
        column_total = lax.psum(column_terms[held_number], "row")
        owned_part = jnp.where(
            owner_row == row_index, column_total.astype(jnp.bfloat16), owned_part
        )
    feature_grad = lax.psum(owned_part.astype(jnp.float32).astype(jnp.bfloat16), "rep")
    return (output, weight_grad, feature_grad)


def solution(mesh):
    placed = (
        P("row", None),
        P("rep", "row", None, None, None),
        P("rep", "row", None),
        P("rep", "row", None),
        P(),
        P("row", None),
    )
    return jax.shard_map(
        body,
        mesh=mesh,
        in_specs=placed,
        out_specs=(P("row", None), P(), P("row", None)),
        check_vma=False,
    )
```

profile of v0, /device:TPU:24, one launch (start us, length us, event | category | flops | bytes accessed | tf_op | source)
XLA Modules:
  0.0 979.8 jit_solution(14018249809832175659)
XLA Ops:
  7.2 1.9 broadcast_select_fusion.1
  9.3 0.8 reduce-window.4
  12.1 1.3 convolution_convert_fusion.1
  13.5 2.8 gather_fusion.1
  16.2 5.7 fusion.7
  22.0 6.7 copy.21
  28.7 4.2 fusion.15
  32.9 0.9 copy.22
  33.8 0.9 copy.23
  34.7 184.0 %all-reduce.14 = (bf16[1024,128]{1,0:T(8,128)(2,1)}, bf16[1024,128]{1,0:T(8,128)(2,1)}) all-reduce(f32[1024,128]{1,0:T(8,128)} %bitcast.49, f32[1024,128]{1,0:T(8,128)} %bitcast.48), channel_id=1, replica_groups=mesh['rep'=16,'row'=32] {'row'}, use_global_device_ids=true, to_apply=%region_7.8 | all-reduce | flops 262144 | bytes 1572864 | tf_op jit(solution)/shard_map/psum | solution.py:75
  218.8 146.1 %all-reduce.12.cloned.1.call-done = (bf16[1024,128]{1,0:T(8,128)(2,1)}, bf16[1024,128]{1,0:T(8,128)(2,1)}) async-done(((bf16[1024,128]{1,0:T(8,128)(2,1)}, bf16[1024,128]{1,0:T(8,128)(2,1)}), (bf16[1024,128]{1,0:T(8,128)(2,1)}, bf16[1024,128]{1,0:T(8,128)(2,1)})) %all-reduce.12.cloned.1.call-update) | async-done | bytes 524304 | tf_op jit(solution)/shard_map/psum | solution.py:11
  364.9 1.9 pad_maximum_fusion
  366.7 3.8 gather_fusion
  370.5 6.9 fusion.4
  377.4 6.7 copy.18
  384.1 4.1 fusion.20
  388.3 0.9 copy.19
  389.2 86.1 %all-reduce.13 = bf16[1024,128]{1,0:T(8,128)(2,1)S(1)} all-reduce(f32[1024,128]{1,0:T(8,128)} %bitcast.50), channel_id=1, replica_groups=mesh['rep'=16,'row'=32] {'rep'}, use_global_device_ids=true, to_apply=%region_4.5 | all-reduce | flops 131072 | bytes 786432 | tf_op jit(solution)/shard_map/psum | solution.py:55
  475.3 2.0 fusion.28
  478.1 1.1 convolution_convert_fusion
  479.2 316.1 %all-reduce.8.cloned.1.call-done = f32[128,256]{1,0:T(8,128)} async-done(((f32[128,256]{1,0:T(8,128)}), f32[128,256]{1,0:T(8,128)}) %all-reduce.8.cloned.1.call-update) | async-done | bytes 131088 | tf_op jit(solution)/shard_map/psum | solution.py:58
  795.3 1.6 broadcast_multiply_fusion
  796.9 174.7 %all-reduce.10.cloned.1.call-done = bf16[1024,128]{1,0:T(8,128)(2,1)} async-done(((bf16[1024,128]{1,0:T(8,128)(2,1)}), bf16[1024,128]{1,0:T(8,128)(2,1)}) %all-reduce.10.cloned.1.call-update) | async-done | bytes 262160 | tf_op jit(solution)/shard_map/psum | solution.py:79
  971.6 1.7 copy.36
  (22 shorter events, 3.0 us)
Async XLA Ops:
  7.2 9.1 copy-start
  7.2 357.7 %all-reduce.12.cloned.1.call-start = ((), (), s32[]{:S(2)}) async-start(), calls=%async_computation.2 | async-start | bytes 1048576 | tf_op jit(solution)/shard_map/psum | solution.py:11
  9.2 786.1 %all-reduce.8.cloned.1.call-start = ((), (), s32[]{:S(2)}) async-start(), calls=%async_computation | async-start | bytes 262144 | tf_op jit(solution)/shard_map/psum | solution.py:58
  22.0 6.7 copy-start.2
  388.3 89.8 %copy-start.1 = (bf16[128,256]{1,0:T(8,128)(2,1)S(1)}, bf16[128,256]{1,0:T(8,128)(2,1)}, u32[]{:S(2)}) copy-start(bf16[128,256]{1,0:T(8,128)(2,1)} %param.10) | copy-start | bytes 196612
  477.3 494.3 %all-reduce.10.cloned.1.call-start = ((), (), s32[]{:S(2)}) async-start(), calls=%async_computation.1 | async-start | bytes 524288 | tf_op jit(solution)/shard_map/psum | solution.py:79
Sparse Core Ops, SparseCore 0:
  11.5 353.3 all-reduce.11
  477.4 317.8 all-reduce.7
  798.8 172.7 all-reduce.9
where the time goes:
time: 981 us; the launch traced here: 980 us
  waiting for transfers between devices  637 us (65%)
  blocking collectives  270 us (28%)
  matrix products  25.3 us (3%)
  local copies, waits for them, and re-layouts  24.9 us (3%)
  between operations  13.9 us (1%)
    psum x1, waiting for transfers between devices, body(): weight_grad = lax.psum(weight_term, 'row') * scaling  316 us
    psum x1, blocking collectives, body(): column_total = lax.psum(column_terms[held_number], 'row')  184 us
    psum x1, waiting for transfers between devices, body(): lax.psum(owned_part.astype(jnp.float32).astype(jnp.bfloat16), 'rep')  175 us
    psum x1, waiting for transfers between devices, spread(): return lax.psum(block, axis)  146 us
    psum x1, blocking collectives, body(): aggregate = lax.psum(partial_value, 'rep').astype(jnp.bfloat16)  86.1 us
  transfers between devices with their start and end apart: 3, of which 3 were waited for; matrix products, arithmetic and copies ran while one was open for 3% of the time, Pallas kernels for 0%

commit v1 on v0

v1 whole, which is shorter than its diff:
```python
import math

import jax
import jax.numpy as jnp
from jax import lax
from jax.experimental import pallas as pl
from jax.experimental.pallas import tpu as pltpu
from jax.sharding import Mesh
from jax.sharding import PartitionSpec as P

REP = ("zl", "x")
ROW = ("zh", "y", "c")
YC = ("y", "c")
F32 = jnp.float32
BF16 = jnp.bfloat16
VMEM = pl.BlockSpec(memory_space=pltpu.VMEM)
SMEM = pl.BlockSpec(memory_space=pltpu.SMEM)
PARAMS = pltpu.CompilerParams(vmem_limit_bytes=40 * 1024 * 1024)

PAIRS = [
    ((zh * 4 + k % 4) * 32 + q + 16 * (k // 4), q * 32 + zh * 8 + k)
    for q in range(16)
    for zh in range(4)
    for k in range(8)
]


def split_high_low(value):
    high = value.astype(BF16)
    return high, (value - high.astype(F32)).astype(BF16)


def backward_kernel(counts, cols, tiles, node_grad, weight, dense, terms, grad_t):
    def clear(b, carry):
        dense[pl.ds(pl.multiple_of(b * 128, 128), 128), :] = jnp.zeros((128, 2048), BF16)
        return carry

    lax.fori_loop(0, 8, clear, 0)
    start = jnp.int32(0)
    for b in range(8):
        count = counts[b]

        def place(i, carry, b=b, start=start):
            slot = start + i
            col = pl.multiple_of(cols[slot] * 128, 128)
            dense[b * 128 : (b + 1) * 128, pl.ds(col, 128)] = tiles[slot]
            return carry

        lax.fori_loop(0, count, place, 0)
        start = start + count
    grad_t[...] = lax.dot_general(
        weight[...], node_grad[...], (((1,), (1,)), ((), ())), preferred_element_type=F32
    ).astype(BF16)
    for k in range(8):
        term = jnp.dot(
            grad_t[...], dense[:, k * 256 : (k + 1) * 256], preferred_element_type=F32
        )
        terms[k] = term.T.astype(BF16)


def forward_kernel(dense, received, partial):
    total = jnp.zeros((128, 128), F32)
    for k in range(8):
        total = total + jnp.dot(
            dense[:, k * 256 : (k + 1) * 256], received[k, 0:256, :], preferred_element_type=F32
        )
    partial[...] = total.astype(BF16)


def aggregate_kernel(rep, scaling, parts, node_grad, column_sum, message):
    total = parts[0].astype(F32)
    for a in range(1, 16):
        total = total + parts[a].astype(F32)
    piece = total.astype(BF16)
    message[:, 0:64, :] = jnp.broadcast_to(piece[None], (16, 64, 128))
    message[:, 64:80, :] = column_sum[...].reshape(16, 16, 128)
    rows = node_grad[pl.ds(pl.multiple_of(rep[0] * 64, 64), 64), :]
    term = lax.dot_general(piece, rows, (((0,), (0,)), ((), ())), preferred_element_type=F32)
    term = term * scaling
    halves = jnp.concatenate(
        [term[:, 0:128].reshape(16, 8, 128), term[:, 128:256].reshape(16, 8, 128)], axis=1
    )
    high, low = split_high_low(halves)
    message[:, 80:96, :] = high
    message[:, 96:112, :] = low


def output_kernel(received, weight, output, column_piece, weight_part):
    for zq in range(4):
        aggregate = received[zq * 4 : zq * 4 + 4, 0:64, :].reshape(256, 128)
        output[zq * 256 : (zq + 1) * 256, :] = jnp.dot(
            aggregate, weight[...], preferred_element_type=F32
        ).astype(BF16)
    for part in range(4):
        total = received[part, 64:80, :].astype(F32)
        for zh in range(1, 4):
            total = total + received[zh * 4 + part, 64:80, :].astype(F32)
        column_piece[part * 16 : (part + 1) * 16, :] = total.astype(BF16)
    total = received[0, 80:96, :].astype(F32) + received[0, 96:112, :].astype(F32)
    for a in range(1, 16):
        total = total + (received[a, 80:96, :].astype(F32) + received[a, 96:112, :].astype(F32))
    weight_part[...] = total


def exchange(block, axes):
    return lax.all_to_all(block, axes, 0, 0)


def broadcast(block, count, axes):
    return exchange(jnp.broadcast_to(block[None], (count, *block.shape)), axes)


def body(features, tile_values, tile_counts, tile_columns, weight, node_grad):
    tiles = tile_values[0, 0]
    rep_index = lax.axis_index(REP)
    scaling = 1.0 / math.sqrt(features.shape[0] * 32)

    quarter = lax.dynamic_slice_in_dim(features, (rep_index % 4) * 256, 256, axis=0)
    quarter = lax.ppermute(quarter, REP + ROW, PAIRS)

    dense, terms = pl.pallas_call(
        backward_kernel,
        out_shape=(
            jax.ShapeDtypeStruct((1024, 2048), BF16),
            jax.ShapeDtypeStruct((8, 256, 128), BF16),
        ),
        in_specs=[SMEM, SMEM, VMEM, VMEM, VMEM],
        out_specs=(VMEM, VMEM),
        scratch_shapes=[pltpu.VMEM((128, 1024), BF16)],
        compiler_params=PARAMS,
        cost_estimate=pl.CostEstimate(
            flops=2 * 128 * 1024 * 2304, bytes_accessed=8 << 20, transcendentals=0
        ),
        name="backward",
    )(tile_counts[0, 0], tile_columns[0, 0], tiles, node_grad, weight)

    received = exchange(
        jnp.concatenate([jnp.broadcast_to(quarter[None], (8, 256, 128)), terms], axis=1), YC
    )

    column_sum = jnp.sum(received[:, 256:].astype(F32), axis=0).astype(BF16)
    column_sum = lax.ppermute(column_sum, REP + ROW, [(d, s) for s, d in PAIRS])

    partial = pl.pallas_call(
        forward_kernel,
        grid=(8,),
        out_shape=jax.ShapeDtypeStruct((1024, 128), BF16),
        in_specs=[
            pl.BlockSpec((128, 2048), lambda b: (b, 0)),
            pl.BlockSpec((8, 512, 128), lambda b: (0, 0, 0)),
        ],
        out_specs=pl.BlockSpec((128, 128), lambda b: (b, 0)),
        compiler_params=PARAMS,
        cost_estimate=pl.CostEstimate(
            flops=2 * 128 * 1024 * 2048, bytes_accessed=6 << 20, transcendentals=0
        ),
        name="forward",
    )(dense, received)
    parts = exchange(partial.reshape(16, 64, 128), REP)

    message = pl.pallas_call(
        lambda rep, *refs: aggregate_kernel(rep, scaling, *refs),
        out_shape=jax.ShapeDtypeStruct((16, 112, 128), BF16),
        in_specs=[SMEM, VMEM, VMEM, VMEM],
        out_specs=VMEM,
        compiler_params=PARAMS,
        name="aggregate",
    )(rep_index.astype(jnp.int32).reshape(1), parts, node_grad, column_sum)
    received = exchange(message, REP)

    output, column_piece, weight_part = pl.pallas_call(
        output_kernel,
        out_shape=(
            jax.ShapeDtypeStruct((1024, 256), BF16),
            jax.ShapeDtypeStruct((64, 128), BF16),
            jax.ShapeDtypeStruct((16, 128), F32),
        ),
        in_specs=[VMEM, VMEM],
        out_specs=(VMEM, VMEM, VMEM),
        compiler_params=PARAMS,
        name="output",
    )(received, weight)

    weight_part = jnp.sum(broadcast(weight_part, 8, YC), axis=0)
    weight_part = jnp.sum(broadcast(weight_part, 4, ("zh",)), axis=0)
    high, low = split_high_low(weight_part)
    final = broadcast(jnp.concatenate([column_piece, high, low], axis=0), 16, REP)
    feature_grad = (
        final[:, 0:64].reshape(16, 4, 16, 128).transpose(1, 0, 2, 3).reshape(1024, 128)
    )
    weight_grad = final[:, 64:80].astype(F32) + final[:, 80:96].astype(F32)
    weight_grad = (
        weight_grad.reshape(16, 2, 8, 128).transpose(0, 2, 1, 3).reshape(128, 256)
    )
    return output, weight_grad, feature_grad


def solution(mesh):
    fine = Mesh(mesh.devices.reshape(4, 4, 4, 4, 2), REP + ROW)
    placed = (
        P(ROW, None),
        P(REP, ROW, None, None, None),
        P(REP, ROW, None),
        P(REP, ROW, None),
        P(),
        P(ROW, None),
    )
    return jax.shard_map(
        body,
        mesh=fine,
        in_specs=placed,
        out_specs=(P(ROW, None), P(), P(ROW, None)),
        check_vma=False,
    )
```

time: 981 us -> 141 us (0.14)
  waiting for transfers between devices: 637 us -> 9.32 us
  blocking collectives: 270 us -> 86.7 us
  starting transfers between devices: 0.12 us -> 27.3 us
  matrix products: 25.3 us -> 0 us
  local copies, waits for them, and re-layouts: 24.9 us -> 6.89 us
  between operations: 13.9 us -> 0.77 us
    psum x3 -> x0, waiting for transfers between devices: 637 us -> none  [the longest x1 316 us: body(): weight_grad = lax.psum(weight_term, 'row') * scaling]
    psum x2 -> x0, blocking collectives: 270 us -> none  [the longest x1 184 us: body(): column_total = lax.psum(column_terms[held_number], 'row')]
    all_to_all x0 -> x5, blocking collectives: none -> 86.7 us  [exchange(): return lax.all_to_all(block, axes, 0, 0)]
    dot_general x7 -> x0, matrix products: 25.3 us -> none  [the longest x1 6.89 us: body(): jnp.einsum('tij,tjf->tif', tile_vals, picked, preferred_element_type=jnp....]
    ppermute x0 -> x2, starting transfers between devices: none -> 19 us  [the longest x1 13 us: body(): column_sum = lax.ppermute(column_sum, REP + ROW, [(d, s) for s, d in PAIRS])]
    dot_general x3 -> x0, local copies, waits for them, and re-layouts: 14.3 us -> none  [the longest x1 6.71 us: body(): jnp.einsum('tji,tjf->tif', tile_vals, grad_picked, preferred_element_type...]
  transfers between devices with their start and end apart: 3 -> 3, of which waited for: 3 -> 2; matrix products, arithmetic and copies ran while one was open for 3% -> 0% of each run, Pallas kernels for 0% -> 1%
where the time goes in v1:
time: 141 us; the launch traced here: 139 us
  blocking collectives  86.7 us (61%)
  starting transfers between devices  27.3 us (19%)
  waiting for transfers between devices  9.32 us (7%)
  Pallas kernels  7.29 us (5%)
  local copies, waits for them, and re-layouts  6.89 us (5%)
    all_to_all x5, blocking collectives, exchange(): return lax.all_to_all(block, axes, 0, 0)  86.7 us
    ppermute x1, starting transfers between devices, body(): column_sum = lax.ppermute(column_sum, REP + ROW, [(d, s) for s, d in PAIRS])  13 us
    all_to_all x1, starting transfers between devices, exchange(): return lax.all_to_all(block, axes, 0, 0)  8.36 us
    ppermute x1, waiting for transfers between devices, body(): quarter = lax.ppermute(quarter, REP + ROW, PAIRS)  7.43 us
    unnamed x16, local copies, waits for them, and re-layouts  6.01 us
    ppermute x1, starting transfers between devices, body(): quarter = lax.ppermute(quarter, REP + ROW, PAIRS)  5.93 us
    pallas_call x1, Pallas kernels, body(): pl.pallas_call(forward_kernel, grid=(8,), out_shape=jax.ShapeDtypeStruct(...  3.95 us
  transfers between devices with their start and end apart: 3, of which 2 were waited for; matrix products, arithmetic and copies ran while one was open for 0% of the time, Pallas kernels for 1%

profile of v1, /device:TPU:24, one launch (start us, length us, event | category | flops | bytes accessed | tf_op | source)
XLA Modules:
  0.0 139.1 jit_solution(11124877768865788550)
XLA Ops:
  0.7 0.9 copy-done
  1.6 5.9 %collective-permute-start = (bf16[256,128]{1,0:T(8,128)(2,1)S(1)}, bf16[256,128]{1,0:T(8,128)(2,1)S(1)}, u32[]{:S(2)}, u32[]{:S(2)}) collective-permute-start(bf16[256,128]{1,0:T(8,128)(2,1)S(1)} %constant_dynamic-slice_fusion), channel_id=1, source_target_pairs={{0,0},{32,1},{64,2},{96,3},{16,4},{48,5},{80,6},{112,7},{128,8},{1... | collective-permute-start | bytes 196616 | tf_op jit(solution)/shard_map/ppermute | solution.py:119
  7.5 1.9 %copy-done.1 = bf16[1,1,96,128,128]{4,3,2,1,0:T(8,128)(2,1)S(1)} copy-done((bf16[1,1,96,128,128]{4,3,2,1,0:T(8,128)(2,1)S(1)}, bf16[1,1,96,128,128]{4,3,2,1,0:T(8,128)(2,1)}, u32[]{:S(2)}) %copy-start.1) | copy-done | bytes 3145752
  9.4 1.0 copy-done.2
  10.5 0.8 copy-done.4
  11.3 0.7 copy-done.6
  12.0 0.7 copy-done.7
  12.6 2.0 %backward.1 = (bf16[1024,2048]{1,0:T(8,128)(2,1)S(1)}, bf16[8,256,128]{2,1,0:T(8,128)(2,1)S(1)}) custom-call(s32[8]{0:T(128)S(1)} %bitcast.16, s32[96]{0:T(128)S(1)} %bitcast.17, bf16[96,128,128]{2,1,0:T(8,128)(2,1)S(1)} %bitcast.15, bf16[1024,256]{1,0:T(8,128)(2,1)S(1)} %copy-done.2, bf16[128,256]{1,0:T(8,128)(2,1)S(1)} %copy-done.4), custom_call_target="tpu_custom_call" | custom-call | flops 603979776 | bytes 8388608 | tf_op jit(solution)/shard_map/backward/pallas_call | solution.py:121
  14.7 7.4 %collective-permute-done = bf16[256,128]{1,0:T(8,128)(2,1)S(1)} collective-permute-done((bf16[256,128]{1,0:T(8,128)(2,1)S(1)}, bf16[256,128]{1,0:T(8,128)(2,1)S(1)}, u32[]{:S(2)}, u32[]{:S(2)}) %collective-permute-start) | collective-permute-done | bytes 65568 | tf_op jit(solution)/shard_map/ppermute | solution.py:119
  22.2 0.1 pad_maximum_fusion
  22.2 18.3 %all_to_all.30.received = bf16[8,512,128]{2,1,0:T(8,128)(2,1)S(1)} all-to-all(bf16[8,512,128]{2,1,0:T(8,128)(2,1)S(1)} %pad_maximum_fusion), channel_id=1, replica_groups=mesh['zl'=4,'x'=4,'zh'=4,'y'=4,'c'=2] {'y','c'}, dimensions={0} | all-to-all | bytes 2097152 | tf_op jit(solution)/shard_map/all_to_all | solution.py:106
  40.6 3.9 %forward.1 = bf16[1024,128]{1,0:T(8,128)(2,1)} custom-call(bf16[1024,2048]{1,0:T(8,128)(2,1)S(1)} %get-tuple-element.8.dense, bf16[8,512,128]{2,1,0:T(8,128)(2,1)S(1)} %all_to_all.30.received), custom_call_target="tpu_custom_call" | custom-call | flops 536870912 | bytes 6291456 | tf_op jit(solution)/shard_map/forward/pallas_call | solution.py:144
  44.5 8.4 %all-to-all-start.1 = ((bf16[16,64,128]{2,1,0:T(8,128)(2,1)}), bf16[16,64,128]{2,1,0:T(8,128)(2,1)S(1)}, u32[]{:S(2)}, u32[]{:S(2)}) async-start(bf16[16,64,128]{2,1,0:T(8,128)(2,1)} %bitcast.4), calls=%async_computation.1 | async-start | bytes 524288 | tf_op jit(solution)/shard_map/all_to_all | solution.py:106
  52.9 0.1 slice_reduce_fusion
  53.0 13.0 %collective-permute-start.1 = (bf16[256,128]{1,0:T(8,128)(2,1)S(1)}, bf16[256,128]{1,0:T(8,128)(2,1)S(1)}, u32[]{:S(2)}, u32[]{:S(2)}) collective-permute-start(bf16[256,128]{1,0:T(8,128)(2,1)S(1)} %slice_reduce_fusion), channel_id=1, source_target_pairs={{0,0},{1,32},{2,64},{3,96},{4,16},{5,48},{6,80},{7,112},{8,128},{9... | collective-permute-start | bytes 196616 | tf_op jit(solution)/shard_map/ppermute | solution.py:142
  66.0 1.9 %collective-permute-done.1.refs_2_ = bf16[256,128]{1,0:T(8,128)(2,1)S(1)} collective-permute-done((bf16[256,128]{1,0:T(8,128)(2,1)S(1)}, bf16[256,128]{1,0:T(8,128)(2,1)S(1)}, u32[]{:S(2)}, u32[]{:S(2)}) %collective-permute-start.1) | collective-permute-done | bytes 65568 | tf_op jit(solution)/shard_map/ppermute | solution.py:142
  67.9 0.2 aggregate.1
  68.1 24.3 %all_to_all.31.received = bf16[16,112,128]{2,1,0:T(8,128)(2,1)S(1)} all-to-all(bf16[16,112,128]{2,1,0:T(8,128)(2,1)S(1)} %aggregate.1), channel_id=1, replica_groups=mesh['zl'=4,'x'=4,'zh'=4,'y'=4,'c'=2] {'zl','x'}, dimensions={0} | all-to-all | bytes 917504 | tf_op jit(solution)/shard_map/all_to_all | solution.py:106
  92.4 1.1 output.1
  93.5 8.1 %all_to_all.32 = f32[8,16,128]{2,1,0:T(8,128)S(1)} all-to-all(f32[8,16,128]{2,1,0:T(8,128)S(1)} %broadcast_in_dim.9), channel_id=1, replica_groups=mesh['zl'=4,'x'=4,'zh'=4,'y'=4,'c'=2] {'y','c'}, dimensions={0} | all-to-all | bytes 131072 | tf_op jit(solution)/shard_map/all_to_all | solution.py:106
  101.6 20.5 %all_to_all.33 = f32[4,16,128]{2,1,0:T(8,128)S(1)} all-to-all(f32[4,16,128]{2,1,0:T(8,128)S(1)} %broadcast_in_dim.10), channel_id=1, replica_groups=mesh['zl'=4,'x'=4,'zh'=4,'y'=4,'c'=2] {'zh'}, dimensions={0} | all-to-all | bytes 65536 | tf_op jit(solution)/shard_map/all_to_all | solution.py:106
  122.1 15.6 %all_to_all.34 = bf16[16,96,128]{2,1,0:T(8,128)(2,1)S(1)} all-to-all(bf16[16,96,128]{2,1,0:T(8,128)(2,1)S(1)} %broadcast_in_dim.11), channel_id=1, replica_groups=mesh['zl'=4,'x'=4,'zh'=4,'y'=4,'c'=2] {'zl','x'}, dimensions={0} | all-to-all | bytes 786432 | tf_op jit(solution)/shard_map/all_to_all | solution.py:106
  137.7 0.7 copy.10
  138.4 0.7 add_bitcast_fusion
  (21 shorter events, 0.2 us)
Async XLA Ops:
  0.6 1.0 copy-start
  1.6 20.5 %collective-permute-start = (bf16[256,128]{1,0:T(8,128)(2,1)S(1)}, bf16[256,128]{1,0:T(8,128)(2,1)S(1)}, u32[]{:S(2)}, u32[]{:S(2)}) collective-permute-start(bf16[256,128]{1,0:T(8,128)(2,1)S(1)} %constant_dynamic-slice_fusion), channel_id=1, source_target_pairs={{0,0},{32,1},{64,2},{96,3},{16,4},{48,5},{80,6},{112,7},{128,8},{1... | collective-permute-start | bytes 196616 | tf_op jit(solution)/shard_map/ppermute | solution.py:119
  7.5 1.9 %copy-start.1 = (bf16[1,1,96,128,128]{4,3,2,1,0:T(8,128)(2,1)S(1)}, bf16[1,1,96,128,128]{4,3,2,1,0:T(8,128)(2,1)}, u32[]{:S(2)}) copy-start(bf16[1,1,96,128,128]{4,3,2,1,0:T(8,128)(2,1)} %param.7) | copy-start | bytes 9437188
  9.4 1.0 copy-start.2
  10.5 0.8 copy-start.4
  11.3 0.7 copy-start.6
  12.0 0.7 copy-start.7
  40.6 27.3 %copy-start.3 = (bf16[1024,256]{1,0:T(8,128)(2,1)S(1)}, bf16[1024,256]{1,0:T(8,128)(2,1)}, u32[]{:S(2)}) copy-start(bf16[1024,256]{1,0:T(8,128)(2,1)} %refs_1_.1) | copy-start | bytes 1572868
  44.5 47.9 %copy-start.5 = (bf16[128,256]{1,0:T(8,128)(2,1)S(1)}, bf16[128,256]{1,0:T(8,128)(2,1)}, u32[]{:S(2)}) copy-start(bf16[128,256]{1,0:T(8,128)(2,1)} %weight.3) | copy-start | bytes 196612
  44.5 23.4 %all-to-all-start.1 = ((bf16[16,64,128]{2,1,0:T(8,128)(2,1)}), bf16[16,64,128]{2,1,0:T(8,128)(2,1)S(1)}, u32[]{:S(2)}, u32[]{:S(2)}) async-start(bf16[16,64,128]{2,1,0:T(8,128)(2,1)} %bitcast.4), calls=%async_computation.1 | async-start | bytes 524288 | tf_op jit(solution)/shard_map/all_to_all | solution.py:106
  53.0 14.9 %collective-permute-start.1 = (bf16[256,128]{1,0:T(8,128)(2,1)S(1)}, bf16[256,128]{1,0:T(8,128)(2,1)S(1)}, u32[]{:S(2)}, u32[]{:S(2)}) collective-permute-start(bf16[256,128]{1,0:T(8,128)(2,1)S(1)} %slice_reduce_fusion), channel_id=1, source_target_pairs={{0,0},{1,32},{2,64},{3,96},{4,16},{5,48},{6,80},{7,112},{8,128},{9... | collective-permute-start | bytes 196616 | tf_op jit(solution)/shard_map/ppermute | solution.py:142

commit v2 on v1

--- a/solution.py
+++ b/solution.py
@@ -58,34 +58,35 @@
         terms[k] = term.T.astype(BF16)
 
 
-def forward_kernel(dense, received, partial):
-    total = jnp.zeros((128, 128), F32)
+def forward_kernel(scaling, dense, received, node_grad, message, total):
     for k in range(8):
-        total = total + jnp.dot(
+        term = jnp.dot(
             dense[:, k * 256 : (k + 1) * 256], received[k, 0:256, :], preferred_element_type=F32
         )
-    partial[...] = total.astype(BF16)
-
-
-def aggregate_kernel(rep, scaling, parts, node_grad, column_sum, message):
+        if k == 0:
+            total[...] = term
+        else:
+            total[...] += term
+    partial = total[...].astype(BF16)
+    message[:, 0:64, :] = partial.reshape(16, 64, 128)
+    term = lax.dot_general(
+        partial, node_grad[...], (((0,), (0,)), ((), ())), preferred_element_type=F32
+    )
+    term = term * scaling
+    message[:, 64:80, :] = jnp.concatenate(
+        [term[:, 0:128].reshape(16, 8, 128), term[:, 128:256].reshape(16, 8, 128)], axis=1
+    ).astype(BF16)
+
+
+def aggregate_kernel(parts, piece, weight_part):
     total = parts[0].astype(F32)
     for a in range(1, 16):
         total = total + parts[a].astype(F32)
-    piece = total.astype(BF16)
-    message[:, 0:64, :] = jnp.broadcast_to(piece[None], (16, 64, 128))
-    message[:, 64:80, :] = column_sum[...].reshape(16, 16, 128)
-    rows = node_grad[pl.ds(pl.multiple_of(rep[0] * 64, 64), 64), :]
-    term = lax.dot_general(piece, rows, (((0,), (0,)), ((), ())), preferred_element_type=F32)
-    term = term * scaling
-    halves = jnp.concatenate(
-        [term[:, 0:128].reshape(16, 8, 128), term[:, 128:256].reshape(16, 8, 128)], axis=1
-    )
-    high, low = split_high_low(halves)
-    message[:, 80:96, :] = high
-    message[:, 96:112, :] = low
-
-
-def output_kernel(received, weight, output, column_piece, weight_part):
+    piece[...] = total[0:64].astype(BF16)
+    weight_part[...] = jnp.broadcast_to(total[64:80][None], (8, 16, 128))
+
+
+def output_kernel(received, weight, output, column_piece):
     for zq in range(4):
         aggregate = received[zq * 4 : zq * 4 + 4, 0:64, :].reshape(256, 128)
         output[zq * 256 : (zq + 1) * 256, :] = jnp.dot(
@@ -96,10 +97,6 @@
         for zh in range(1, 4):
             total = total + received[zh * 4 + part, 64:80, :].astype(F32)
         column_piece[part * 16 : (part + 1) * 16, :] = total.astype(BF16)
-    total = received[0, 80:96, :].astype(F32) + received[0, 96:112, :].astype(F32)
-    for a in range(1, 16):
-        total = total + (received[a, 80:96, :].astype(F32) + received[a, 96:112, :].astype(F32))
-    weight_part[...] = total
 
 
 def exchange(block, axes):
@@ -139,50 +136,57 @@
     )
 
     column_sum = jnp.sum(received[:, 256:].astype(F32), axis=0).astype(BF16)
+    received, column_sum = lax.optimization_barrier((received, column_sum))
     column_sum = lax.ppermute(column_sum, REP + ROW, [(d, s) for s, d in PAIRS])
 
-    partial = pl.pallas_call(
-        forward_kernel,
-        grid=(8,),
-        out_shape=jax.ShapeDtypeStruct((1024, 128), BF16),
-        in_specs=[
-            pl.BlockSpec((128, 2048), lambda b: (b, 0)),
-            pl.BlockSpec((8, 512, 128), lambda b: (0, 0, 0)),
-        ],
-        out_specs=pl.BlockSpec((128, 128), lambda b: (b, 0)),
+    message = pl.pallas_call(
+        lambda *refs: forward_kernel(scaling, *refs),
+        out_shape=jax.ShapeDtypeStruct((16, 80, 128), BF16),
+        in_specs=[VMEM, VMEM, VMEM],
+        out_specs=VMEM,
+        scratch_shapes=[pltpu.VMEM((1024, 128), F32)],
         compiler_params=PARAMS,
         cost_estimate=pl.CostEstimate(
-            flops=2 * 128 * 1024 * 2048, bytes_accessed=6 << 20, transcendentals=0
+            flops=2 * 128 * 1024 * 2304, bytes_accessed=6 << 20, transcendentals=0
         ),
         name="forward",
-    )(dense, received)
-    parts = exchange(partial.reshape(16, 64, 128), REP)
-
-    message = pl.pallas_call(
-        lambda rep, *refs: aggregate_kernel(rep, scaling, *refs),
-        out_shape=jax.ShapeDtypeStruct((16, 112, 128), BF16),
-        in_specs=[SMEM, VMEM, VMEM, VMEM],
-        out_specs=VMEM,
+    )(dense, received, node_grad)
+    parts = exchange(message, REP)
+
+    piece, weight_part = pl.pallas_call(
+        aggregate_kernel,
+        out_shape=(
+            jax.ShapeDtypeStruct((64, 128), BF16),
+            jax.ShapeDtypeStruct((8, 16, 128), F32),
+        ),
+        in_specs=[VMEM],
+        out_specs=(VMEM, VMEM),
         compiler_params=PARAMS,
         name="aggregate",
-    )(rep_index.astype(jnp.int32).reshape(1), parts, node_grad, column_sum)
+    )(parts)
+    weight_part = jnp.sum(exchange(weight_part, YC), axis=0)
+    message = jnp.concatenate(
+        [jnp.broadcast_to(piece[None], (16, 64, 128)), column_sum.reshape(16, 16, 128)], axis=1
+    )
+    message, weight_part = lax.optimization_barrier((message, weight_part))
+    others = [
+        lax.ppermute(weight_part, "zh", [(i, (i + k) % 4) for i in range(4)]) for k in (1, 2, 3)
+    ]
     received = exchange(message, REP)
 
-    output, column_piece, weight_part = pl.pallas_call(
+    output, column_piece = pl.pallas_call(
         output_kernel,
         out_shape=(
             jax.ShapeDtypeStruct((1024, 256), BF16),
             jax.ShapeDtypeStruct((64, 128), BF16),
-            jax.ShapeDtypeStruct((16, 128), F32),
         ),
         in_specs=[VMEM, VMEM],
-        out_specs=(VMEM, VMEM, VMEM),
+        out_specs=(VMEM, VMEM),
         compiler_params=PARAMS,
         name="output",
     )(received, weight)
 
-    weight_part = jnp.sum(broadcast(weight_part, 8, YC), axis=0)
-    weight_part = jnp.sum(broadcast(weight_part, 4, ("zh",)), axis=0)
+    weight_part = (weight_part + others[1]) + (others[0] + others[2])
     high, low = split_high_low(weight_part)
     final = broadcast(jnp.concatenate([column_piece, high, low], axis=0), 16, REP)
     feature_grad = (

time: 141 us -> 128 us (0.908)
  blocking collectives: 86.7 us -> 37 us
  starting transfers between devices: 27.3 us -> 57.4 us
  waiting for transfers between devices: 9.32 us -> 17.1 us
    all_to_all x5 -> x2, blocking collectives: 86.7 us -> 37 us  [exchange(): return lax.all_to_all(block, axes, 0, 0)]
    ppermute x0 -> x3, starting transfers between devices: none -> 19.7 us  [body(): lax.ppermute(weight_part, 'zh', [(i, (i + k) % 4) for i in range(4)])]
    all_to_all x1 -> x3, starting transfers between devices: 8.36 us -> 18.9 us  [exchange(): return lax.all_to_all(block, axes, 0, 0)]
    ppermute x0 -> x3, waiting for transfers between devices: none -> 6.96 us  [body(): lax.ppermute(weight_part, 'zh', [(i, (i + k) % 4) for i in range(4)])]
    all_to_all x1 -> x3, waiting for transfers between devices: 0.01 us -> 2.73 us  [exchange(): return lax.all_to_all(block, axes, 0, 0)]
    ppermute x1, waiting for transfers between devices: 1.88 us -> 0.01 us  [body(): column_sum = lax.ppermute(column_sum, REP + ROW, [(d, s) for s, d in PAIRS])]
    unnamed x16 -> x14, local copies, waits for them, and re-layouts: 6.01 us -> 6.01 us
  transfers between devices with their start and end apart: 3 -> 8, of which waited for: 2 -> 3; matrix products, arithmetic and copies ran while one was open for 0% -> 1% of each run, Pallas kernels for 1% -> 2%
where the time goes in v2:
time: 128 us; the launch traced here: 127 us
  starting transfers between devices  57.4 us (45%)
  blocking collectives  37 us (29%)
  waiting for transfers between devices  17.1 us (13%)
  local copies, waits for them, and re-layouts  6.92 us (5%)
  Pallas kernels  5.98 us (5%)
  other arithmetic  1.58 us (1%)
    all_to_all x2, blocking collectives, exchange(): return lax.all_to_all(block, axes, 0, 0)  37 us
    ppermute x3, starting transfers between devices, body(): lax.ppermute(weight_part, 'zh', [(i, (i + k) % 4) for i in range(4)])  19.7 us
    all_to_all x3, starting transfers between devices, exchange(): return lax.all_to_all(block, axes, 0, 0)  18.9 us
    ppermute x1, starting transfers between devices, body(): column_sum = lax.ppermute(column_sum, REP + ROW, [(d, s) for s, d in PAIRS])  12.8 us
    ppermute x1, waiting for transfers between devices, body(): quarter = lax.ppermute(quarter, REP + ROW, PAIRS)  7.46 us
    ppermute x3, waiting for transfers between devices, body(): lax.ppermute(weight_part, 'zh', [(i, (i + k) % 4) for i in range(4)])  6.96 us
    unnamed x14, local copies, waits for them, and re-layouts  6.01 us
    ppermute x1, starting transfers between devices, body(): quarter = lax.ppermute(quarter, REP + ROW, PAIRS)  5.93 us
  transfers between devices with their start and end apart: 8, of which 3 were waited for; matrix products, arithmetic and copies ran while one was open for 1% of the time, Pallas kernels for 2%

profile of v2, /device:TPU:24, one launch (start us, length us, event | category | flops | bytes accessed | tf_op | source)
XLA Modules:
  0.0 126.8 jit_solution(12527610503422089850)
XLA Ops:
  0.7 0.9 copy-done
  1.6 5.9 %collective-permute-start = (bf16[256,128]{1,0:T(8,128)(2,1)S(1)}, bf16[256,128]{1,0:T(8,128)(2,1)S(1)}, u32[]{:S(2)}, u32[]{:S(2)}) collective-permute-start(bf16[256,128]{1,0:T(8,128)(2,1)S(1)} %constant_dynamic-slice_fusion), channel_id=1, source_target_pairs={{0,0},{32,1},{64,2},{96,3},{16,4},{48,5},{80,6},{112,7},{128,8},{1... | collective-permute-start | bytes 196616 | tf_op jit(solution)/shard_map/ppermute | solution.py:116
  7.5 1.9 %copy-done.1 = bf16[1,1,96,128,128]{4,3,2,1,0:T(8,128)(2,1)S(1)} copy-done((bf16[1,1,96,128,128]{4,3,2,1,0:T(8,128)(2,1)S(1)}, bf16[1,1,96,128,128]{4,3,2,1,0:T(8,128)(2,1)}, u32[]{:S(2)}) %copy-start.1) | copy-done | bytes 3145752
  9.4 1.0 copy-done.2
  10.5 0.8 copy-done.3
  11.3 0.7 copy-done.5
  12.6 2.0 %backward.1 = (bf16[1024,2048]{1,0:T(8,128)(2,1)S(1)}, bf16[8,256,128]{2,1,0:T(8,128)(2,1)S(1)}) custom-call(s32[8]{0:T(128)S(1)} %bitcast.15, s32[96]{0:T(128)S(1)} %bitcast.16, bf16[96,128,128]{2,1,0:T(8,128)(2,1)S(1)} %bitcast.14, bf16[1024,256]{1,0:T(8,128)(2,1)S(1)} %copy-done.2, bf16[128,256]{1,0:T(8,128)(2,1)S(1)} %copy-done.3), custom_call_target="tpu_custom_call" | custom-call | flops 603979776 | bytes 8388608 | tf_op jit(solution)/shard_map/backward/pallas_call | solution.py:118
  14.6 7.5 %collective-permute-done = bf16[256,128]{1,0:T(8,128)(2,1)S(1)} collective-permute-done((bf16[256,128]{1,0:T(8,128)(2,1)S(1)}, bf16[256,128]{1,0:T(8,128)(2,1)S(1)}, u32[]{:S(2)}, u32[]{:S(2)}) %collective-permute-start) | collective-permute-done | bytes 65568 | tf_op jit(solution)/shard_map/ppermute | solution.py:116
  22.2 18.3 %all_to_all.25.refs_1_ = bf16[8,512,128]{2,1,0:T(8,128)(2,1)S(1)} all-to-all(bf16[8,512,128]{2,1,0:T(8,128)(2,1)S(1)} %pad_maximum_fusion), channel_id=1, replica_groups=mesh['zl'=4,'x'=4,'zh'=4,'y'=4,'c'=2] {'y','c'}, dimensions={0} | all-to-all | bytes 2097152 | tf_op jit(solution)/shard_map/all_to_all | solution.py:103
  40.7 2.2 %forward.1 = bf16[16,80,128]{2,1,0:T(8,128)(2,1)} custom-call(bf16[1024,2048]{1,0:T(8,128)(2,1)S(1)} %get-tuple-element.13.refs_0_, bf16[8,512,128]{2,1,0:T(8,128)(2,1)S(1)} %all_to_all.25.refs_1_, bf16[1024,256]{1,0:T(8,128)(2,1)S(1)} %copy-done.2), custom_call_target="tpu_custom_call" | custom-call | flops 603979776 | bytes 6291456 | tf_op jit(solution)/shard_map/forward/pallas_call | solution.py:142
  42.9 8.6 %all-to-all-start.1 = ((bf16[16,80,128]{2,1,0:T(8,128)(2,1)}), bf16[16,80,128]{2,1,0:T(8,128)(2,1)S(1)}, u32[]{:S(2)}, u32[]{:S(2)}) async-start(bf16[16,80,128]{2,1,0:T(8,128)(2,1)} %forward.1), calls=%async_computation.1 | async-start | bytes 655360 | tf_op jit(solution)/shard_map/all_to_all | solution.py:103
  51.5 12.8 %collective-permute-start.1 = (bf16[256,128]{1,0:T(8,128)(2,1)S(1)}, bf16[256,128]{1,0:T(8,128)(2,1)S(1)}, u32[]{:S(2)}, u32[]{:S(2)}) collective-permute-start(bf16[256,128]{1,0:T(8,128)(2,1)S(1)} %slice_reduce_fusion), channel_id=1, source_target_pairs={{0,0},{1,32},{2,64},{3,96},{4,16},{5,48},{6,80},{7,112},{8,128},{9... | collective-permute-start | bytes 196616 | tf_op jit(solution)/shard_map/ppermute | solution.py:140
  65.0 5.3 %all-to-all-start.2 = ((f32[8,16,128]{2,1,0:T(8,128)}), f32[8,16,128]{2,1,0:T(8,128)S(1)}, u32[]{:S(2)}, u32[]{:S(2)}) async-start(f32[8,16,128]{2,1,0:T(8,128)} %get-tuple-element.18), calls=%async_computation.2 | async-start | bytes 131072 | tf_op jit(solution)/shard_map/all_to_all | solution.py:103
  70.3 0.7 pad_maximum_fusion.1
  71.0 2.7 %all-to-all-done.2 = f32[8,16,128]{2,1,0:T(8,128)S(1)} async-done(((f32[8,16,128]{2,1,0:T(8,128)}), f32[8,16,128]{2,1,0:T(8,128)S(1)}, u32[]{:S(2)}, u32[]{:S(2)}) %all-to-all-start.2) | async-done | bytes 65568 | tf_op jit(solution)/shard_map/all_to_all | solution.py:103
  73.8 5.1 %all-to-all-start.3 = ((bf16[16,80,128]{2,1,0:T(8,128)(2,1)}), bf16[16,80,128]{2,1,0:T(8,128)(2,1)S(1)}, u32[]{:S(2)}, u32[]{:S(2)}) async-start(bf16[16,80,128]{2,1,0:T(8,128)(2,1)} %pad_maximum_fusion.1), calls=%async_computation.3 | async-start | bytes 655360 | tf_op jit(solution)/shard_map/all_to_all | solution.py:103
  78.9 6.8 %collective-permute-start.4 = (f32[16,128]{1,0:T(8,128)S(1)}, f32[16,128]{1,0:T(8,128)S(1)}, u32[]{:S(2)}, u32[]{:S(2)}) collective-permute-start(f32[16,128]{1,0:T(8,128)S(1)} %reduce_sum.22), channel_id=1, source_target_pairs={{0,24},{8,0},{16,8},{24,16},{1,25},{9,1},{17,9},{25,17},{2,26},{10... | collective-permute-start | bytes 24584 | tf_op jit(solution)/shard_map/ppermute | solution.py:173
  85.7 5.7 %collective-permute-start.3 = (f32[16,128]{1,0:T(8,128)S(1)}, f32[16,128]{1,0:T(8,128)S(1)}, u32[]{:S(2)}, u32[]{:S(2)}) collective-permute-start(f32[16,128]{1,0:T(8,128)S(1)} %reduce_sum.22), channel_id=1, source_target_pairs={{0,8},{8,16},{16,24},{24,0},{1,9},{9,17},{17,25},{25,1},{2,10},{10... | collective-permute-start | bytes 24584 | tf_op jit(solution)/shard_map/ppermute | solution.py:173
  91.4 7.3 %collective-permute-start.2 = (f32[16,128]{1,0:T(8,128)S(1)}, f32[16,128]{1,0:T(8,128)S(1)}, u32[]{:S(2)}, u32[]{:S(2)}) collective-permute-start(f32[16,128]{1,0:T(8,128)S(1)} %reduce_sum.22), channel_id=1, source_target_pairs={{0,16},{8,24},{16,0},{24,8},{1,17},{9,25},{17,1},{25,9},{2,18},{10... | collective-permute-start | bytes 24584 | tf_op jit(solution)/shard_map/ppermute | solution.py:173
  98.7 7.0 %collective-permute-done.2 = f32[16,128]{1,0:T(8,128)S(1)} collective-permute-done((f32[16,128]{1,0:T(8,128)S(1)}, f32[16,128]{1,0:T(8,128)S(1)}, u32[]{:S(2)}, u32[]{:S(2)}) %collective-permute-start.2) | collective-permute-done | bytes 8224 | tf_op jit(solution)/shard_map/ppermute | solution.py:173
  105.6 1.1 output.1
  106.8 18.6 %all_to_all.26 = bf16[16,96,128]{2,1,0:T(8,128)(2,1)S(1)} all-to-all(bf16[16,96,128]{2,1,0:T(8,128)(2,1)S(1)} %broadcast_in_dim.8), channel_id=1, replica_groups=mesh['zl'=4,'x'=4,'zh'=4,'y'=4,'c'=2] {'zl','x'}, dimensions={0} | all-to-all | bytes 786432 | tf_op jit(solution)/shard_map/all_to_all | solution.py:103
  125.4 0.7 copy.9
  126.2 0.7 add_bitcast_fusion
  (25 shorter events, 1.7 us)
Async XLA Ops:
  0.6 1.0 copy-start
  1.6 20.5 %collective-permute-start = (bf16[256,128]{1,0:T(8,128)(2,1)S(1)}, bf16[256,128]{1,0:T(8,128)(2,1)S(1)}, u32[]{:S(2)}, u32[]{:S(2)}) collective-permute-start(bf16[256,128]{1,0:T(8,128)(2,1)S(1)} %constant_dynamic-slice_fusion), channel_id=1, source_target_pairs={{0,0},{32,1},{64,2},{96,3},{16,4},{48,5},{80,6},{112,7},{128,8},{1... | collective-permute-start | bytes 196616 | tf_op jit(solution)/shard_map/ppermute | solution.py:116
  7.5 1.9 %copy-start.1 = (bf16[1,1,96,128,128]{4,3,2,1,0:T(8,128)(2,1)S(1)}, bf16[1,1,96,128,128]{4,3,2,1,0:T(8,128)(2,1)}, u32[]{:S(2)}) copy-start(bf16[1,1,96,128,128]{4,3,2,1,0:T(8,128)(2,1)} %param.7) | copy-start | bytes 9437188
  9.4 1.0 copy-start.2
  10.5 0.8 copy-start.3
  11.3 0.7 copy-start.5
  12.0 0.7 copy-start.6
  42.9 62.7 %copy-start.4 = (bf16[128,256]{1,0:T(8,128)(2,1)S(1)}, bf16[128,256]{1,0:T(8,128)(2,1)}, u32[]{:S(2)}) copy-start(bf16[128,256]{1,0:T(8,128)(2,1)} %weight.3) | copy-start | bytes 196612
  42.9 21.4 %all-to-all-start.1 = ((bf16[16,80,128]{2,1,0:T(8,128)(2,1)}), bf16[16,80,128]{2,1,0:T(8,128)(2,1)S(1)}, u32[]{:S(2)}, u32[]{:S(2)}) async-start(bf16[16,80,128]{2,1,0:T(8,128)(2,1)} %forward.1), calls=%async_computation.1 | async-start | bytes 655360 | tf_op jit(solution)/shard_map/all_to_all | solution.py:103
  51.5 18.7 %collective-permute-start.1 = (bf16[256,128]{1,0:T(8,128)(2,1)S(1)}, bf16[256,128]{1,0:T(8,128)(2,1)S(1)}, u32[]{:S(2)}, u32[]{:S(2)}) collective-permute-start(bf16[256,128]{1,0:T(8,128)(2,1)S(1)} %slice_reduce_fusion), channel_id=1, source_target_pairs={{0,0},{1,32},{2,64},{3,96},{4,16},{5,48},{6,80},{7,112},{8,128},{9... | collective-permute-start | bytes 196616 | tf_op jit(solution)/shard_map/ppermute | solution.py:140
  65.0 8.8 %all-to-all-start.2 = ((f32[8,16,128]{2,1,0:T(8,128)}), f32[8,16,128]{2,1,0:T(8,128)S(1)}, u32[]{:S(2)}, u32[]{:S(2)}) async-start(f32[8,16,128]{2,1,0:T(8,128)} %get-tuple-element.18), calls=%async_computation.2 | async-start | bytes 131072 | tf_op jit(solution)/shard_map/all_to_all | solution.py:103
  73.8 31.9 %all-to-all-start.3 = ((bf16[16,80,128]{2,1,0:T(8,128)(2,1)}), bf16[16,80,128]{2,1,0:T(8,128)(2,1)S(1)}, u32[]{:S(2)}, u32[]{:S(2)}) async-start(bf16[16,80,128]{2,1,0:T(8,128)(2,1)} %pad_maximum_fusion.1), calls=%async_computation.3 | async-start | bytes 655360 | tf_op jit(solution)/shard_map/all_to_all | solution.py:103
  78.9 19.8 %collective-permute-start.4 = (f32[16,128]{1,0:T(8,128)S(1)}, f32[16,128]{1,0:T(8,128)S(1)}, u32[]{:S(2)}, u32[]{:S(2)}) collective-permute-start(f32[16,128]{1,0:T(8,128)S(1)} %reduce_sum.22), channel_id=1, source_target_pairs={{0,24},{8,0},{16,8},{24,16},{1,25},{9,1},{17,9},{25,17},{2,26},{10... | collective-permute-start | bytes 24584 | tf_op jit(solution)/shard_map/ppermute | solution.py:173
  85.7 13.0 %collective-permute-start.3 = (f32[16,128]{1,0:T(8,128)S(1)}, f32[16,128]{1,0:T(8,128)S(1)}, u32[]{:S(2)}, u32[]{:S(2)}) collective-permute-start(f32[16,128]{1,0:T(8,128)S(1)} %reduce_sum.22), channel_id=1, source_target_pairs={{0,8},{8,16},{16,24},{24,0},{1,9},{9,17},{17,25},{25,1},{2,10},{10... | collective-permute-start | bytes 24584 | tf_op jit(solution)/shard_map/ppermute | solution.py:173
  91.4 14.3 %collective-permute-start.2 = (f32[16,128]{1,0:T(8,128)S(1)}, f32[16,128]{1,0:T(8,128)S(1)}, u32[]{:S(2)}, u32[]{:S(2)}) collective-permute-start(f32[16,128]{1,0:T(8,128)S(1)} %reduce_sum.22), channel_id=1, source_target_pairs={{0,16},{8,24},{16,0},{24,8},{1,17},{9,25},{17,1},{25,9},{2,18},{10... | collective-permute-start | bytes 24584 | tf_op jit(solution)/shard_map/ppermute | solution.py:173

commit v3 on v2

v3 whole, which is shorter than its diff:
```python
import math

import jax
import jax.numpy as jnp
from jax import lax
from jax.experimental import pallas as pl
from jax.experimental.pallas import tpu as pltpu
from jax.sharding import Mesh
from jax.sharding import PartitionSpec as P

REP = ("zl", "x")
ROW = ("zh", "y", "c")
F32 = jnp.float32
BF16 = jnp.bfloat16
VMEM = pl.BlockSpec(memory_space=pltpu.VMEM)
SMEM = pl.BlockSpec(memory_space=pltpu.SMEM)
HBM = pl.BlockSpec(memory_space=pltpu.HBM)

PAIRS = [
    ((zh * 4 + k % 4) * 32 + q + 16 * (k // 4), q * 32 + zh * 8 + k)
    for q in range(16)
    for zh in range(4)
    for k in range(8)
]
SWAP = [(0, 1), (1, 0)]


def shape(*dims, dtype=BF16):
    return jax.ShapeDtypeStruct(dims, dtype)


def columns(dense, k):
    return dense[:, pl.ds(pl.multiple_of(k * 256, 256), 256)]


def backward_kernel(
    counts, cols, tiles_hbm, grad_hbm, weight_hbm, dense, terms,
    tiles, node_grad, weight, grad_t, sems,
):
    copies = [
        pltpu.make_async_copy(weight_hbm, weight, sems.at[0]),
        pltpu.make_async_copy(grad_hbm, node_grad, sems.at[1]),
        pltpu.make_async_copy(tiles_hbm, tiles, sems.at[2]),
    ]
    for copy in copies:
        copy.start()

    def clear(b, carry):
        dense[pl.ds(pl.multiple_of(b * 128, 128), 128), :] = jnp.zeros((128, 2048), BF16)
        return carry

    lax.fori_loop(0, 8, clear, 0)
    copies[0].wait()
    copies[1].wait()
    grad_t[...] = lax.dot_general(
        weight[...], node_grad[...], (((1,), (1,)), ((), ())), preferred_element_type=F32
    ).astype(BF16)
    copies[2].wait()
    start = jnp.int32(0)
    for b in range(8):
        count = counts[b]

        def place(i, carry, b=b, start=start):
            slot = start + i
            col = pl.multiple_of(cols[slot] * 128, 128)
            dense[b * 128 : (b + 1) * 128, pl.ds(col, 128)] = tiles[slot]
            return carry

        lax.fori_loop(0, count, place, 0)
        start = start + count
    for k in range(8):
        term = jnp.dot(
            grad_t[...], dense[:, k * 256 : (k + 1) * 256], preferred_element_type=F32
        )
        terms[k % 2, k // 2] = term.T.astype(BF16)


def pack_kernel(terms, quarter, message):
    for y in range(4):
        message[y, 0:256, :] = quarter[...]
        message[y, 256:512, :] = (terms[0, y].astype(F32) + terms[1, y].astype(F32)).astype(BF16)


def split_kernel(received, held, column_sum):
    total = received[0, 256:512, :].astype(F32)
    for y in range(1, 4):
        total = total + received[y, 256:512, :].astype(F32)
    column_sum[...] = total.astype(BF16)
    held[...] = received[:, 0:256, :]


def half_kernel(core, dense, held, total):
    for y in range(4):
        term = jnp.dot(columns(dense, 2 * y + core[0]), held[y], preferred_element_type=F32)
        if y == 0:
            total[...] = term
        else:
            total[...] += term


def forward_kernel(scaling, core, dense, held, half, node_grad, column_sum, message, total):
    for y in range(4):
        term = jnp.dot(columns(dense, 2 * y + 1 - core[0]), held[y], preferred_element_type=F32)
        if y == 0:
            total[...] = half[...] + term
        else:
            total[...] += term
    partial = total[...].astype(BF16)
    message[:, 0:64, :] = partial.reshape(16, 64, 128)
    message[:, 64:80, :] = column_sum[...].reshape(16, 16, 128)
    term = lax.dot_general(
        partial, node_grad[...], (((0,), (0,)), ((), ())), preferred_element_type=F32
    )
    term = term * scaling
    message[:, 80:96, :] = jnp.concatenate(
        [term[:, 0:128].reshape(16, 8, 128), term[:, 128:256].reshape(16, 8, 128)], axis=1
    ).astype(BF16)


def weight_kernel(parts, weight_part):
    total = parts[0, 80:96, :].astype(F32)
    for a in range(1, 16):
        total = total + parts[a, 80:96, :].astype(F32)
    weight_part[...] = total


def reduce_kernel(parts, piece):
    total = parts[0, 0:64, :].astype(F32)
    for a in range(1, 16):
        total = total + parts[a, 0:64, :].astype(F32)
    piece[0:64, :] = total.astype(BF16)
    for part in range(4):
        total = parts[part, 64:80, :].astype(F32)
        for zh in range(1, 4):
            total = total + parts[zh * 4 + part, 64:80, :].astype(F32)
        piece[64 + part * 16 : 80 + part * 16, :] = total.astype(BF16)


def gather_kernel(piece, weight_parts, message):
    message[:, 0:128, :] = jnp.broadcast_to(piece[...][None], (16, 128, 128))
    total = weight_parts[0]
    for i in range(1, 16):
        total = total + weight_parts[i]
    message[:, 128:144, :] = jnp.broadcast_to(total.astype(BF16)[None], (16, 16, 128))


def output_kernel(received, weight, output, weight_grad, feature_grad):
    parts = received[:, 128:144, :].astype(F32)
    weight_grad[:, 0:128] = parts[:, 0:8, :].reshape(128, 128)
    weight_grad[:, 128:256] = parts[:, 8:16, :].reshape(128, 128)
    for zq in range(4):
        aggregate = received[zq * 4 : zq * 4 + 4, 0:64, :].reshape(256, 128)
        output[zq * 256 : (zq + 1) * 256, :] = jnp.dot(
            aggregate, weight[...], preferred_element_type=F32
        ).astype(BF16)
        feature_grad[zq * 256 : (zq + 1) * 256, :] = received[
            :, 64 + zq * 16 : 80 + zq * 16, :
        ].reshape(256, 128)


def call(kernel, name, outs, ins, scratch=(), flops=0, moved=1 << 20, limit=16):
    return pl.pallas_call(
        kernel,
        out_shape=outs,
        in_specs=ins,
        out_specs=jax.tree.map(lambda _: VMEM, outs),
        scratch_shapes=list(scratch),
        compiler_params=pltpu.CompilerParams(vmem_limit_bytes=limit << 20),
        cost_estimate=pl.CostEstimate(flops=flops, bytes_accessed=moved, transcendentals=0),
        name=name,
    )


def exchange(block, axes):
    return lax.all_to_all(block, axes, 0, 0)


def broadcast(block, count, axes):
    return exchange(jnp.broadcast_to(block[None], (count, *block.shape)), axes)


def body(features, tile_values, tile_counts, tile_columns, weight, node_grad):
    rep_index = lax.axis_index(REP)
    core = lax.axis_index("c").astype(jnp.int32).reshape(1)
    scaling = 1.0 / math.sqrt(features.shape[0] * 32)

    quarter = lax.dynamic_slice_in_dim(features, (rep_index % 4) * 256, 256, axis=0)
    quarter = lax.ppermute(quarter, REP + ROW, PAIRS)

    dense, terms = call(
        backward_kernel,
        "backward",
        (shape(1024, 2048), shape(2, 4, 256, 128)),
        [SMEM, SMEM, HBM, HBM, HBM],
        [
            pltpu.VMEM((96, 128, 128), BF16),
            pltpu.VMEM((1024, 256), BF16),
            pltpu.VMEM((128, 256), BF16),
            pltpu.VMEM((128, 1024), BF16),
            pltpu.SemaphoreType.DMA((3,)),
        ],
        flops=2 * 128 * 1024 * 2304,
        moved=8 << 20,
        limit=58,
    )(tile_counts[0, 0], tile_columns[0, 0], tile_values[0, 0], node_grad, weight)
    terms = exchange(terms, "c")
    message = call(pack_kernel, "pack", shape(4, 512, 128), [VMEM] * 2)(terms, quarter)
    received = exchange(message, "y")

    held, column_sum = call(
        split_kernel, "split", (shape(4, 256, 128), shape(256, 128)), [VMEM]
    )(received)
    column_sum = lax.ppermute(column_sum, REP + ROW, [(d, s) for s, d in PAIRS])
    theirs = lax.ppermute(held, "c", SWAP)
    half = call(
        half_kernel,
        "half",
        shape(1024, 128, dtype=F32),
        [SMEM, VMEM, VMEM],
        flops=2 * 128 * 1024 * 1024,
        moved=3 << 20,
    )(core, dense, held)
    message = call(
        lambda *refs: forward_kernel(scaling, *refs),
        "forward",
        shape(16, 96, 128),
        [SMEM] + [VMEM] * 5,
        [pltpu.VMEM((1024, 128), F32)],
        flops=2 * 128 * 1024 * 1280,
        moved=3 << 20,
    )(core, dense, theirs, half, node_grad, column_sum)
    parts = exchange(message, REP)

    weight_part = call(weight_kernel, "weight", shape(16, 128, dtype=F32), [VMEM])(parts)
    weight_other = lax.ppermute(weight_part, "c", SWAP)
    piece = call(reduce_kernel, "reduce", shape(128, 128), [VMEM])(parts)
    weight_parts = broadcast(weight_part + weight_other, 16, ("zh", "y"))
    message = call(gather_kernel, "gather", shape(16, 144, 128), [VMEM] * 2)(piece, weight_parts)
    received = exchange(message, REP)
    return call(
        output_kernel,
        "output",
        (shape(1024, 256), shape(128, 256, dtype=F32), shape(1024, 128)),
        [VMEM, VMEM],
    )(received, weight)


def solution(mesh):
    fine = Mesh(mesh.devices.reshape(4, 4, 4, 4, 2), REP + ROW)
    placed = (
        P(ROW, None),
        P(REP, ROW, None, None, None),
        P(REP, ROW, None),
        P(REP, ROW, None),
        P(),
        P(ROW, None),
    )
    return jax.shard_map(
        body,
        mesh=fine,
        in_specs=placed,
        out_specs=(P(ROW, None), P(), P(ROW, None)),
        check_vma=False,
    )
```

time: 128 us -> 130 us (1.016)
  starting transfers between devices: 57.4 us -> 30.8 us
  blocking collectives: 37 us -> 63.1 us
  waiting for transfers between devices: 17.1 us -> 20.1 us
  Pallas kernels: 5.98 us -> 8.4 us
  local copies, waits for them, and re-layouts: 6.92 us -> 5.23 us
  other arithmetic: 1.58 us -> 0.01 us
    all_to_all x2 -> x4, blocking collectives: 37 us -> 63.1 us  [exchange(): return lax.all_to_all(block, axes, 0, 0)]
    ppermute x3 -> x2, starting transfers between devices: 19.7 us -> 3.84 us  [the longest x1 1.92 us: body(): theirs = lax.ppermute(held, 'c', SWAP)]
    all_to_all x3 -> x1, waiting for transfers between devices: 2.73 us -> 15.1 us  [exchange(): return lax.all_to_all(block, axes, 0, 0)]
    all_to_all x3 -> x1, starting transfers between devices: 18.9 us -> 8 us  [exchange(): return lax.all_to_all(block, axes, 0, 0)]
    ppermute x3 -> x2, waiting for transfers between devices: 6.96 us -> 1.14 us  [the longest x1 1.14 us: body(): weight_other = lax.ppermute(weight_part, 'c', SWAP)]
    ppermute x1, waiting for transfers between devices: 7.46 us -> 3.86 us  [body(): quarter = lax.ppermute(quarter, REP + ROW, PAIRS)]
    pallas_call x4 -> x9, Pallas kernels: 5.98 us -> 8.4 us  [the longest x1 5.33 us: body(): call(backward_kernel, 'backward', (shape(1024, 2048), shape(2, 4, 256, 12...]
    unnamed x14 -> x10, local copies, waits for them, and re-layouts: 6.01 us -> 4.56 us
  transfers between devices with their start and end apart: 8 -> 5, of which waited for: 3 -> 3; matrix products, arithmetic and copies ran while one was open for 1% -> 0% of each run, Pallas kernels for 2% -> 5%
where the time goes in v3:
time: 130 us; the launch traced here: 128 us
  blocking collectives  63.1 us (49%)
  starting transfers between devices  30.8 us (24%)
  waiting for transfers between devices  20.1 us (15%)
  Pallas kernels  8.4 us (6%)
  local copies, waits for them, and re-layouts  5.23 us (4%)
    all_to_all x4, blocking collectives, exchange(): return lax.all_to_all(block, axes, 0, 0)  63.1 us
    all_to_all x1, waiting for transfers between devices, exchange(): return lax.all_to_all(block, axes, 0, 0)  15.1 us
    ppermute x1, starting transfers between devices, body(): column_sum = lax.ppermute(column_sum, REP + ROW, [(d, s) for s, d in PAIRS])  13 us
    all_to_all x1, starting transfers between devices, exchange(): return lax.all_to_all(block, axes, 0, 0)  8 us
    ppermute x1, starting transfers between devices, body(): quarter = lax.ppermute(quarter, REP + ROW, PAIRS)  5.93 us
    pallas_call x1, Pallas kernels, body(): call(backward_kernel, 'backward', (shape(1024, 2048), shape(2, 4, 256, 12...  5.33 us
    unnamed x10, local copies, waits for them, and re-layouts  4.56 us
    ppermute x1, waiting for transfers between devices, body(): quarter = lax.ppermute(quarter, REP + ROW, PAIRS)  3.86 us
  transfers between devices with their start and end apart: 5, of which 3 were waited for; matrix products, arithmetic and copies ran while one was open for 0% of the time, Pallas kernels for 5%

profile of v3, /device:TPU:24, one launch (start us, length us, event | category | flops | bytes accessed | tf_op | source)
XLA Modules:
  0.0 128.4 jit_solution(12380469730172027353)
XLA Ops:
  0.6 0.0 copy-start
  0.7 0.9 copy-done
  1.6 5.9 %collective-permute-start = (bf16[256,128]{1,0:T(8,128)(2,1)S(1)}, bf16[256,128]{1,0:T(8,128)(2,1)S(1)}, u32[]{:S(2)}, u32[]{:S(2)}) collective-permute-start(bf16[256,128]{1,0:T(8,128)(2,1)S(1)} %constant_dynamic-slice_fusion), channel_id=1, source_target_pairs={{0,0},{32,1},{64,2},{96,3},{16,4},{48,5},{80,6},{112,7},{128,8},{1... | collective-permute-start | bytes 196616 | tf_op jit(solution)/shard_map/ppermute | solution.py:188
  7.5 5.3 %backward.1 = (bf16[1024,2048]{1,0:T(8,128)(2,1)}, bf16[2,4,256,128]{3,2,1,0:T(8,128)(2,1)}) custom-call(s32[8]{0:T(128)} %bitcast.5, s32[96]{0:T(128)} %bitcast.6, bf16[96,128,128]{2,1,0:T(8,128)(2,1)} %bitcast.4, bf16[1024,256]{1,0:T(8,128)(2,1)} %refs_4_.1, bf16[128,256]{1,0:T(8,128)(2,1)} %weight.3), custom_call_target="tpu_custom_call" | custom-call | flops 603979776 | bytes 8388608 | tf_op jit(solution)/shard_map/backward/pallas_call | solution.py:190
  12.9 0.0 copy-start.3
  12.9 5.4 %all_to_all.25.terms = bf16[2,4,256,128]{3,2,1,0:T(8,128)(2,1)S(1)} all-to-all(bf16[2,4,256,128]{3,2,1,0:T(8,128)(2,1)} %get-tuple-element.8), channel_id=1, replica_groups=mesh['zl'=4,'x'=4,'zh'=4,'y'=4,'c'=2] {'c'}, dimensions={0} | all-to-all | bytes 1048576 | tf_op jit(solution)/shard_map/all_to_all | solution.py:175
  18.2 3.9 %collective-permute-done.quarter = bf16[256,128]{1,0:T(8,128)(2,1)S(1)} collective-permute-done((bf16[256,128]{1,0:T(8,128)(2,1)S(1)}, bf16[256,128]{1,0:T(8,128)(2,1)S(1)}, u32[]{:S(2)}, u32[]{:S(2)}) %collective-permute-start) | collective-permute-done | bytes 65568 | tf_op jit(solution)/shard_map/ppermute | solution.py:188
  22.1 0.1 pack.1
  22.2 11.4 %all_to_all.26.received = bf16[4,512,128]{2,1,0:T(8,128)(2,1)S(1)} all-to-all(bf16[4,512,128]{2,1,0:T(8,128)(2,1)S(1)} %pack.1), channel_id=1, replica_groups=mesh['zl'=4,'x'=4,'zh'=4,'y'=4,'c'=2] {'y'}, dimensions={0} | all-to-all | bytes 1048576 | tf_op jit(solution)/shard_map/all_to_all | solution.py:175
  33.7 1.9 %collective-permute-start.1 = (bf16[4,256,128]{2,1,0:T(8,128)(2,1)S(1)}, bf16[4,256,128]{2,1,0:T(8,128)(2,1)S(1)}, u32[]{:S(2)}, u32[]{:S(2)}) collective-permute-start(bf16[4,256,128]{2,1,0:T(8,128)(2,1)S(1)} %get-tuple-element.9.held), channel_id=1, source_target_pairs={{0,1},{1,0},{2,3},{3,2},{4,5},{5,4},{6,7},{7,6},{8,9},{9,8},{10,11... | collective-permute-start | bytes 786440 | tf_op jit(solution)/shard_map/ppermute | solution.py:214
  35.6 13.0 %collective-permute-start.2 = (bf16[256,128]{1,0:T(8,128)(2,1)S(1)}, bf16[256,128]{1,0:T(8,128)(2,1)S(1)}, u32[]{:S(2)}, u32[]{:S(2)}) collective-permute-start(bf16[256,128]{1,0:T(8,128)(2,1)S(1)} %get-tuple-element.10), channel_id=1, source_target_pairs={{0,0},{1,32},{2,64},{3,96},{4,16},{5,48},{6,80},{7,112},{8,128},{9... | collective-permute-start | bytes 196616 | tf_op jit(solution)/shard_map/ppermute | solution.py:213
  48.6 2.2 %copy-done.1 = bf16[1024,2048]{1,0:T(8,128)(2,1)S(1)} copy-done((bf16[1024,2048]{1,0:T(8,128)(2,1)S(1)}, bf16[1024,2048]{1,0:T(8,128)(2,1)}, u32[]{:S(2)}) %copy-start.1) | copy-done | bytes 4194328
  50.8 0.7 half.1.refs_3_
  51.5 1.4 %copy-done.2 = bf16[1024,2048]{1,0:T(8,128)(2,1)S(1)} copy-done((bf16[1024,2048]{1,0:T(8,128)(2,1)S(1)}, bf16[1024,2048]{1,0:T(8,128)(2,1)}, u32[]{:S(2)}) %copy-start.2) | copy-done | bytes 4194328
  53.0 1.0 forward.1
  53.9 26.1 %all_to_all.27.parts = bf16[16,96,128]{2,1,0:T(8,128)(2,1)S(1)} all-to-all(bf16[16,96,128]{2,1,0:T(8,128)(2,1)S(1)} %forward.1), channel_id=1, replica_groups=mesh['zl'=4,'x'=4,'zh'=4,'y'=4,'c'=2] {'zl','x'}, dimensions={0} | all-to-all | bytes 786432 | tf_op jit(solution)/shard_map/all_to_all | solution.py:175
  80.0 1.9 %collective-permute-start.3 = (f32[16,128]{1,0:T(8,128)S(1)}, f32[16,128]{1,0:T(8,128)S(1)}, u32[]{:S(2)}, u32[]{:S(2)}) collective-permute-start(f32[16,128]{1,0:T(8,128)S(1)} %weight.2), channel_id=1, source_target_pairs={{0,1},{1,0},{2,3},{3,2},{4,5},{5,4},{6,7},{7,6},{8,9},{9,8},{10,11... | collective-permute-start | bytes 24584 | tf_op jit(solution)/shard_map/ppermute | solution.py:235
  82.0 1.1 collective-permute-done.3
  83.1 0.7 broadcast_in_dim.2
  83.8 8.0 %all-to-all-start.3 = ((f32[16,16,128]{2,1,0:T(8,128)}), f32[16,16,128]{2,1,0:T(8,128)S(1)}, u32[]{:S(2)}, u32[]{:S(2)}) async-start(f32[16,16,128]{2,1,0:T(8,128)} %broadcast_in_dim.2), calls=%async_computation.3 | async-start | bytes 262144 | tf_op jit(solution)/shard_map/all_to_all | solution.py:175
  91.8 15.1 %all-to-all-done.3.weight_parts = f32[16,16,128]{2,1,0:T(8,128)S(1)} async-done(((f32[16,16,128]{2,1,0:T(8,128)}), f32[16,16,128]{2,1,0:T(8,128)S(1)}, u32[]{:S(2)}, u32[]{:S(2)}) %all-to-all-start.3) | async-done | bytes 131104 | tf_op jit(solution)/shard_map/all_to_all | solution.py:175
  106.9 0.1 gather.1
  107.0 20.3 %all_to_all.28.received = bf16[16,144,128]{2,1,0:T(8,128)(2,1)S(1)} all-to-all(bf16[16,144,128]{2,1,0:T(8,128)(2,1)S(1)} %gather.1), channel_id=1, replica_groups=mesh['zl'=4,'x'=4,'zh'=4,'y'=4,'c'=2] {'zl','x'}, dimensions={0} | all-to-all | bytes 1179648 | tf_op jit(solution)/shard_map/all_to_all | solution.py:175
  127.3 1.1 output.1
  (12 shorter events, 0.1 us)
Async XLA Ops:
  0.6 1.0 copy-start
  1.6 20.5 %collective-permute-start = (bf16[256,128]{1,0:T(8,128)(2,1)S(1)}, bf16[256,128]{1,0:T(8,128)(2,1)S(1)}, u32[]{:S(2)}, u32[]{:S(2)}) collective-permute-start(bf16[256,128]{1,0:T(8,128)(2,1)S(1)} %constant_dynamic-slice_fusion), channel_id=1, source_target_pairs={{0,0},{32,1},{64,2},{96,3},{16,4},{48,5},{80,6},{112,7},{128,8},{1... | collective-permute-start | bytes 196616 | tf_op jit(solution)/shard_map/ppermute | solution.py:188
  12.9 38.6 %copy-start.3 = (bf16[1024,256]{1,0:T(8,128)(2,1)S(1)}, bf16[1024,256]{1,0:T(8,128)(2,1)}, u32[]{:S(2)}) copy-start(bf16[1024,256]{1,0:T(8,128)(2,1)} %refs_4_.1) | copy-start | bytes 1572868
  33.7 17.9 %collective-permute-start.1 = (bf16[4,256,128]{2,1,0:T(8,128)(2,1)S(1)}, bf16[4,256,128]{2,1,0:T(8,128)(2,1)S(1)}, u32[]{:S(2)}, u32[]{:S(2)}) collective-permute-start(bf16[4,256,128]{2,1,0:T(8,128)(2,1)S(1)} %get-tuple-element.9.held), channel_id=1, source_target_pairs={{0,1},{1,0},{2,3},{3,2},{4,5},{5,4},{6,7},{7,6},{8,9},{9,8},{10,11... | collective-permute-start | bytes 786440 | tf_op jit(solution)/shard_map/ppermute | solution.py:214
  35.6 15.9 %collective-permute-start.2 = (bf16[256,128]{1,0:T(8,128)(2,1)S(1)}, bf16[256,128]{1,0:T(8,128)(2,1)S(1)}, u32[]{:S(2)}, u32[]{:S(2)}) collective-permute-start(bf16[256,128]{1,0:T(8,128)(2,1)S(1)} %get-tuple-element.10), channel_id=1, source_target_pairs={{0,0},{1,32},{2,64},{3,96},{4,16},{5,48},{6,80},{7,112},{8,128},{9... | collective-permute-start | bytes 196616 | tf_op jit(solution)/shard_map/ppermute | solution.py:213
  48.6 2.2 %copy-start.1 = (bf16[1024,2048]{1,0:T(8,128)(2,1)S(1)}, bf16[1024,2048]{1,0:T(8,128)(2,1)}, u32[]{:S(2)}) copy-start(bf16[1024,2048]{1,0:T(8,128)(2,1)} %get-tuple-element.7.dense.refs_1_) | copy-start | bytes 12582916
  50.8 2.2 %copy-start.2 = (bf16[1024,2048]{1,0:T(8,128)(2,1)S(1)}, bf16[1024,2048]{1,0:T(8,128)(2,1)}, u32[]{:S(2)}) copy-start(bf16[1024,2048]{1,0:T(8,128)(2,1)} %get-tuple-element.7.dense.refs_1_) | copy-start | bytes 12582916
  51.5 75.8 %copy-start.4 = (bf16[128,256]{1,0:T(8,128)(2,1)S(1)}, bf16[128,256]{1,0:T(8,128)(2,1)}, u32[]{:S(2)}) copy-start(bf16[128,256]{1,0:T(8,128)(2,1)} %weight.3) | copy-start | bytes 196612
  80.0 3.1 %collective-permute-start.3 = (f32[16,128]{1,0:T(8,128)S(1)}, f32[16,128]{1,0:T(8,128)S(1)}, u32[]{:S(2)}, u32[]{:S(2)}) collective-permute-start(f32[16,128]{1,0:T(8,128)S(1)} %weight.2), channel_id=1, source_target_pairs={{0,1},{1,0},{2,3},{3,2},{4,5},{5,4},{6,7},{7,6},{8,9},{9,8},{10,11... | collective-permute-start | bytes 24584 | tf_op jit(solution)/shard_map/ppermute | solution.py:235
  83.8 23.1 %all-to-all-start.3 = ((f32[16,16,128]{2,1,0:T(8,128)}), f32[16,16,128]{2,1,0:T(8,128)S(1)}, u32[]{:S(2)}, u32[]{:S(2)}) async-start(f32[16,16,128]{2,1,0:T(8,128)} %broadcast_in_dim.2), calls=%async_computation.3 | async-start | bytes 262144 | tf_op jit(solution)/shard_map/all_to_all | solution.py:175

commit v4 on v2

v4 whole, which is shorter than its diff:
```python
import math

import jax
import jax.numpy as jnp
from jax import lax
from jax.experimental import pallas as pl
from jax.experimental.pallas import tpu as pltpu
from jax.sharding import Mesh
from jax.sharding import PartitionSpec as P

REP = ("zl", "x")
ROW = ("zh", "y", "c")
YC = ("y", "c")
F32 = jnp.float32
BF16 = jnp.bfloat16
VMEM = pl.BlockSpec(memory_space=pltpu.VMEM)
SMEM = pl.BlockSpec(memory_space=pltpu.SMEM)
PARAMS = pltpu.CompilerParams(vmem_limit_bytes=40 * 1024 * 1024)

PAIRS = [
    ((zh * 4 + k % 4) * 32 + q + 16 * (k // 4), q * 32 + zh * 8 + k)
    for q in range(16)
    for zh in range(4)
    for k in range(8)
]


def split_high_low(value):
    high = value.astype(BF16)
    return high, (value - high.astype(F32)).astype(BF16)


def backward_kernel(counts, cols, tiles, node_grad, weight, dense, terms, grad_t):
    def clear(b, carry):
        dense[pl.ds(pl.multiple_of(b * 128, 128), 128), :] = jnp.zeros((128, 2048), BF16)
        return carry

    lax.fori_loop(0, 8, clear, 0)
    start = jnp.int32(0)
    for b in range(8):
        count = counts[b]

        def place(i, carry, b=b, start=start):
            slot = start + i
            col = pl.multiple_of(cols[slot] * 128, 128)
            dense[b * 128 : (b + 1) * 128, pl.ds(col, 128)] = tiles[slot]
            return carry

        lax.fori_loop(0, count, place, 0)
        start = start + count
    grad_t[...] = lax.dot_general(
        weight[...], node_grad[...], (((1,), (1,)), ((), ())), preferred_element_type=F32
    ).astype(BF16)
    for k in range(8):
        term = jnp.dot(
            grad_t[...], dense[:, k * 256 : (k + 1) * 256], preferred_element_type=F32
        )
        terms[k] = term.T.astype(BF16)


def forward_kernel(scaling, dense, quarters, node_grad, message, total):
    for k in range(8):
        term = jnp.dot(
            dense[:, k * 256 : (k + 1) * 256], quarters[k], preferred_element_type=F32
        )
        if k == 0:
            total[...] = term
        else:
            total[...] += term
    partial = total[...].astype(BF16)
    message[:, 0:64, :] = partial.reshape(16, 64, 128)
    term = lax.dot_general(
        partial, node_grad[...], (((0,), (0,)), ((), ())), preferred_element_type=F32
    )
    term = term * scaling
    message[:, 64:80, :] = jnp.concatenate(
        [term[:, 0:128].reshape(16, 8, 128), term[:, 128:256].reshape(16, 8, 128)], axis=1
    ).astype(BF16)


def sum_parts(parts, first, last):
    total = parts[0, first:last, :].astype(F32)
    for i in range(1, parts.shape[0]):
        total = total + parts[i, first:last, :].astype(F32)
    return total


def reduce_kernel(parts, terms, piece, message):
    piece[...] = sum_parts(parts, 0, 64).astype(BF16)
    high, low = split_high_low(sum_parts(parts, 64, 80))
    message[:, 0:256, :] = terms[...]
    message[:, 256:272, :] = jnp.broadcast_to(high[None], (8, 16, 128))
    message[:, 272:288, :] = jnp.broadcast_to(low[None], (8, 16, 128))


def column_kernel(parts, message):
    message[:, 0:64, :] = sum_parts(parts, 0, 256).astype(BF16).reshape(4, 64, 128)
    high, low = split_high_low(sum_parts(parts, 256, 272) + sum_parts(parts, 272, 288))
    message[:, 64:80, :] = jnp.broadcast_to(high[None], (4, 16, 128))
    message[:, 80:96, :] = jnp.broadcast_to(low[None], (4, 16, 128))


def column_sum_kernel(parts, column_piece):
    column_piece[...] = sum_parts(parts, 0, 64).astype(BF16)


def gather_kernel(piece, column_piece, parts, message):
    weight_part = (sum_parts(parts, 64, 80) + sum_parts(parts, 80, 96)).astype(BF16)
    message[:, 0:64, :] = jnp.broadcast_to(piece[...][None], (16, 64, 128))
    message[:, 64:128, :] = jnp.broadcast_to(column_piece[...][None], (16, 64, 128))
    message[:, 128:144, :] = jnp.broadcast_to(weight_part[None], (16, 16, 128))


def output_kernel(received, weight, output, weight_grad, feature_grad):
    parts = received[:, 128:144, :].astype(F32)
    weight_grad[:, 0:128] = parts[:, 0:8, :].reshape(128, 128)
    weight_grad[:, 128:256] = parts[:, 8:16, :].reshape(128, 128)
    for a in range(16):
        row = a % 4 * 256 + a // 4 * 64
        feature_grad[row : row + 64, :] = received[a, 64:128, :]
    for quarter in range(4):
        aggregate = received[quarter * 4 : quarter * 4 + 4, 0:64, :].reshape(256, 128)
        output[quarter * 256 : (quarter + 1) * 256, :] = jnp.dot(
            aggregate, weight[...], preferred_element_type=F32
        ).astype(BF16)


def shape(*dims, dtype=BF16):
    return jax.ShapeDtypeStruct(dims, dtype)


def call(kernel, name, outs, ins, scratch=(), flops=0, moved=1 << 20):
    return pl.pallas_call(
        kernel,
        out_shape=outs,
        in_specs=ins,
        out_specs=jax.tree.map(lambda _: VMEM, outs),
        scratch_shapes=list(scratch),
        compiler_params=PARAMS,
        cost_estimate=pl.CostEstimate(flops=flops, bytes_accessed=moved, transcendentals=0),
        name=name,
    )


def exchange(block, axes):
    return lax.all_to_all(block, axes, 0, 0)


def body(features, tile_values, tile_counts, tile_columns, weight, node_grad):
    rep_index = lax.axis_index(REP)
    scaling = 1.0 / math.sqrt(features.shape[0] * 32)

    quarter = lax.dynamic_slice_in_dim(features, (rep_index % 4) * 256, 256, axis=0)
    quarter = lax.ppermute(quarter, REP + ROW, PAIRS)
    dense, terms = call(
        backward_kernel,
        "backward",
        (shape(1024, 2048), shape(8, 256, 128)),
        [SMEM, SMEM, VMEM, VMEM, VMEM],
        [pltpu.VMEM((128, 1024), BF16)],
        flops=2 * 128 * 1024 * 2304,
        moved=8 << 20,
    )(tile_counts[0, 0], tile_columns[0, 0], tile_values[0, 0], node_grad, weight)

    quarter, terms = lax.optimization_barrier((quarter, terms))
    quarters = exchange(jnp.broadcast_to(quarter[None], (8, 256, 128)), YC)
    message = call(
        lambda *refs: forward_kernel(scaling, *refs),
        "forward",
        shape(16, 80, 128),
        [VMEM] * 3,
        [pltpu.VMEM((1024, 128), F32)],
        flops=2 * 128 * 1024 * 2304,
        moved=6 << 20,
    )(dense, quarters, node_grad)
    parts = exchange(message, REP)

    piece, message = call(
        reduce_kernel, "reduce", (shape(64, 128), shape(8, 288, 128)), [VMEM] * 2
    )(parts, terms)
    parts = exchange(message, YC)
    message = call(column_kernel, "column", shape(4, 96, 128), [VMEM])(parts)
    parts = exchange(message, "zh")
    column_piece = call(column_sum_kernel, "column_sum", shape(64, 128), [VMEM])(parts)
    column_piece = lax.ppermute(column_piece, REP + ROW, [(d, s) for s, d in PAIRS])
    message = call(gather_kernel, "gather", shape(16, 144, 128), [VMEM] * 3)(
        piece, column_piece, parts
    )
    received = exchange(message, REP)
    return call(
        output_kernel,
        "output",
        (shape(1024, 256), shape(128, 256, dtype=F32), shape(1024, 128)),
        [VMEM] * 2,
    )(received, weight)


def solution(mesh):
    fine = Mesh(mesh.devices.reshape(4, 4, 4, 4, 2), REP + ROW)
    placed = (
        P(ROW, None),
        P(REP, ROW, None, None, None),
        P(REP, ROW, None),
        P(REP, ROW, None),
        P(),
        P(ROW, None),
    )
    return jax.shard_map(
        body,
        mesh=fine,
        in_specs=placed,
        out_specs=(P(ROW, None), P(), P(ROW, None)),
        check_vma=False,
    )
```

time: 128 us -> 128 us (level)
  blocking collectives: 37 us -> 92.7 us
  starting transfers between devices: 57.4 us -> 10.4 us
  waiting for transfers between devices: 17.1 us -> 12.9 us
  other arithmetic: 1.58 us -> 0 us
    all_to_all x2 -> x5, blocking collectives: 37 us -> 92.7 us  [exchange(): return lax.all_to_all(block, axes, 0, 0)]
    ppermute x4 -> x1, starting transfers between devices: 32.5 us -> 4.49 us  [body(): lax.ppermute(column_piece, REP + ROW, [(d, s) for s, d in PAIRS])]
    all_to_all x3 -> x0, starting transfers between devices: 18.9 us -> none  [exchange(): return lax.all_to_all(block, axes, 0, 0)]
    all_to_all x3 -> x0, waiting for transfers between devices: 2.73 us -> none  [exchange(): return lax.all_to_all(block, axes, 0, 0)]
    ppermute x4 -> x1, waiting for transfers between devices: 6.96 us -> 5.65 us  [body(): lax.ppermute(column_piece, REP + ROW, [(d, s) for s, d in PAIRS])]
    pallas_call x4 -> x7, Pallas kernels: 5.98 us -> 5.13 us  [the longest x1 2.23 us: body(): call(backward_kernel, 'backward', (shape(1024, 2048), shape(8, 256, 128))...]
    unnamed x14 -> x12, local copies, waits for them, and re-layouts: 6.01 us -> 6 us
  transfers between devices with their start and end apart: 8 -> 2, of which waited for: 3 -> 2; matrix products, arithmetic and copies ran while one was open for 1% -> 0% of each run, Pallas kernels for 2% -> 2%
where the time goes in v4:
time: 128 us
  blocking collectives  92.7 us (72%)
  waiting for transfers between devices  12.9 us (10%)
  starting transfers between devices  10.4 us (8%)
  local copies, waits for them, and re-layouts  6.08 us (5%)
  Pallas kernels  5.13 us (4%)
    all_to_all x5, blocking collectives, exchange(): return lax.all_to_all(block, axes, 0, 0)  92.7 us
    ppermute x1, waiting for transfers between devices, body(): quarter = lax.ppermute(quarter, REP + ROW, PAIRS)  7.24 us
    unnamed x12, local copies, waits for them, and re-layouts  6 us
    ppermute x1, starting transfers between devices, body(): quarter = lax.ppermute(quarter, REP + ROW, PAIRS)  5.93 us
    ppermute x1, waiting for transfers between devices, body(): lax.ppermute(column_piece, REP + ROW, [(d, s) for s, d in PAIRS])  5.65 us
    ppermute x1, starting transfers between devices, body(): lax.ppermute(column_piece, REP + ROW, [(d, s) for s, d in PAIRS])  4.49 us
  transfers between devices with their start and end apart: 2, of which 2 were waited for; matrix products, arithmetic and copies ran while one was open for 0% of the time, Pallas kernels for 2%

profile of v4, /device:TPU:24, one launch (start us, length us, event | category | flops | bytes accessed | tf_op | source)
XLA Modules:
  0.0 128.0 jit_solution(6799899044762370662)
XLA Ops:
  0.6 0.0 copy-start
  0.7 0.9 copy-done
  1.6 5.9 %collective-permute-start = (bf16[256,128]{1,0:T(8,128)(2,1)S(1)}, bf16[256,128]{1,0:T(8,128)(2,1)S(1)}, u32[]{:S(2)}, u32[]{:S(2)}) collective-permute-start(bf16[256,128]{1,0:T(8,128)(2,1)S(1)} %constant_dynamic-slice_fusion), channel_id=1, source_target_pairs={{0,0},{32,1},{64,2},{96,3},{16,4},{48,5},{80,6},{112,7},{128,8},{1... | collective-permute-start | bytes 196616 | tf_op jit(solution)/shard_map/ppermute | solution.py:154
  7.5 0.0 copy-start.1
  7.5 1.9 %copy-done.1 = bf16[1,1,96,128,128]{4,3,2,1,0:T(8,128)(2,1)S(1)} copy-done((bf16[1,1,96,128,128]{4,3,2,1,0:T(8,128)(2,1)S(1)}, bf16[1,1,96,128,128]{4,3,2,1,0:T(8,128)(2,1)}, u32[]{:S(2)}) %copy-start.1) | copy-done | bytes 3145752
  9.4 1.0 copy-done.2
  10.5 0.8 copy-done.3
  11.3 0.7 copy-done.4
  12.0 0.7 copy-done.5
  12.6 2.2 %backward.1 = (bf16[1024,2048]{1,0:T(8,128)(2,1)S(1)}, bf16[8,256,128]{2,1,0:T(8,128)(2,1)S(1)}) custom-call(s32[8]{0:T(128)S(1)} %bitcast.4, s32[96]{0:T(128)S(1)} %bitcast.5, bf16[96,128,128]{2,1,0:T(8,128)(2,1)S(1)} %bitcast.3, bf16[1024,256]{1,0:T(8,128)(2,1)S(1)} %copy-done.2, bf16[128,256]{1,0:T(8,128)(2,1)S(1)} %copy-done.3), custom_call_target="tpu_custom_call" | custom-call | flops 603979776 | bytes 8388608 | tf_op jit(solution)/shard_map/backward/pallas_call | solution.py:155
  14.9 7.2 %collective-permute-done = bf16[256,128]{1,0:T(8,128)(2,1)S(1)} collective-permute-done((bf16[256,128]{1,0:T(8,128)(2,1)S(1)}, bf16[256,128]{1,0:T(8,128)(2,1)S(1)}, u32[]{:S(2)}, u32[]{:S(2)}) %collective-permute-start) | collective-permute-done | bytes 65568 | tf_op jit(solution)/shard_map/ppermute | solution.py:154
  22.1 0.1 broadcast_in_dim.2
  22.2 12.6 %all_to_all.25.refs_1_ = bf16[8,256,128]{2,1,0:T(8,128)(2,1)S(1)} all-to-all(bf16[8,256,128]{2,1,0:T(8,128)(2,1)S(1)} %broadcast_in_dim.2), channel_id=1, replica_groups=mesh['zl'=4,'x'=4,'zh'=4,'y'=4,'c'=2] {'y','c'}, dimensions={0} | all-to-all | bytes 1048576 | tf_op jit(solution)/shard_map/all_to_all | solution.py:146
  34.8 1.5 %forward.1 = bf16[16,80,128]{2,1,0:T(8,128)(2,1)S(1)} custom-call(bf16[1024,2048]{1,0:T(8,128)(2,1)S(1)} %get-tuple-element.9.refs_0_, bf16[8,256,128]{2,1,0:T(8,128)(2,1)S(1)} %all_to_all.25.refs_1_, bf16[1024,256]{1,0:T(8,128)(2,1)S(1)} %copy-done.2), custom_call_target="tpu_custom_call" | custom-call | flops 603979776 | bytes 6291456 | tf_op jit(solution)/shard_map/forward/pallas_call | solution.py:167
  36.3 19.5 %all_to_all.26.parts = bf16[16,80,128]{2,1,0:T(8,128)(2,1)S(1)} all-to-all(bf16[16,80,128]{2,1,0:T(8,128)(2,1)S(1)} %forward.1), channel_id=1, replica_groups=mesh['zl'=4,'x'=4,'zh'=4,'y'=4,'c'=2] {'zl','x'}, dimensions={0} | all-to-all | bytes 655360 | tf_op jit(solution)/shard_map/all_to_all | solution.py:146
  55.9 0.1 reduce.1
  55.9 13.5 %all_to_all.27.parts = bf16[8,288,128]{2,1,0:T(8,128)(2,1)S(1)} all-to-all(bf16[8,288,128]{2,1,0:T(8,128)(2,1)S(1)} %get-tuple-element.14), channel_id=1, replica_groups=mesh['zl'=4,'x'=4,'zh'=4,'y'=4,'c'=2] {'y','c'}, dimensions={0} | all-to-all | bytes 1179648 | tf_op jit(solution)/shard_map/all_to_all | solution.py:146
  69.4 0.1 column.1
  69.5 22.0 %all_to_all.28.parts = bf16[4,96,128]{2,1,0:T(8,128)(2,1)S(1)} all-to-all(bf16[4,96,128]{2,1,0:T(8,128)(2,1)S(1)} %column.1), channel_id=1, replica_groups=mesh['zl'=4,'x'=4,'zh'=4,'y'=4,'c'=2] {'zh'}, dimensions={0} | all-to-all | bytes 196608 | tf_op jit(solution)/shard_map/all_to_all | solution.py:146
  91.5 4.5 %collective-permute-start.1 = (bf16[64,128]{1,0:T(8,128)(2,1)S(1)}, bf16[64,128]{1,0:T(8,128)(2,1)S(1)}, u32[]{:S(2)}, u32[]{:S(2)}) collective-permute-start(bf16[64,128]{1,0:T(8,128)(2,1)S(1)} %column_sum.1), channel_id=1, source_target_pairs={{0,0},{1,32},{2,64},{3,96},{4,16},{5,48},{6,80},{7,112},{8,128},{9... | collective-permute-start | bytes 49160 | tf_op jit(solution)/shard_map/ppermute | solution.py:185
  96.0 5.7 %collective-permute-done.1.column_piece = bf16[64,128]{1,0:T(8,128)(2,1)S(1)} collective-permute-done((bf16[64,128]{1,0:T(8,128)(2,1)S(1)}, bf16[64,128]{1,0:T(8,128)(2,1)S(1)}, u32[]{:S(2)}, u32[]{:S(2)}) %collective-permute-start.1) | collective-permute-done | bytes 16416 | tf_op jit(solution)/shard_map/ppermute | solution.py:185
  101.7 0.1 gather.1
  101.8 25.1 %all_to_all.29.received = bf16[16,144,128]{2,1,0:T(8,128)(2,1)S(1)} all-to-all(bf16[16,144,128]{2,1,0:T(8,128)(2,1)S(1)} %gather.1), channel_id=1, replica_groups=mesh['zl'=4,'x'=4,'zh'=4,'y'=4,'c'=2] {'zl','x'}, dimensions={0} | all-to-all | bytes 1179648 | tf_op jit(solution)/shard_map/all_to_all | solution.py:146
  126.8 1.1 output.1
  (6 shorter events, 0.0 us)
Async XLA Ops:
  0.6 1.0 copy-start
  1.6 20.5 %collective-permute-start = (bf16[256,128]{1,0:T(8,128)(2,1)S(1)}, bf16[256,128]{1,0:T(8,128)(2,1)S(1)}, u32[]{:S(2)}, u32[]{:S(2)}) collective-permute-start(bf16[256,128]{1,0:T(8,128)(2,1)S(1)} %constant_dynamic-slice_fusion), channel_id=1, source_target_pairs={{0,0},{32,1},{64,2},{96,3},{16,4},{48,5},{80,6},{112,7},{128,8},{1... | collective-permute-start | bytes 196616 | tf_op jit(solution)/shard_map/ppermute | solution.py:154
  7.5 1.9 %copy-start.1 = (bf16[1,1,96,128,128]{4,3,2,1,0:T(8,128)(2,1)S(1)}, bf16[1,1,96,128,128]{4,3,2,1,0:T(8,128)(2,1)}, u32[]{:S(2)}) copy-start(bf16[1,1,96,128,128]{4,3,2,1,0:T(8,128)(2,1)} %param.7) | copy-start | bytes 9437188
  9.4 1.0 copy-start.2
  10.5 0.8 copy-start.3
  11.3 0.7 copy-start.4
  12.0 0.7 copy-start.5
  91.5 10.1 %collective-permute-start.1 = (bf16[64,128]{1,0:T(8,128)(2,1)S(1)}, bf16[64,128]{1,0:T(8,128)(2,1)S(1)}, u32[]{:S(2)}, u32[]{:S(2)}) collective-permute-start(bf16[64,128]{1,0:T(8,128)(2,1)S(1)} %column_sum.1), channel_id=1, source_target_pairs={{0,0},{1,32},{2,64},{3,96},{4,16},{5,48},{6,80},{7,112},{8,128},{9... | collective-permute-start | bytes 49160 | tf_op jit(solution)/shard_map/ppermute | solution.py:185

commit v5 on v3

--- a/solution.py
+++ b/solution.py
@@ -16,12 +16,16 @@
 SMEM = pl.BlockSpec(memory_space=pltpu.SMEM)
 HBM = pl.BlockSpec(memory_space=pltpu.HBM)
 
-PAIRS = [
-    ((zh * 4 + k % 4) * 32 + q + 16 * (k // 4), q * 32 + zh * 8 + k)
-    for q in range(16)
-    for zh in range(4)
-    for k in range(8)
-]
+NEAR = ((1, 2, 3, 0), (2, 3, 0, 1))
+
+
+def pair(q, zh, k):
+    home = k // 4 * 2 + q // 8
+    a = NEAR[q // 8][(zh - home) % 4] * 4 + k % 4
+    return a * 32 + q + k // 4 * 16, q * 32 + zh * 8 + k
+
+
+PAIRS = [pair(q, zh, k) for q in range(16) for zh in range(4) for k in range(8)]
 SWAP = [(0, 1), (1, 0)]
 
 
@@ -33,9 +37,31 @@
     return dense[:, pl.ds(pl.multiple_of(k * 256, 256), 256)]
 
 
+def fill(counts, cols, tiles, dense):
+    def clear(b, carry):
+        dense[pl.ds(pl.multiple_of(b * 128, 128), 128), :] = jnp.zeros((128, 2048), BF16)
+        return carry
+
+    lax.fori_loop(0, 8, clear, 0)
+    yield
+    start = jnp.int32(0)
+    for b in range(8):
+        count = counts[b]
+
+        def place(i, carry, b=b, start=start):
+            slot = start + i
+            col = pl.multiple_of(cols[slot] * 128, 128)
+            dense[b * 128 : (b + 1) * 128, pl.ds(col, 128)] = tiles[slot]
+            return carry
+
+        lax.fori_loop(0, count, place, 0)
+        start = start + count
+    yield
+
+
 def backward_kernel(
-    counts, cols, tiles_hbm, grad_hbm, weight_hbm, dense, terms,
-    tiles, node_grad, weight, grad_t, sems,
+    counts, cols, tiles_hbm, grad_hbm, weight_hbm, terms,
+    tiles, node_grad, weight, dense, grad_t, sems,
 ):
     copies = [
         pltpu.make_async_copy(weight_hbm, weight, sems.at[0]),
@@ -44,30 +70,15 @@
     ]
     for copy in copies:
         copy.start()
-
-    def clear(b, carry):
-        dense[pl.ds(pl.multiple_of(b * 128, 128), 128), :] = jnp.zeros((128, 2048), BF16)
-        return carry
-
-    lax.fori_loop(0, 8, clear, 0)
+    filling = fill(counts, cols, tiles, dense)
+    next(filling)
     copies[0].wait()
     copies[1].wait()
     grad_t[...] = lax.dot_general(
         weight[...], node_grad[...], (((1,), (1,)), ((), ())), preferred_element_type=F32
     ).astype(BF16)
     copies[2].wait()
-    start = jnp.int32(0)
-    for b in range(8):
-        count = counts[b]
-
-        def place(i, carry, b=b, start=start):
-            slot = start + i
-            col = pl.multiple_of(cols[slot] * 128, 128)
-            dense[b * 128 : (b + 1) * 128, pl.ds(col, 128)] = tiles[slot]
-            return carry
-
-        lax.fori_loop(0, count, place, 0)
-        start = start + count
+    next(filling)
     for k in range(8):
         term = jnp.dot(
             grad_t[...], dense[:, k * 256 : (k + 1) * 256], preferred_element_type=F32
@@ -89,7 +100,9 @@
     held[...] = received[:, 0:256, :]
 
 
-def half_kernel(core, dense, held, total):
+def half_kernel(core, counts, cols, tiles, held, dense, total):
+    for _ in fill(counts, cols, tiles, dense):
+        pass
     for y in range(4):
         term = jnp.dot(columns(dense, 2 * y + core[0]), held[y], preferred_element_type=F32)
         if y == 0:
@@ -117,30 +130,27 @@
     ).astype(BF16)
 
 
-def weight_kernel(parts, weight_part):
-    total = parts[0, 80:96, :].astype(F32)
-    for a in range(1, 16):
-        total = total + parts[a, 80:96, :].astype(F32)
-    weight_part[...] = total
-
-
-def reduce_kernel(parts, piece):
+def reduce_kernel(parts, piece, weight_part):
     total = parts[0, 0:64, :].astype(F32)
     for a in range(1, 16):
         total = total + parts[a, 0:64, :].astype(F32)
     piece[0:64, :] = total.astype(BF16)
     for part in range(4):
         total = parts[part, 64:80, :].astype(F32)
-        for zh in range(1, 4):
-            total = total + parts[zh * 4 + part, 64:80, :].astype(F32)
+        for zl in range(1, 4):
+            total = total + parts[zl * 4 + part, 64:80, :].astype(F32)
         piece[64 + part * 16 : 80 + part * 16, :] = total.astype(BF16)
+    total = parts[0, 80:96, :].astype(F32)
+    for a in range(1, 16):
+        total = total + parts[a, 80:96, :].astype(F32)
+    weight_part[...] = jnp.broadcast_to(total.astype(BF16)[None], (32, 16, 128))
 
 
 def gather_kernel(piece, weight_parts, message):
     message[:, 0:128, :] = jnp.broadcast_to(piece[...][None], (16, 128, 128))
-    total = weight_parts[0]
-    for i in range(1, 16):
-        total = total + weight_parts[i]
+    total = weight_parts[0].astype(F32)
+    for r in range(1, 32):
+        total = total + weight_parts[r].astype(F32)
     message[:, 128:144, :] = jnp.broadcast_to(total.astype(BF16)[None], (16, 16, 128))
 
 
@@ -175,10 +185,6 @@
     return lax.all_to_all(block, axes, 0, 0)
 
 
-def broadcast(block, count, axes):
-    return exchange(jnp.broadcast_to(block[None], (count, *block.shape)), axes)
-
-
 def body(features, tile_values, tile_counts, tile_columns, weight, node_grad):
     rep_index = lax.axis_index(REP)
     core = lax.axis_index("c").astype(jnp.int32).reshape(1)
@@ -187,22 +193,24 @@
     quarter = lax.dynamic_slice_in_dim(features, (rep_index % 4) * 256, 256, axis=0)
     quarter = lax.ppermute(quarter, REP + ROW, PAIRS)
 
-    dense, terms = call(
+    counts, cols, tiles = tile_counts[0, 0], tile_columns[0, 0], tile_values[0, 0]
+    terms = call(
         backward_kernel,
         "backward",
-        (shape(1024, 2048), shape(2, 4, 256, 128)),
+        shape(2, 4, 256, 128),
         [SMEM, SMEM, HBM, HBM, HBM],
         [
             pltpu.VMEM((96, 128, 128), BF16),
             pltpu.VMEM((1024, 256), BF16),
             pltpu.VMEM((128, 256), BF16),
+            pltpu.VMEM((1024, 2048), BF16),
             pltpu.VMEM((128, 1024), BF16),
             pltpu.SemaphoreType.DMA((3,)),
         ],
         flops=2 * 128 * 1024 * 2304,
         moved=8 << 20,
         limit=58,
-    )(tile_counts[0, 0], tile_columns[0, 0], tile_values[0, 0], node_grad, weight)
+    )(counts, cols, tiles, node_grad, weight)
     terms = exchange(terms, "c")
     message = call(pack_kernel, "pack", shape(4, 512, 128), [VMEM] * 2)(terms, quarter)
     received = exchange(message, "y")
@@ -212,14 +220,14 @@
     )(received)
     column_sum = lax.ppermute(column_sum, REP + ROW, [(d, s) for s, d in PAIRS])
     theirs = lax.ppermute(held, "c", SWAP)
-    half = call(
+    dense, half = call(
         half_kernel,
         "half",
-        shape(1024, 128, dtype=F32),
-        [SMEM, VMEM, VMEM],
+        (shape(1024, 2048), shape(1024, 128, dtype=F32)),
+        [SMEM, SMEM, SMEM, VMEM, VMEM],
         flops=2 * 128 * 1024 * 1024,
         moved=3 << 20,
-    )(core, dense, held)
+    )(core, counts, cols, tiles, held)
     message = call(
         lambda *refs: forward_kernel(scaling, *refs),
         "forward",
@@ -231,10 +239,10 @@
     )(core, dense, theirs, half, node_grad, column_sum)
     parts = exchange(message, REP)
 
-    weight_part = call(weight_kernel, "weight", shape(16, 128, dtype=F32), [VMEM])(parts)
-    weight_other = lax.ppermute(weight_part, "c", SWAP)
-    piece = call(reduce_kernel, "reduce", shape(128, 128), [VMEM])(parts)
-    weight_parts = broadcast(weight_part + weight_other, 16, ("zh", "y"))
+    piece, weight_part = call(
+        reduce_kernel, "reduce", (shape(128, 128), shape(32, 16, 128)), [VMEM]
+    )(parts)
+    weight_parts = exchange(weight_part, ROW)
     message = call(gather_kernel, "gather", shape(16, 144, 128), [VMEM] * 2)(piece, weight_parts)
     received = exchange(message, REP)
     return call(

time: 130 us -> 128 us (0.985)
  blocking collectives: 63.1 us -> 83.2 us
  waiting for transfers between devices: 20.1 us -> 7.27 us
  starting transfers between devices: 30.8 us -> 22.4 us
  local copies, waits for them, and re-layouts: 5.23 us -> 1.96 us
  Pallas kernels: 8.4 us -> 11.1 us
    all_to_all x4 -> x5, blocking collectives: 63.1 us -> 83.2 us  [exchange(): return lax.all_to_all(block, axes, 0, 0)]
    all_to_all x1 -> x0, waiting for transfers between devices: 15.1 us -> none  [exchange(): return lax.all_to_all(block, axes, 0, 0)]
    ppermute x1, starting transfers between devices: 5.93 us -> 14.5 us  [body(): quarter = lax.ppermute(quarter, REP + ROW, PAIRS)]
    all_to_all x1 -> x0, starting transfers between devices: 8 us -> none  [exchange(): return lax.all_to_all(block, axes, 0, 0)]
    ppermute x1, waiting for transfers between devices: 0.01 us -> 7.27 us  [body(): column_sum = lax.ppermute(column_sum, REP + ROW, [(d, s) for s, d in PAIRS])]
    ppermute x1, starting transfers between devices: 13 us -> 5.99 us  [body(): column_sum = lax.ppermute(column_sum, REP + ROW, [(d, s) for s, d in PAIRS])]
    ppermute x1, waiting for transfers between devices: 3.86 us -> 0.01 us  [body(): quarter = lax.ppermute(quarter, REP + ROW, PAIRS)]
    unnamed x10 -> x12, local copies, waits for them, and re-layouts: 4.56 us -> 1.96 us
  transfers between devices with their start and end apart: 5 -> 3, of which waited for: 3 -> 1; matrix products, arithmetic and copies ran while one was open for 0% -> 0% of each run, Pallas kernels for 5% -> 6%
where the time goes in v5:
time: 128 us; the launch traced here: 127 us
  blocking collectives  83.2 us (65%)
  starting transfers between devices  22.4 us (18%)
  Pallas kernels  11.1 us (9%)
  waiting for transfers between devices  7.27 us (6%)
  local copies, waits for them, and re-layouts  1.96 us (2%)
    all_to_all x5, blocking collectives, exchange(): return lax.all_to_all(block, axes, 0, 0)  83.2 us
    ppermute x1, starting transfers between devices, body(): quarter = lax.ppermute(quarter, REP + ROW, PAIRS)  14.5 us
    ppermute x1, waiting for transfers between devices, body(): column_sum = lax.ppermute(column_sum, REP + ROW, [(d, s) for s, d in PAIRS])  7.27 us
    ppermute x1, starting transfers between devices, body(): column_sum = lax.ppermute(column_sum, REP + ROW, [(d, s) for s, d in PAIRS])  5.99 us
    pallas_call x1, Pallas kernels, body(): call(backward_kernel, 'backward', shape(2, 4, 256, 128), [SMEM, SMEM, HBM...  4.71 us
  transfers between devices with their start and end apart: 3, of which 1 were waited for; matrix products, arithmetic and copies ran while one was open for 0% of the time, Pallas kernels for 6%

profile of v5, /device:TPU:24, one launch (start us, length us, event | category | flops | bytes accessed | tf_op | source)
XLA Modules:
  0.0 126.7 jit_solution(4892502405887586746)
XLA Ops:
  0.6 0.0 copy-start
  0.6 0.0 copy-start.5
  0.7 0.0 copy-start.4
  0.7 0.0 copy-start.1
  0.7 0.9 copy-done
  1.6 14.5 %collective-permute-start = (bf16[256,128]{1,0:T(8,128)(2,1)S(1)}, bf16[256,128]{1,0:T(8,128)(2,1)S(1)}, u32[]{:S(2)}, u32[]{:S(2)}) collective-permute-start(bf16[256,128]{1,0:T(8,128)(2,1)S(1)} %constant_dynamic-slice_fusion), channel_id=1, source_target_pairs={{128,0},{160,1},{192,2},{224,3},{400,4},{432,5},{464,6},{496,7},{2... | collective-permute-start | bytes 196616 | tf_op jit(solution)/shard_map/ppermute | solution.py:194
  16.1 4.7 %backward.1 = bf16[2,4,256,128]{3,2,1,0:T(8,128)(2,1)} custom-call(s32[8]{0:T(128)} %bitcast.6, s32[96]{0:T(128)} %bitcast.8, bf16[96,128,128]{2,1,0:T(8,128)(2,1)} %bitcast.4, bf16[1024,256]{1,0:T(8,128)(2,1)} %refs_4_.1, bf16[128,256]{1,0:T(8,128)(2,1)} %weight.1), custom_call_target="tpu_custom_call" | custom-call | flops 603979776 | bytes 8388608 | tf_op jit(solution)/shard_map/backward/pallas_call | solution.py:197
  20.8 5.2 %all_to_all.25.terms = bf16[2,4,256,128]{3,2,1,0:T(8,128)(2,1)S(1)} all-to-all(bf16[2,4,256,128]{3,2,1,0:T(8,128)(2,1)} %backward.1), channel_id=1, replica_groups=mesh['zl'=4,'x'=4,'zh'=4,'y'=4,'c'=2] {'c'}, dimensions={0} | all-to-all | bytes 1048576 | tf_op jit(solution)/shard_map/all_to_all | solution.py:185
  26.1 0.0 collective-permute-done.quarter
  26.1 0.1 pack.1
  26.2 12.0 %all_to_all.26.received = bf16[4,512,128]{2,1,0:T(8,128)(2,1)S(1)} all-to-all(bf16[4,512,128]{2,1,0:T(8,128)(2,1)S(1)} %pack.1), channel_id=1, replica_groups=mesh['zl'=4,'x'=4,'zh'=4,'y'=4,'c'=2] {'y'}, dimensions={0} | all-to-all | bytes 1048576 | tf_op jit(solution)/shard_map/all_to_all | solution.py:185
  38.2 0.7 split.1
  38.9 1.9 %collective-permute-start.1 = (bf16[4,256,128]{2,1,0:T(8,128)(2,1)}, bf16[4,256,128]{2,1,0:T(8,128)(2,1)}, u32[]{:S(2)}, u32[]{:S(2)}) collective-permute-start(bf16[4,256,128]{2,1,0:T(8,128)(2,1)} %get-tuple-element.9.held), channel_id=1, source_target_pairs={{0,1},{1,0},{2,3},{3,2},{4,5},{5,4},{6,7},{7,6},{8,9},{9,8},{10,11... | collective-permute-start | bytes 786440 | tf_op jit(solution)/shard_map/ppermute | solution.py:222
  40.8 6.0 %collective-permute-start.2 = (bf16[256,128]{1,0:T(8,128)(2,1)S(1)}, bf16[256,128]{1,0:T(8,128)(2,1)S(1)}, u32[]{:S(2)}, u32[]{:S(2)}) collective-permute-start(bf16[256,128]{1,0:T(8,128)(2,1)S(1)} %get-tuple-element.12), channel_id=1, source_target_pairs={{0,128},{1,160},{2,192},{3,224},{4,400},{5,432},{6,464},{7,496},{8... | collective-permute-start | bytes 196616 | tf_op jit(solution)/shard_map/ppermute | solution.py:221
  46.9 2.3 %half.1 = (bf16[1024,2048]{1,0:T(8,128)(2,1)S(1)}, f32[1024,128]{1,0:T(8,128)S(1)}) custom-call(s32[1]{0:T(128)} %bitcast.core.refs_0_, s32[8]{0:T(128)S(1)} %bitcast.7, s32[96]{0:T(128)S(1)} %bitcast.9, bf16[96,128,128]{2,1,0:T(8,128)(2,1)S(1)} %bitcast.5, bf16[4,256,128]{2,1,0:T(8,128)(2,1)} %get-tuple-element.9.held), custom_call_target="tpu_custom_call" | custom-call | flops 268435456 | bytes 3145728 | tf_op jit(solution)/shard_map/half/pallas_call | solution.py:223
  49.2 7.3 %collective-permute-done.2.refs_5_ = bf16[256,128]{1,0:T(8,128)(2,1)S(1)} collective-permute-done((bf16[256,128]{1,0:T(8,128)(2,1)S(1)}, bf16[256,128]{1,0:T(8,128)(2,1)S(1)}, u32[]{:S(2)}, u32[]{:S(2)}) %collective-permute-start.2) | collective-permute-done | bytes 65568 | tf_op jit(solution)/shard_map/ppermute | solution.py:221
  56.4 1.0 copy-done.2
  57.5 2.0 %forward.1 = bf16[16,96,128]{2,1,0:T(8,128)(2,1)S(1)} custom-call(s32[1]{0:T(128)} %bitcast.core.refs_0_, bf16[1024,2048]{1,0:T(8,128)(2,1)S(1)} %get-tuple-element.10.refs_1_, bf16[4,256,128]{2,1,0:T(8,128)(2,1)} %collective-permute-done.1.refs_2_, f32[1024,128]{1,0:T(8,128)S(1)} %get-tuple-element.11.refs_3_, bf16[1024,256]{1,0:T(8,128)(2,1)S(1)} %copy-done.2, ...), custom_call_target="tpu_custom_call" | custom-call | flops 335544320 | bytes 3145728 | tf_op jit(solution)/shard_map/forward/pallas_call | solution.py:231
  59.4 21.5 %all_to_all.27.parts = bf16[16,96,128]{2,1,0:T(8,128)(2,1)S(1)} all-to-all(bf16[16,96,128]{2,1,0:T(8,128)(2,1)S(1)} %forward.1), channel_id=1, replica_groups=mesh['zl'=4,'x'=4,'zh'=4,'y'=4,'c'=2] {'zl','x'}, dimensions={0} | all-to-all | bytes 786432 | tf_op jit(solution)/shard_map/all_to_all | solution.py:185
  80.9 0.1 reduce.1
  81.0 21.2 %all_to_all.28.weight_parts = bf16[32,16,128]{2,1,0:T(8,128)(2,1)S(1)} all-to-all(bf16[32,16,128]{2,1,0:T(8,128)(2,1)S(1)} %get-tuple-element.14), channel_id=1, replica_groups=mesh['zl'=4,'x'=4,'zh'=4,'y'=4,'c'=2] {'zh','y','c'}, dimensions={0} | all-to-all | bytes 262144 | tf_op jit(solution)/shard_map/all_to_all | solution.py:185
  102.2 0.1 gather.1
  102.3 23.3 %all_to_all.29.received = bf16[16,144,128]{2,1,0:T(8,128)(2,1)S(1)} all-to-all(bf16[16,144,128]{2,1,0:T(8,128)(2,1)S(1)} %gather.1), channel_id=1, replica_groups=mesh['zl'=4,'x'=4,'zh'=4,'y'=4,'c'=2] {'zl','x'}, dimensions={0} | all-to-all | bytes 1179648 | tf_op jit(solution)/shard_map/all_to_all | solution.py:185
  125.6 1.1 output.1
  (8 shorter events, 0.0 us)
Async XLA Ops:
  0.6 1.0 copy-start
  0.6 46.2 %copy-start.5 = (s32[1,1,96]{2,1,0:T(1,128)S(1)}, s32[1,1,96]{2,1,0:T(1,128)}, u32[]{:S(2)}) copy-start(s32[1,1,96]{2,1,0:T(1,128)} %param.9) | copy-start | bytes 1156
  0.7 46.2 %copy-start.4 = (s32[1,1,8]{2,1,0:T(1,128)S(1)}, s32[1,1,8]{2,1,0:T(1,128)}, u32[]{:S(2)}) copy-start(s32[1,1,8]{2,1,0:T(1,128)} %param.8) | copy-start | bytes 100
  0.7 46.2 %copy-start.1 = (bf16[1,1,96,128,128]{4,3,2,1,0:T(8,128)(2,1)S(1)}, bf16[1,1,96,128,128]{4,3,2,1,0:T(8,128)(2,1)}, u32[]{:S(2)}) copy-start(bf16[1,1,96,128,128]{4,3,2,1,0:T(8,128)(2,1)} %param.7) | copy-start | bytes 9437188
  1.6 24.5 %collective-permute-start = (bf16[256,128]{1,0:T(8,128)(2,1)S(1)}, bf16[256,128]{1,0:T(8,128)(2,1)S(1)}, u32[]{:S(2)}, u32[]{:S(2)}) collective-permute-start(bf16[256,128]{1,0:T(8,128)(2,1)S(1)} %constant_dynamic-slice_fusion), channel_id=1, source_target_pairs={{128,0},{160,1},{192,2},{224,3},{400,4},{432,5},{464,6},{496,7},{2... | collective-permute-start | bytes 196616 | tf_op jit(solution)/shard_map/ppermute | solution.py:194
  38.9 17.5 %collective-permute-start.1 = (bf16[4,256,128]{2,1,0:T(8,128)(2,1)}, bf16[4,256,128]{2,1,0:T(8,128)(2,1)}, u32[]{:S(2)}, u32[]{:S(2)}) collective-permute-start(bf16[4,256,128]{2,1,0:T(8,128)(2,1)} %get-tuple-element.9.held), channel_id=1, source_target_pairs={{0,1},{1,0},{2,3},{3,2},{4,5},{5,4},{6,7},{7,6},{8,9},{9,8},{10,11... | collective-permute-start | bytes 786440 | tf_op jit(solution)/shard_map/ppermute | solution.py:222
  40.8 15.6 %collective-permute-start.2 = (bf16[256,128]{1,0:T(8,128)(2,1)S(1)}, bf16[256,128]{1,0:T(8,128)(2,1)S(1)}, u32[]{:S(2)}, u32[]{:S(2)}) collective-permute-start(bf16[256,128]{1,0:T(8,128)(2,1)S(1)} %get-tuple-element.12), channel_id=1, source_target_pairs={{0,128},{1,160},{2,192},{3,224},{4,400},{5,432},{6,464},{7,496},{8... | collective-permute-start | bytes 196616 | tf_op jit(solution)/shard_map/ppermute | solution.py:221
  56.4 1.0 copy-start.2
  57.5 68.1 %copy-start.3 = (bf16[128,256]{1,0:T(8,128)(2,1)S(1)}, bf16[128,256]{1,0:T(8,128)(2,1)}, u32[]{:S(2)}) copy-start(bf16[128,256]{1,0:T(8,128)(2,1)} %weight.1) | copy-start | bytes 196612

commit v6 on v5

--- a/solution.py
+++ b/solution.py
@@ -19,22 +19,29 @@
 NEAR = ((1, 2, 3, 0), (2, 3, 0, 1))
 
 
+def farther(q, half):
+    return 1 - (((q >> 1) + 1) >> 1 & 1) ^ half
+
+
 def pair(q, zh, k):
-    home = k // 4 * 2 + q // 8
-    a = NEAR[q // 8][(zh - home) % 4] * 4 + k % 4
-    return a * 32 + q + k // 4 * 16, q * 32 + zh * 8 + k
+    half, turn = k // 4, k % 2
+    if k // 2 % 2 != farther(q, half):
+        turn += 2
+    a = NEAR[q // 8][(zh - half * 2 - q // 8) % 4] * 4 + (q + turn) % 4
+    return a * 32 + q + half * 16, q * 32 + zh * 8 + k
+
+
+def quarter_of(a, s):
+    turn = (a - s) % 4
+    far = farther(s % 16, s // 16)
+    return jnp.where(turn < 2, far, 1 - far) * 2 + turn % 2
 
 
 PAIRS = [pair(q, zh, k) for q in range(16) for zh in range(4) for k in range(8)]
-SWAP = [(0, 1), (1, 0)]
 
 
 def shape(*dims, dtype=BF16):
     return jax.ShapeDtypeStruct(dims, dtype)
-
-
-def columns(dense, k):
-    return dense[:, pl.ds(pl.multiple_of(k * 256, 256), 256)]
 
 
 def fill(counts, cols, tiles, dense):
@@ -97,35 +104,31 @@
     for y in range(1, 4):
         total = total + received[y, 256:512, :].astype(F32)
     column_sum[...] = total.astype(BF16)
-    held[...] = received[:, 0:256, :]
-
-
-def half_kernel(core, counts, cols, tiles, held, dense, total):
+    for c in range(2):
+        held[c] = received[:, 0:256, :]
+
+
+def dense_kernel(counts, cols, tiles, dense):
     for _ in fill(counts, cols, tiles, dense):
         pass
-    for y in range(4):
-        term = jnp.dot(columns(dense, 2 * y + core[0]), held[y], preferred_element_type=F32)
-        if y == 0:
+
+
+def forward_kernel(scaling, dense, held, node_grad, message, total):
+    for k in range(8):
+        term = jnp.dot(
+            dense[:, k * 256 : (k + 1) * 256], held[k % 2, k // 2], preferred_element_type=F32
+        )
+        if k == 0:
             total[...] = term
-        else:
-            total[...] += term
-
-
-def forward_kernel(scaling, core, dense, held, half, node_grad, column_sum, message, total):
-    for y in range(4):
-        term = jnp.dot(columns(dense, 2 * y + 1 - core[0]), held[y], preferred_element_type=F32)
-        if y == 0:
-            total[...] = half[...] + term
         else:
             total[...] += term
     partial = total[...].astype(BF16)
     message[:, 0:64, :] = partial.reshape(16, 64, 128)
-    message[:, 64:80, :] = column_sum[...].reshape(16, 16, 128)
     term = lax.dot_general(
         partial, node_grad[...], (((0,), (0,)), ((), ())), preferred_element_type=F32
     )
     term = term * scaling
-    message[:, 80:96, :] = jnp.concatenate(
+    message[:, 64:80, :] = jnp.concatenate(
         [term[:, 0:128].reshape(16, 8, 128), term[:, 128:256].reshape(16, 8, 128)], axis=1
     ).astype(BF16)
 
@@ -136,13 +139,13 @@
         total = total + parts[a, 0:64, :].astype(F32)
     piece[0:64, :] = total.astype(BF16)
     for part in range(4):
-        total = parts[part, 64:80, :].astype(F32)
+        total = parts[part, 80:96, :].astype(F32)
         for zl in range(1, 4):
-            total = total + parts[zl * 4 + part, 64:80, :].astype(F32)
+            total = total + parts[zl * 4 + part, 80:96, :].astype(F32)
         piece[64 + part * 16 : 80 + part * 16, :] = total.astype(BF16)
-    total = parts[0, 80:96, :].astype(F32)
+    total = parts[0, 64:80, :].astype(F32)
     for a in range(1, 16):
-        total = total + parts[a, 80:96, :].astype(F32)
+        total = total + parts[a, 64:80, :].astype(F32)
     weight_part[...] = jnp.broadcast_to(total.astype(BF16)[None], (32, 16, 128))
 
 
@@ -154,7 +157,7 @@
     message[:, 128:144, :] = jnp.broadcast_to(total.astype(BF16)[None], (16, 16, 128))
 
 
-def output_kernel(received, weight, output, weight_grad, feature_grad):
+def output_kernel(order, received, weight, output, weight_grad, feature_grad):
     parts = received[:, 128:144, :].astype(F32)
     weight_grad[:, 0:128] = parts[:, 0:8, :].reshape(128, 128)
     weight_grad[:, 128:256] = parts[:, 8:16, :].reshape(128, 128)
@@ -163,7 +166,8 @@
         output[zq * 256 : (zq + 1) * 256, :] = jnp.dot(
             aggregate, weight[...], preferred_element_type=F32
         ).astype(BF16)
-        feature_grad[zq * 256 : (zq + 1) * 256, :] = received[
+        row = pl.multiple_of(order[zq] * 256, 256)
+        feature_grad[pl.ds(row, 256), :] = received[
             :, 64 + zq * 16 : 80 + zq * 16, :
         ].reshape(256, 128)
 
@@ -187,13 +191,11 @@
 
 def body(features, tile_values, tile_counts, tile_columns, weight, node_grad):
     rep_index = lax.axis_index(REP)
-    core = lax.axis_index("c").astype(jnp.int32).reshape(1)
+    row_index = lax.axis_index(ROW)
     scaling = 1.0 / math.sqrt(features.shape[0] * 32)
-
-    quarter = lax.dynamic_slice_in_dim(features, (rep_index % 4) * 256, 256, axis=0)
-    quarter = lax.ppermute(quarter, REP + ROW, PAIRS)
-
     counts, cols, tiles = tile_counts[0, 0], tile_columns[0, 0], tile_values[0, 0]
+    order = quarter_of(jnp.arange(4, dtype=jnp.int32), row_index).astype(jnp.int32)
+
     terms = call(
         backward_kernel,
         "backward",
@@ -211,32 +213,33 @@
         moved=8 << 20,
         limit=58,
     )(counts, cols, tiles, node_grad, weight)
+    start = quarter_of(rep_index, row_index) * 256
+    quarter = lax.dynamic_slice_in_dim(features, start, 256, axis=0)
+    quarter, terms = lax.optimization_barrier((quarter, terms))
+    quarter = lax.ppermute(quarter, REP + ROW, PAIRS)
     terms = exchange(terms, "c")
     message = call(pack_kernel, "pack", shape(4, 512, 128), [VMEM] * 2)(terms, quarter)
     received = exchange(message, "y")
 
     held, column_sum = call(
-        split_kernel, "split", (shape(4, 256, 128), shape(256, 128)), [VMEM]
+        split_kernel, "split", (shape(2, 4, 256, 128), shape(256, 128)), [VMEM]
     )(received)
     column_sum = lax.ppermute(column_sum, REP + ROW, [(d, s) for s, d in PAIRS])
-    theirs = lax.ppermute(held, "c", SWAP)
-    dense, half = call(
-        half_kernel,
-        "half",
-        (shape(1024, 2048), shape(1024, 128, dtype=F32)),
-        [SMEM, SMEM, SMEM, VMEM, VMEM],
-        flops=2 * 128 * 1024 * 1024,
-        moved=3 << 20,
-    )(core, counts, cols, tiles, held)
+    dense = call(dense_kernel, "dense", shape(1024, 2048), [SMEM, SMEM, VMEM])(
+        counts, cols, tiles
+    )
+    held, dense = lax.optimization_barrier((held, dense))
+    held = exchange(held, "c")
     message = call(
         lambda *refs: forward_kernel(scaling, *refs),
         "forward",
-        shape(16, 96, 128),
-        [SMEM] + [VMEM] * 5,
+        shape(16, 80, 128),
+        [VMEM] * 3,
         [pltpu.VMEM((1024, 128), F32)],
-        flops=2 * 128 * 1024 * 1280,
+        flops=2 * 128 * 1024 * 2304,
         moved=3 << 20,
-    )(core, dense, theirs, half, node_grad, column_sum)
+    )(dense, held, node_grad)
+    message = jnp.concatenate([message, column_sum.reshape(16, 16, 128)], axis=1)
     parts = exchange(message, REP)
 
     piece, weight_part = call(
@@ -249,8 +252,8 @@
         output_kernel,
         "output",
         (shape(1024, 256), shape(128, 256, dtype=F32), shape(1024, 128)),
-        [VMEM, VMEM],
-    )(received, weight)
+        [SMEM, VMEM, VMEM],
+    )(order, received, weight)
 
 
 def solution(mesh):

time: 128 us -> 124 us (0.969)
  blocking collectives: 83.2 us -> 63.1 us
  waiting for transfers between devices: 7.27 us -> 16.9 us
  starting transfers between devices: 22.4 us -> 30.2 us
    all_to_all x5, blocking collectives: 83.2 us -> 63.1 us  [exchange(): return lax.all_to_all(block, axes, 0, 0)]
    all_to_all x0 -> x1, waiting for transfers between devices: none -> 16.9 us  [exchange(): return lax.all_to_all(block, axes, 0, 0)]
    ppermute x1, waiting for transfers between devices: 7.27 us -> 0.01 us  [body(): column_sum = lax.ppermute(column_sum, REP + ROW, [(d, s) for s, d in PAIRS])]
    all_to_all x0 -> x1, starting transfers between devices: none -> 5.02 us  [exchange(): return lax.all_to_all(block, axes, 0, 0)]
    ppermute x1, starting transfers between devices: 5.99 us -> 10.8 us  [body(): column_sum = lax.ppermute(column_sum, REP + ROW, [(d, s) for s, d in PAIRS])]
    pallas_call x3, Pallas kernels: 4.99 us -> 2.62 us  [the longest x1 1.51 us: body(): call(lambda *refs: forward_kernel(scaling, *refs), 'forward', shape(16, 8...]
    ppermute x1 -> x0, starting transfers between devices: 1.91 us -> none  [body(): theirs = lax.ppermute(held, 'c', SWAP)]
  transfers between devices with their start and end apart: 3 -> 3, of which waited for: 1 -> 1; matrix products, arithmetic and copies ran while one was open for 0% -> 0% of each run, Pallas kernels for 6% -> 2%
where the time goes in v6:
time: 124 us; the launch traced here: 122 us
  blocking collectives  63.1 us (51%)
  starting transfers between devices  30.2 us (24%)
  waiting for transfers between devices  16.9 us (14%)
  Pallas kernels  10 us (8%)
    all_to_all x5, blocking collectives, exchange(): return lax.all_to_all(block, axes, 0, 0)  63.1 us
    all_to_all x1, waiting for transfers between devices, exchange(): return lax.all_to_all(block, axes, 0, 0)  16.9 us
    ppermute x1, starting transfers between devices, body(): quarter = lax.ppermute(quarter, REP + ROW, PAIRS)  14.4 us
    ppermute x1, starting transfers between devices, body(): column_sum = lax.ppermute(column_sum, REP + ROW, [(d, s) for s, d in PAIRS])  10.8 us
    all_to_all x1, starting transfers between devices, exchange(): return lax.all_to_all(block, axes, 0, 0)  5.02 us
    pallas_call x1, Pallas kernels, body(): call(backward_kernel, 'backward', shape(2, 4, 256, 128), [SMEM, SMEM, HBM...  4.7 us
  transfers between devices with their start and end apart: 3, of which 1 were waited for; matrix products, arithmetic and copies ran while one was open for 0% of the time, Pallas kernels for 2%

profile of v6, /device:TPU:24, one launch (start us, length us, event | category | flops | bytes accessed | tf_op | source)
XLA Modules:
  0.0 122.0 jit_solution(3509587301552919080)
XLA Ops:
  0.6 0.0 copy-start
  0.6 0.0 copy-start.5
  0.7 0.0 copy-start.4
  0.7 0.0 copy-start.1
  0.8 0.8 copy-done
  1.6 4.7 %backward.1 = bf16[2,4,256,128]{3,2,1,0:T(8,128)(2,1)} custom-call(s32[8]{0:T(128)} %bitcast.6, s32[96]{0:T(128)} %bitcast.8, bf16[96,128,128]{2,1,0:T(8,128)(2,1)} %bitcast.4, bf16[1024,256]{1,0:T(8,128)(2,1)} %refs_2_.1, bf16[128,256]{1,0:T(8,128)(2,1)} %weight.1), custom_call_target="tpu_custom_call" | custom-call | flops 603979776 | bytes 8388608 | tf_op jit(solution)/shard_map/backward/pallas_call | solution.py:199
  6.3 14.4 %collective-permute-start = (bf16[256,128]{1,0:T(8,128)(2,1)S(1)}, bf16[256,128]{1,0:T(8,128)(2,1)S(1)}, u32[]{:S(2)}, u32[]{:S(2)}) collective-permute-start(bf16[256,128]{1,0:T(8,128)(2,1)S(1)} %constant_dynamic-slice_fusion), channel_id=1, source_target_pairs={{192,0},{224,1},{128,2},{160,3},{400,4},{432,5},{464,6},{496,7},{3... | collective-permute-start | bytes 196616 | tf_op jit(solution)/shard_map/ppermute | solution.py:219
  20.7 5.3 %all_to_all.30.terms = bf16[2,4,256,128]{3,2,1,0:T(8,128)(2,1)S(1)} all-to-all(bf16[2,4,256,128]{3,2,1,0:T(8,128)(2,1)} %backward.1), channel_id=1, replica_groups=mesh['zl'=4,'x'=4,'zh'=4,'y'=4,'c'=2] {'c'}, dimensions={0} | all-to-all | bytes 1048576 | tf_op jit(solution)/shard_map/all_to_all | solution.py:189
  26.0 0.1 pack.1
  26.0 12.0 %all_to_all.31.received = bf16[4,512,128]{2,1,0:T(8,128)(2,1)S(1)} all-to-all(bf16[4,512,128]{2,1,0:T(8,128)(2,1)S(1)} %pack.1), channel_id=1, replica_groups=mesh['zl'=4,'x'=4,'zh'=4,'y'=4,'c'=2] {'y'}, dimensions={0} | all-to-all | bytes 1048576 | tf_op jit(solution)/shard_map/all_to_all | solution.py:189
  38.1 0.1 split.1
  38.1 0.0 copy-start.2
  38.2 10.8 %collective-permute-start.1 = (bf16[256,128]{1,0:T(8,128)(2,1)S(1)}, bf16[256,128]{1,0:T(8,128)(2,1)S(1)}, u32[]{:S(2)}, u32[]{:S(2)}) collective-permute-start(bf16[256,128]{1,0:T(8,128)(2,1)S(1)} %get-tuple-element.16), channel_id=1, source_target_pairs={{0,192},{1,224},{2,128},{3,160},{4,400},{5,432},{6,464},{7,496},{8... | collective-permute-start | bytes 196616 | tf_op jit(solution)/shard_map/ppermute | solution.py:227
  49.0 1.0 dense.1.refs_0_
  50.0 4.2 %all_to_all.32.refs_1_ = bf16[2,4,256,128]{3,2,1,0:T(8,128)(2,1)S(1)} all-to-all(bf16[2,4,256,128]{3,2,1,0:T(8,128)(2,1)S(1)} %get-tuple-element.15), channel_id=1, replica_groups=mesh['zl'=4,'x'=4,'zh'=4,'y'=4,'c'=2] {'c'}, dimensions={0} | all-to-all | bytes 1048576 | tf_op jit(solution)/shard_map/all_to_all | solution.py:189
  54.2 1.5 %forward.1 = bf16[16,80,128]{2,1,0:T(8,128)(2,1)S(1)} custom-call(bf16[1024,2048]{1,0:T(8,128)(2,1)S(1)} %dense.1.refs_0_, bf16[2,4,256,128]{3,2,1,0:T(8,128)(2,1)S(1)} %all_to_all.32.refs_1_, bf16[1024,256]{1,0:T(8,128)(2,1)S(1)} %copy-done.2), custom_call_target="tpu_custom_call" | custom-call | flops 603979776 | bytes 3145728 | tf_op jit(solution)/shard_map/forward/pallas_call | solution.py:233
  55.7 0.0 collective-permute-done.1
  55.7 19.0 %all_to_all.33.parts = bf16[16,96,128]{2,1,0:T(8,128)(2,1)S(1)} all-to-all(bf16[16,96,128]{2,1,0:T(8,128)(2,1)S(1)} %pad_maximum_fusion), channel_id=1, replica_groups=mesh['zl'=4,'x'=4,'zh'=4,'y'=4,'c'=2] {'zl','x'}, dimensions={0} | all-to-all | bytes 786432 | tf_op jit(solution)/shard_map/all_to_all | solution.py:189
  74.8 0.1 reduce.1
  74.8 22.6 %all_to_all.34.weight_parts = bf16[32,16,128]{2,1,0:T(8,128)(2,1)S(1)} all-to-all(bf16[32,16,128]{2,1,0:T(8,128)(2,1)S(1)} %get-tuple-element.18), channel_id=1, replica_groups=mesh['zl'=4,'x'=4,'zh'=4,'y'=4,'c'=2] {'zh','y','c'}, dimensions={0} | all-to-all | bytes 262144 | tf_op jit(solution)/shard_map/all_to_all | solution.py:189
  97.5 0.9 gather.1
  98.4 5.0 %all-to-all-start.5 = ((bf16[16,144,128]{2,1,0:T(8,128)(2,1)}), bf16[16,144,128]{2,1,0:T(8,128)(2,1)S(1)}, u32[]{:S(2)}, u32[]{:S(2)}) async-start(bf16[16,144,128]{2,1,0:T(8,128)(2,1)} %gather.1), calls=%async_computation.5 | async-start | bytes 1179648 | tf_op jit(solution)/shard_map/all_to_all | solution.py:189
  103.4 16.9 %all-to-all-done.5.received = bf16[16,144,128]{2,1,0:T(8,128)(2,1)S(1)} async-done(((bf16[16,144,128]{2,1,0:T(8,128)(2,1)}), bf16[16,144,128]{2,1,0:T(8,128)(2,1)S(1)}, u32[]{:S(2)}, u32[]{:S(2)}) %all-to-all-start.5) | async-done | bytes 589856 | tf_op jit(solution)/shard_map/all_to_all | solution.py:189
  120.3 1.7 %output.1 = (bf16[1024,256]{1,0:T(8,128)(2,1)}, f32[128,256]{1,0:T(8,128)}, bf16[1024,128]{1,0:T(8,128)(2,1)}) custom-call(s32[4]{0:T(128)S(1)} %fusion.order, bf16[16,144,128]{2,1,0:T(8,128)(2,1)S(1)} %all-to-all-done.5.received, bf16[128,256]{1,0:T(8,128)(2,1)S(1)} %copy-done.3), custom_call_target="tpu_custom_call" | custom-call | bytes 1048576 | tf_op jit(solution)/shard_map/output/pallas_call | solution.py:251
  (10 shorter events, 0.1 us)
Async XLA Ops:
  0.6 1.0 copy-start
  0.6 48.3 %copy-start.5 = (s32[1,1,96]{2,1,0:T(1,128)S(1)}, s32[1,1,96]{2,1,0:T(1,128)}, u32[]{:S(2)}) copy-start(s32[1,1,96]{2,1,0:T(1,128)} %param.9) | copy-start | bytes 1156
  0.7 48.3 %copy-start.4 = (s32[1,1,8]{2,1,0:T(1,128)S(1)}, s32[1,1,8]{2,1,0:T(1,128)}, u32[]{:S(2)}) copy-start(s32[1,1,8]{2,1,0:T(1,128)} %param.8) | copy-start | bytes 100
  0.7 48.3 %copy-start.1 = (bf16[1,1,96,128,128]{4,3,2,1,0:T(8,128)(2,1)S(1)}, bf16[1,1,96,128,128]{4,3,2,1,0:T(8,128)(2,1)}, u32[]{:S(2)}) copy-start(bf16[1,1,96,128,128]{4,3,2,1,0:T(8,128)(2,1)} %param.7) | copy-start | bytes 9437188
  6.3 19.7 %collective-permute-start = (bf16[256,128]{1,0:T(8,128)(2,1)S(1)}, bf16[256,128]{1,0:T(8,128)(2,1)S(1)}, u32[]{:S(2)}, u32[]{:S(2)}) collective-permute-start(bf16[256,128]{1,0:T(8,128)(2,1)S(1)} %constant_dynamic-slice_fusion), channel_id=1, source_target_pairs={{192,0},{224,1},{128,2},{160,3},{400,4},{432,5},{464,6},{496,7},{3... | collective-permute-start | bytes 196616 | tf_op jit(solution)/shard_map/ppermute | solution.py:219
  38.1 16.0 %copy-start.2 = (bf16[1024,256]{1,0:T(8,128)(2,1)S(1)}, bf16[1024,256]{1,0:T(8,128)(2,1)}, u32[]{:S(2)}) copy-start(bf16[1024,256]{1,0:T(8,128)(2,1)} %refs_2_.1) | copy-start | bytes 1572868
  38.2 17.5 %collective-permute-start.1 = (bf16[256,128]{1,0:T(8,128)(2,1)S(1)}, bf16[256,128]{1,0:T(8,128)(2,1)S(1)}, u32[]{:S(2)}, u32[]{:S(2)}) collective-permute-start(bf16[256,128]{1,0:T(8,128)(2,1)S(1)} %get-tuple-element.16), channel_id=1, source_target_pairs={{0,192},{1,224},{2,128},{3,160},{4,400},{5,432},{6,464},{7,496},{8... | collective-permute-start | bytes 196616 | tf_op jit(solution)/shard_map/ppermute | solution.py:227
  54.2 66.2 %copy-start.3 = (bf16[128,256]{1,0:T(8,128)(2,1)S(1)}, bf16[128,256]{1,0:T(8,128)(2,1)}, u32[]{:S(2)}) copy-start(bf16[128,256]{1,0:T(8,128)(2,1)} %weight.1) | copy-start | bytes 196612
  98.4 22.0 %all-to-all-start.5 = ((bf16[16,144,128]{2,1,0:T(8,128)(2,1)}), bf16[16,144,128]{2,1,0:T(8,128)(2,1)S(1)}, u32[]{:S(2)}, u32[]{:S(2)}) async-start(bf16[16,144,128]{2,1,0:T(8,128)(2,1)} %gather.1), calls=%async_computation.5 | async-start | bytes 1179648 | tf_op jit(solution)/shard_map/all_to_all | solution.py:189

commit v7 on v6

--- a/solution.py
+++ b/solution.py
@@ -66,16 +66,25 @@
     yield
 
 
+def tile_copies(tiles_hbm, tiles, sems):
+    return [
+        pltpu.make_async_copy(
+            tiles_hbm.at[pl.ds(i * 12, 12)], tiles.at[pl.ds(i * 12, 12)], sems.at[i]
+        )
+        for i in range(8)
+    ]
+
+
 def backward_kernel(
     counts, cols, tiles_hbm, grad_hbm, weight_hbm, terms,
     tiles, node_grad, weight, dense, grad_t, sems,
 ):
     copies = [
-        pltpu.make_async_copy(weight_hbm, weight, sems.at[0]),
-        pltpu.make_async_copy(grad_hbm, node_grad, sems.at[1]),
-        pltpu.make_async_copy(tiles_hbm, tiles, sems.at[2]),
+        pltpu.make_async_copy(weight_hbm, weight, sems.at[8]),
+        pltpu.make_async_copy(grad_hbm, node_grad, sems.at[9]),
     ]
-    for copy in copies:
+    loads = tile_copies(tiles_hbm, tiles, sems)
+    for copy in copies + loads:
         copy.start()
     filling = fill(counts, cols, tiles, dense)
     next(filling)
@@ -84,7 +93,8 @@
     grad_t[...] = lax.dot_general(
         weight[...], node_grad[...], (((1,), (1,)), ((), ())), preferred_element_type=F32
     ).astype(BF16)
-    copies[2].wait()
+    for copy in loads:
+        copy.wait()
     next(filling)
     for k in range(8):
         term = jnp.dot(
@@ -207,7 +217,7 @@
             pltpu.VMEM((128, 256), BF16),
             pltpu.VMEM((1024, 2048), BF16),
             pltpu.VMEM((128, 1024), BF16),
-            pltpu.SemaphoreType.DMA((3,)),
+            pltpu.SemaphoreType.DMA((10,)),
         ],
         flops=2 * 128 * 1024 * 2304,
         moved=8 << 20,
@@ -215,7 +225,6 @@
     )(counts, cols, tiles, node_grad, weight)
     start = quarter_of(rep_index, row_index) * 256
     quarter = lax.dynamic_slice_in_dim(features, start, 256, axis=0)
-    quarter, terms = lax.optimization_barrier((quarter, terms))
     quarter = lax.ppermute(quarter, REP + ROW, PAIRS)
     terms = exchange(terms, "c")
     message = call(pack_kernel, "pack", shape(4, 512, 128), [VMEM] * 2)(terms, quarter)

time: 124 us -> 122 us (0.984)
  starting transfers between devices: 30.2 us -> 25 us
  blocking collectives: 63.1 us -> 65.5 us
    ppermute x1, starting transfers between devices: 10.8 us -> 6.38 us  [body(): column_sum = lax.ppermute(column_sum, REP + ROW, [(d, s) for s, d in PAIRS])]
    all_to_all x5, blocking collectives: 63.1 us -> 65.5 us  [exchange(): return lax.all_to_all(block, axes, 0, 0)]
  transfers between devices with their start and end apart: 3 -> 3, of which waited for: 1 -> 2; matrix products, arithmetic and copies ran while one was open for 0% -> 0% of each run, Pallas kernels for 2% -> 6%
where the time goes in v7:
time: 122 us; the launch traced here: 120 us
  blocking collectives  65.5 us (54%)
  starting transfers between devices  25 us (20%)
  waiting for transfers between devices  18 us (15%)
  Pallas kernels  10.1 us (8%)
    all_to_all x5, blocking collectives, exchange(): return lax.all_to_all(block, axes, 0, 0)  65.5 us
    all_to_all x1, waiting for transfers between devices, exchange(): return lax.all_to_all(block, axes, 0, 0)  17 us
    ppermute x1, starting transfers between devices, body(): quarter = lax.ppermute(quarter, REP + ROW, PAIRS)  14.5 us
    ppermute x1, starting transfers between devices, body(): column_sum = lax.ppermute(column_sum, REP + ROW, [(d, s) for s, d in PAIRS])  6.38 us
    pallas_call x1, Pallas kernels, body(): call(backward_kernel, 'backward', shape(2, 4, 256, 128), [SMEM, SMEM, HBM...  4.67 us
    all_to_all x1, starting transfers between devices, exchange(): return lax.all_to_all(block, axes, 0, 0)  4.13 us
  transfers between devices with their start and end apart: 3, of which 2 were waited for; matrix products, arithmetic and copies ran while one was open for 0% of the time, Pallas kernels for 6%

profile of v7, /device:TPU:24, one launch (start us, length us, event | category | flops | bytes accessed | tf_op | source)
XLA Modules:
  0.0 120.4 jit_solution(14837381465620212136)
XLA Ops:
  0.6 0.0 copy-start
  0.6 0.0 copy-start.5
  0.7 0.0 copy-start.4
  0.7 0.0 copy-start.1
  0.8 0.8 copy-done
  1.6 14.5 %collective-permute-start = (bf16[256,128]{1,0:T(8,128)(2,1)S(1)}, bf16[256,128]{1,0:T(8,128)(2,1)S(1)}, u32[]{:S(2)}, u32[]{:S(2)}) collective-permute-start(bf16[256,128]{1,0:T(8,128)(2,1)S(1)} %constant_dynamic-slice_fusion), channel_id=1, source_target_pairs={{192,0},{224,1},{128,2},{160,3},{400,4},{432,5},{464,6},{496,7},{3... | collective-permute-start | bytes 196616 | tf_op jit(solution)/shard_map/ppermute | solution.py:228
  16.1 4.7 %backward.1 = bf16[2,4,256,128]{3,2,1,0:T(8,128)(2,1)} custom-call(s32[8]{0:T(128)} %bitcast.6, s32[96]{0:T(128)} %bitcast.8, bf16[96,128,128]{2,1,0:T(8,128)(2,1)} %bitcast.4, bf16[1024,256]{1,0:T(8,128)(2,1)} %refs_2_.1, bf16[128,256]{1,0:T(8,128)(2,1)} %weight.1), custom_call_target="tpu_custom_call" | custom-call | flops 603979776 | bytes 8388608 | tf_op jit(solution)/shard_map/backward/pallas_call | solution.py:209
  20.8 5.2 %all_to_all.30.terms = bf16[2,4,256,128]{3,2,1,0:T(8,128)(2,1)S(1)} all-to-all(bf16[2,4,256,128]{3,2,1,0:T(8,128)(2,1)} %backward.1), channel_id=1, replica_groups=mesh['zl'=4,'x'=4,'zh'=4,'y'=4,'c'=2] {'c'}, dimensions={0} | all-to-all | bytes 1048576 | tf_op jit(solution)/shard_map/all_to_all | solution.py:199
  26.0 0.1 pack.1
  26.1 12.0 %all_to_all.31.received = bf16[4,512,128]{2,1,0:T(8,128)(2,1)S(1)} all-to-all(bf16[4,512,128]{2,1,0:T(8,128)(2,1)S(1)} %pack.1), channel_id=1, replica_groups=mesh['zl'=4,'x'=4,'zh'=4,'y'=4,'c'=2] {'y'}, dimensions={0} | all-to-all | bytes 1048576 | tf_op jit(solution)/shard_map/all_to_all | solution.py:199
  38.1 0.1 split.1
  38.2 0.0 copy-start.2
  38.2 6.4 %collective-permute-start.1 = (bf16[256,128]{1,0:T(8,128)(2,1)S(1)}, bf16[256,128]{1,0:T(8,128)(2,1)S(1)}, u32[]{:S(2)}, u32[]{:S(2)}) collective-permute-start(bf16[256,128]{1,0:T(8,128)(2,1)S(1)} %get-tuple-element.12), channel_id=1, source_target_pairs={{0,192},{1,224},{2,128},{3,160},{4,400},{5,432},{6,464},{7,496},{8... | collective-permute-start | bytes 196616 | tf_op jit(solution)/shard_map/ppermute | solution.py:236
  44.6 1.1 dense.1.refs_0_
  45.8 4.2 %all_to_all.32.refs_1_ = bf16[2,4,256,128]{3,2,1,0:T(8,128)(2,1)S(1)} all-to-all(bf16[2,4,256,128]{3,2,1,0:T(8,128)(2,1)S(1)} %get-tuple-element.11), channel_id=1, replica_groups=mesh['zl'=4,'x'=4,'zh'=4,'y'=4,'c'=2] {'c'}, dimensions={0} | all-to-all | bytes 1048576 | tf_op jit(solution)/shard_map/all_to_all | solution.py:199
  50.0 1.5 %forward.1 = bf16[16,80,128]{2,1,0:T(8,128)(2,1)S(1)} custom-call(bf16[1024,2048]{1,0:T(8,128)(2,1)S(1)} %dense.1.refs_0_, bf16[2,4,256,128]{3,2,1,0:T(8,128)(2,1)S(1)} %all_to_all.32.refs_1_, bf16[1024,256]{1,0:T(8,128)(2,1)S(1)} %copy-done.2), custom_call_target="tpu_custom_call" | custom-call | flops 603979776 | bytes 3145728 | tf_op jit(solution)/shard_map/forward/pallas_call | solution.py:242
  51.5 1.0 collective-permute-done.1
  52.5 20.3 %all_to_all.33.parts = bf16[16,96,128]{2,1,0:T(8,128)(2,1)S(1)} all-to-all(bf16[16,96,128]{2,1,0:T(8,128)(2,1)S(1)} %pad_maximum_fusion), channel_id=1, replica_groups=mesh['zl'=4,'x'=4,'zh'=4,'y'=4,'c'=2] {'zl','x'}, dimensions={0} | all-to-all | bytes 786432 | tf_op jit(solution)/shard_map/all_to_all | solution.py:199
  72.8 0.1 reduce.1
  72.9 23.8 %all_to_all.34.weight_parts = bf16[32,16,128]{2,1,0:T(8,128)(2,1)S(1)} all-to-all(bf16[32,16,128]{2,1,0:T(8,128)(2,1)S(1)} %get-tuple-element.14), channel_id=1, replica_groups=mesh['zl'=4,'x'=4,'zh'=4,'y'=4,'c'=2] {'zh','y','c'}, dimensions={0} | all-to-all | bytes 262144 | tf_op jit(solution)/shard_map/all_to_all | solution.py:199
  96.7 0.9 gather.1
  97.6 4.1 %all-to-all-start.5 = ((bf16[16,144,128]{2,1,0:T(8,128)(2,1)}), bf16[16,144,128]{2,1,0:T(8,128)(2,1)S(1)}, u32[]{:S(2)}, u32[]{:S(2)}) async-start(bf16[16,144,128]{2,1,0:T(8,128)(2,1)} %gather.1), calls=%async_computation.5 | async-start | bytes 1179648 | tf_op jit(solution)/shard_map/all_to_all | solution.py:199
  101.8 17.0 %all-to-all-done.5.received = bf16[16,144,128]{2,1,0:T(8,128)(2,1)S(1)} async-done(((bf16[16,144,128]{2,1,0:T(8,128)(2,1)}), bf16[16,144,128]{2,1,0:T(8,128)(2,1)S(1)}, u32[]{:S(2)}, u32[]{:S(2)}) %all-to-all-start.5) | async-done | bytes 589856 | tf_op jit(solution)/shard_map/all_to_all | solution.py:199
  118.7 1.7 %output.1 = (bf16[1024,256]{1,0:T(8,128)(2,1)}, f32[128,256]{1,0:T(8,128)}, bf16[1024,128]{1,0:T(8,128)(2,1)}) custom-call(s32[4]{0:T(128)S(1)} %fusion.order, bf16[16,144,128]{2,1,0:T(8,128)(2,1)S(1)} %all-to-all-done.5.received, bf16[128,256]{1,0:T(8,128)(2,1)S(1)} %copy-done.3), custom_call_target="tpu_custom_call" | custom-call | bytes 1048576 | tf_op jit(solution)/shard_map/output/pallas_call | solution.py:260
  (10 shorter events, 0.1 us)
Async XLA Ops:
  0.6 1.0 copy-start
  0.6 44.0 %copy-start.5 = (s32[1,1,96]{2,1,0:T(1,128)S(1)}, s32[1,1,96]{2,1,0:T(1,128)}, u32[]{:S(2)}) copy-start(s32[1,1,96]{2,1,0:T(1,128)} %param.9) | copy-start | bytes 1156
  0.7 44.0 %copy-start.4 = (s32[1,1,8]{2,1,0:T(1,128)S(1)}, s32[1,1,8]{2,1,0:T(1,128)}, u32[]{:S(2)}) copy-start(s32[1,1,8]{2,1,0:T(1,128)} %param.8) | copy-start | bytes 100
  0.7 44.0 %copy-start.1 = (bf16[1,1,96,128,128]{4,3,2,1,0:T(8,128)(2,1)S(1)}, bf16[1,1,96,128,128]{4,3,2,1,0:T(8,128)(2,1)}, u32[]{:S(2)}) copy-start(bf16[1,1,96,128,128]{4,3,2,1,0:T(8,128)(2,1)} %param.7) | copy-start | bytes 9437188
  1.6 24.4 %collective-permute-start = (bf16[256,128]{1,0:T(8,128)(2,1)S(1)}, bf16[256,128]{1,0:T(8,128)(2,1)S(1)}, u32[]{:S(2)}, u32[]{:S(2)}) collective-permute-start(bf16[256,128]{1,0:T(8,128)(2,1)S(1)} %constant_dynamic-slice_fusion), channel_id=1, source_target_pairs={{192,0},{224,1},{128,2},{160,3},{400,4},{432,5},{464,6},{496,7},{3... | collective-permute-start | bytes 196616 | tf_op jit(solution)/shard_map/ppermute | solution.py:228
  38.2 11.7 %copy-start.2 = (bf16[1024,256]{1,0:T(8,128)(2,1)S(1)}, bf16[1024,256]{1,0:T(8,128)(2,1)}, u32[]{:S(2)}) copy-start(bf16[1024,256]{1,0:T(8,128)(2,1)} %refs_2_.1) | copy-start | bytes 1572868
  38.2 14.3 %collective-permute-start.1 = (bf16[256,128]{1,0:T(8,128)(2,1)S(1)}, bf16[256,128]{1,0:T(8,128)(2,1)S(1)}, u32[]{:S(2)}, u32[]{:S(2)}) collective-permute-start(bf16[256,128]{1,0:T(8,128)(2,1)S(1)} %get-tuple-element.12), channel_id=1, source_target_pairs={{0,192},{1,224},{2,128},{3,160},{4,400},{5,432},{6,464},{7,496},{8... | collective-permute-start | bytes 196616 | tf_op jit(solution)/shard_map/ppermute | solution.py:236
  50.0 68.8 %copy-start.3 = (bf16[128,256]{1,0:T(8,128)(2,1)S(1)}, bf16[128,256]{1,0:T(8,128)(2,1)}, u32[]{:S(2)}) copy-start(bf16[128,256]{1,0:T(8,128)(2,1)} %weight.1) | copy-start | bytes 196612
  97.6 21.1 %all-to-all-start.5 = ((bf16[16,144,128]{2,1,0:T(8,128)(2,1)}), bf16[16,144,128]{2,1,0:T(8,128)(2,1)S(1)}, u32[]{:S(2)}, u32[]{:S(2)}) async-start(bf16[16,144,128]{2,1,0:T(8,128)(2,1)} %gather.1), calls=%async_computation.5 | async-start | bytes 1179648 | tf_op jit(solution)/shard_map/all_to_all | solution.py:199

commit v8 on v7

--- a/solution.py
+++ b/solution.py
@@ -2,6 +2,7 @@
 
 import jax
 import jax.numpy as jnp
+import numpy as np
 from jax import lax
 from jax.experimental import pallas as pl
 from jax.experimental.pallas import tpu as pltpu
@@ -19,29 +20,31 @@
 NEAR = ((1, 2, 3, 0), (2, 3, 0, 1))
 
 
-def farther(q, half):
-    return 1 - (((q >> 1) + 1) >> 1 & 1) ^ half
+def chunk(q, zh, k):
+    step = (k // 2 - q // 2) % 4
+    near_half = int((zh - q // 8) % 4 < 2)
+    half = near_half if step < 2 else 1 - near_half
+    return half * 4 + (0 if step in (1, 2) else 2) + k % 2
 
 
 def pair(q, zh, k):
-    half, turn = k // 4, k % 2
-    if k // 2 % 2 != farther(q, half):
-        turn += 2
-    a = NEAR[q // 8][(zh - half * 2 - q // 8) % 4] * 4 + (q + turn) % 4
+    half, quarter = divmod(chunk(q, zh, k), 4)
+    a = NEAR[q // 8][(zh - half * 2 - q // 8) % 4] * 4 + (q + quarter) % 4
     return a * 32 + q + half * 16, q * 32 + zh * 8 + k
 
 
-def quarter_of(a, s):
-    turn = (a - s) % 4
-    far = farther(s % 16, s // 16)
-    return jnp.where(turn < 2, far, 1 - far) * 2 + turn % 2
-
-
 PAIRS = [pair(q, zh, k) for q in range(16) for zh in range(4) for k in range(8)]
+CHUNKS = np.array(
+    [[[chunk(q, zh, k) for k in range(8)] for zh in range(4)] for q in range(16)], np.int32
+)
 
 
 def shape(*dims, dtype=BF16):
     return jax.ShapeDtypeStruct(dims, dtype)
+
+
+def columns(dense, index):
+    return dense[:, pl.ds(pl.multiple_of(index * 256, 256), 256)]
 
 
 def fill(counts, cols, tiles, dense):
@@ -76,7 +79,7 @@
 
 
 def backward_kernel(
-    counts, cols, tiles_hbm, grad_hbm, weight_hbm, terms,
+    chunks, counts, cols, tiles_hbm, grad_hbm, weight_hbm, terms,
     tiles, node_grad, weight, dense, grad_t, sems,
 ):
     copies = [
@@ -97,9 +100,7 @@
         copy.wait()
     next(filling)
     for k in range(8):
-        term = jnp.dot(
-            grad_t[...], dense[:, k * 256 : (k + 1) * 256], preferred_element_type=F32
-        )
+        term = jnp.dot(grad_t[...], columns(dense, chunks[k]), preferred_element_type=F32)
         terms[k % 2, k // 2] = term.T.astype(BF16)
 
 
@@ -123,10 +124,10 @@
         pass
 
 
-def forward_kernel(scaling, dense, held, node_grad, message, total):
+def forward_kernel(scaling, chunks, dense, held, node_grad, message, total):
     for k in range(8):
         term = jnp.dot(
-            dense[:, k * 256 : (k + 1) * 256], held[k % 2, k // 2], preferred_element_type=F32
+            columns(dense, chunks[k]), held[k % 2, k // 2], preferred_element_type=F32
         )
         if k == 0:
             total[...] = term
@@ -204,13 +205,14 @@
     row_index = lax.axis_index(ROW)
     scaling = 1.0 / math.sqrt(features.shape[0] * 32)
     counts, cols, tiles = tile_counts[0, 0], tile_columns[0, 0], tile_values[0, 0]
-    order = quarter_of(jnp.arange(4, dtype=jnp.int32), row_index).astype(jnp.int32)
+    order = (jnp.arange(4, dtype=jnp.int32) - row_index) & 3
+    chunks = jnp.asarray(CHUNKS)[rep_index, lax.axis_index("zh")]
 
     terms = call(
         backward_kernel,
         "backward",
         shape(2, 4, 256, 128),
-        [SMEM, SMEM, HBM, HBM, HBM],
+        [SMEM, SMEM, SMEM, HBM, HBM, HBM],
         [
             pltpu.VMEM((96, 128, 128), BF16),
             pltpu.VMEM((1024, 256), BF16),
@@ -222,8 +224,8 @@
         flops=2 * 128 * 1024 * 2304,
         moved=8 << 20,
         limit=58,
-    )(counts, cols, tiles, node_grad, weight)
-    start = quarter_of(rep_index, row_index) * 256
+    )(chunks, counts, cols, tiles, node_grad, weight)
+    start = ((rep_index - row_index) & 3) * 256
     quarter = lax.dynamic_slice_in_dim(features, start, 256, axis=0)
     quarter = lax.ppermute(quarter, REP + ROW, PAIRS)
     terms = exchange(terms, "c")
@@ -243,11 +245,11 @@
         lambda *refs: forward_kernel(scaling, *refs),
         "forward",
         shape(16, 80, 128),
-        [VMEM] * 3,
+        [SMEM] + [VMEM] * 3,
         [pltpu.VMEM((1024, 128), F32)],
         flops=2 * 128 * 1024 * 2304,
         moved=3 << 20,
-    )(dense, held, node_grad)
+    )(chunks, dense, held, node_grad)
     message = jnp.concatenate([message, column_sum.reshape(16, 16, 128)], axis=1)
     parts = exchange(message, REP)
 

time: 122 us -> 125 us (1.025)
  starting transfers between devices: 25 us -> 21.1 us
  blocking collectives: 65.5 us -> 69.1 us
  waiting for transfers between devices: 18 us -> 19.4 us
  local copies, waits for them, and re-layouts: 0.87 us -> 2.14 us
    ppermute x1, starting transfers between devices: 6.38 us -> 2.05 us  [body(): column_sum = lax.ppermute(column_sum, REP + ROW, [(d, s) for s, d in PAIRS])]
    all_to_all x5, blocking collectives: 65.5 us -> 69.1 us  [exchange(): return lax.all_to_all(block, axes, 0, 0)]
    ppermute x1, waiting for transfers between devices: 1.03 us -> 2.43 us  [body(): column_sum = lax.ppermute(column_sum, REP + ROW, [(d, s) for s, d in PAIRS])]
  transfers between devices with their start and end apart: 3 -> 3, of which waited for: 2 -> 2; matrix products, arithmetic and copies ran while one was open for 0% -> 1% of each run, Pallas kernels for 6% -> 6%
where the time goes in v8:
time: 125 us; the launch traced here: 123 us
  blocking collectives  69.1 us (55%)
  starting transfers between devices  21.1 us (17%)
  waiting for transfers between devices  19.4 us (16%)
  Pallas kernels  10.4 us (8%)
  local copies, waits for them, and re-layouts  2.14 us (2%)
    all_to_all x5, blocking collectives, exchange(): return lax.all_to_all(block, axes, 0, 0)  69.1 us
    all_to_all x1, waiting for transfers between devices, exchange(): return lax.all_to_all(block, axes, 0, 0)  17 us
    ppermute x1, starting transfers between devices, body(): quarter = lax.ppermute(quarter, REP + ROW, PAIRS)  14.9 us
    pallas_call x1, Pallas kernels, body(): call(backward_kernel, 'backward', shape(2, 4, 256, 128), [SMEM, SMEM, SME...  4.54 us
    all_to_all x1, starting transfers between devices, exchange(): return lax.all_to_all(block, axes, 0, 0)  4.13 us
  transfers between devices with their start and end apart: 3, of which 2 were waited for; matrix products, arithmetic and copies ran while one was open for 1% of the time, Pallas kernels for 6%

profile of v8, /device:TPU:24, one launch (start us, length us, event | category | flops | bytes accessed | tf_op | source)
XLA Modules:
  0.0 122.9 jit_solution(9988899657856580494)
XLA Ops:
  0.6 0.0 copy-start
  0.6 0.0 copy-start.6
  0.7 0.0 copy-start.1
  0.7 0.9 copy-done
  1.6 14.9 %collective-permute-start = (bf16[256,128]{1,0:T(8,128)(2,1)S(1)}, bf16[256,128]{1,0:T(8,128)(2,1)S(1)}, u32[]{:S(2)}, u32[]{:S(2)}) collective-permute-start(bf16[256,128]{1,0:T(8,128)(2,1)S(1)} %constant_dynamic-slice_fusion), channel_id=1, source_target_pairs={{464,0},{496,1},{400,2},{432,3},{128,4},{160,5},{192,6},{224,7},{8... | collective-permute-start | bytes 196616 | tf_op jit(solution)/shard_map/ppermute | solution.py:230
  16.5 1.2 dynamic-slice_bitcast_fusion.chunks.refs_0_
  17.7 4.5 %backward.1 = bf16[2,4,256,128]{3,2,1,0:T(8,128)(2,1)} custom-call(s32[8]{0:T(128)} %dynamic-slice_bitcast_fusion.chunks.refs_0_, s32[8]{0:T(128)} %bitcast.8, s32[96]{0:T(128)} %bitcast.10, bf16[96,128,128]{2,1,0:T(8,128)(2,1)} %bitcast.6, bf16[1024,256]{1,0:T(8,128)(2,1)} %refs_3_.1, bf16[128,256]{1,0:T(8,128)(2,1)} %weight.1), custom_call_target="tpu_custom_call" | custom-call | flops 603979776 | bytes 8388608 | tf_op jit(solution)/shard_map/backward/pallas_call | solution.py:211
  22.2 5.2 %all_to_all.30.terms = bf16[2,4,256,128]{3,2,1,0:T(8,128)(2,1)S(1)} all-to-all(bf16[2,4,256,128]{3,2,1,0:T(8,128)(2,1)} %backward.1), channel_id=1, replica_groups=mesh['zl'=4,'x'=4,'zh'=4,'y'=4,'c'=2] {'c'}, dimensions={0} | all-to-all | bytes 1048576 | tf_op jit(solution)/shard_map/all_to_all | solution.py:200
  27.5 0.1 pack.1
  27.5 12.0 %all_to_all.31.received = bf16[4,512,128]{2,1,0:T(8,128)(2,1)S(1)} all-to-all(bf16[4,512,128]{2,1,0:T(8,128)(2,1)S(1)} %pack.1), channel_id=1, replica_groups=mesh['zl'=4,'x'=4,'zh'=4,'y'=4,'c'=2] {'y'}, dimensions={0} | all-to-all | bytes 1048576 | tf_op jit(solution)/shard_map/all_to_all | solution.py:200
  39.6 0.1 split.1
  39.6 0.0 copy-start.2
  39.7 2.1 %collective-permute-start.1 = (bf16[256,128]{1,0:T(8,128)(2,1)S(1)}, bf16[256,128]{1,0:T(8,128)(2,1)S(1)}, u32[]{:S(2)}, u32[]{:S(2)}) collective-permute-start(bf16[256,128]{1,0:T(8,128)(2,1)S(1)} %get-tuple-element.12), channel_id=1, source_target_pairs={{0,464},{1,496},{2,400},{3,432},{4,128},{5,160},{6,192},{7,224},{8... | collective-permute-start | bytes 196616 | tf_op jit(solution)/shard_map/ppermute | solution.py:238
  41.7 1.0 dense.1.refs_1_
  42.7 4.2 %all_to_all.32.refs_2_ = bf16[2,4,256,128]{3,2,1,0:T(8,128)(2,1)S(1)} all-to-all(bf16[2,4,256,128]{3,2,1,0:T(8,128)(2,1)S(1)} %get-tuple-element.11), channel_id=1, replica_groups=mesh['zl'=4,'x'=4,'zh'=4,'y'=4,'c'=2] {'c'}, dimensions={0} | all-to-all | bytes 1048576 | tf_op jit(solution)/shard_map/all_to_all | solution.py:200
  46.9 2.0 %forward.1 = bf16[16,80,128]{2,1,0:T(8,128)(2,1)S(1)} custom-call(s32[8]{0:T(128)S(1)} %copy-done.4, bf16[1024,2048]{1,0:T(8,128)(2,1)S(1)} %dense.1.refs_1_, bf16[2,4,256,128]{3,2,1,0:T(8,128)(2,1)S(1)} %all_to_all.32.refs_2_, bf16[1024,256]{1,0:T(8,128)(2,1)S(1)} %copy-done.2), custom_call_target="tpu_custom_call" | custom-call | flops 603979776 | bytes 3145728 | tf_op jit(solution)/shard_map/forward/pallas_call | solution.py:244
  48.9 2.4 %collective-permute-done.1 = bf16[256,128]{1,0:T(8,128)(2,1)S(1)} collective-permute-done((bf16[256,128]{1,0:T(8,128)(2,1)S(1)}, bf16[256,128]{1,0:T(8,128)(2,1)S(1)}, u32[]{:S(2)}, u32[]{:S(2)}) %collective-permute-start.1) | collective-permute-done | bytes 65568 | tf_op jit(solution)/shard_map/ppermute | solution.py:238
  51.4 22.6 %all_to_all.33.parts = bf16[16,96,128]{2,1,0:T(8,128)(2,1)S(1)} all-to-all(bf16[16,96,128]{2,1,0:T(8,128)(2,1)S(1)} %pad_maximum_fusion), channel_id=1, replica_groups=mesh['zl'=4,'x'=4,'zh'=4,'y'=4,'c'=2] {'zl','x'}, dimensions={0} | all-to-all | bytes 786432 | tf_op jit(solution)/shard_map/all_to_all | solution.py:200
  74.0 0.1 reduce.1
  74.1 25.1 %all_to_all.34.weight_parts = bf16[32,16,128]{2,1,0:T(8,128)(2,1)S(1)} all-to-all(bf16[32,16,128]{2,1,0:T(8,128)(2,1)S(1)} %get-tuple-element.14), channel_id=1, replica_groups=mesh['zl'=4,'x'=4,'zh'=4,'y'=4,'c'=2] {'zh','y','c'}, dimensions={0} | all-to-all | bytes 262144 | tf_op jit(solution)/shard_map/all_to_all | solution.py:200
  99.2 0.9 gather.1
  100.1 4.1 %all-to-all-start.5 = ((bf16[16,144,128]{2,1,0:T(8,128)(2,1)}), bf16[16,144,128]{2,1,0:T(8,128)(2,1)S(1)}, u32[]{:S(2)}, u32[]{:S(2)}) async-start(bf16[16,144,128]{2,1,0:T(8,128)(2,1)} %gather.1), calls=%async_computation.5 | async-start | bytes 1179648 | tf_op jit(solution)/shard_map/all_to_all | solution.py:200
  104.2 17.0 %all-to-all-done.5.received = bf16[16,144,128]{2,1,0:T(8,128)(2,1)S(1)} async-done(((bf16[16,144,128]{2,1,0:T(8,128)(2,1)}), bf16[16,144,128]{2,1,0:T(8,128)(2,1)S(1)}, u32[]{:S(2)}, u32[]{:S(2)}) %all-to-all-start.5) | async-done | bytes 589856 | tf_op jit(solution)/shard_map/all_to_all | solution.py:200
  121.2 1.7 %output.1 = (bf16[1024,256]{1,0:T(8,128)(2,1)}, f32[128,256]{1,0:T(8,128)}, bf16[1024,128]{1,0:T(8,128)(2,1)}) custom-call(s32[4]{0:T(128)S(1)} %subtract_and_fusion.order, bf16[16,144,128]{2,1,0:T(8,128)(2,1)S(1)} %all-to-all-done.5.received, bf16[128,256]{1,0:T(8,128)(2,1)S(1)} %copy-done.3), custom_call_target="tpu_custom_call" | custom-call | bytes 1048576 | tf_op jit(solution)/shard_map/output/pallas_call | solution.py:262
  (13 shorter events, 0.1 us)
Async XLA Ops:
  0.6 1.0 copy-start
  0.6 41.1 %copy-start.6 = (s32[1,1,96]{2,1,0:T(1,128)S(1)}, s32[1,1,96]{2,1,0:T(1,128)}, u32[]{:S(2)}) copy-start(s32[1,1,96]{2,1,0:T(1,128)} %param.10) | copy-start | bytes 1156
  0.7 41.1 %copy-start.5 = (s32[1,1,8]{2,1,0:T(1,128)S(1)}, s32[1,1,8]{2,1,0:T(1,128)}, u32[]{:S(2)}) copy-start(s32[1,1,8]{2,1,0:T(1,128)} %param.9) | copy-start | bytes 100
  0.7 41.1 %copy-start.1 = (bf16[1,1,96,128,128]{4,3,2,1,0:T(8,128)(2,1)S(1)}, bf16[1,1,96,128,128]{4,3,2,1,0:T(8,128)(2,1)}, u32[]{:S(2)}) copy-start(bf16[1,1,96,128,128]{4,3,2,1,0:T(8,128)(2,1)} %param.8) | copy-start | bytes 9437188
  1.6 25.9 %collective-permute-start = (bf16[256,128]{1,0:T(8,128)(2,1)S(1)}, bf16[256,128]{1,0:T(8,128)(2,1)S(1)}, u32[]{:S(2)}, u32[]{:S(2)}) collective-permute-start(bf16[256,128]{1,0:T(8,128)(2,1)S(1)} %constant_dynamic-slice_fusion), channel_id=1, source_target_pairs={{464,0},{496,1},{400,2},{432,3},{128,4},{160,5},{192,6},{224,7},{8... | collective-permute-start | bytes 196616 | tf_op jit(solution)/shard_map/ppermute | solution.py:230
  39.6 7.2 %copy-start.2 = (bf16[1024,256]{1,0:T(8,128)(2,1)S(1)}, bf16[1024,256]{1,0:T(8,128)(2,1)}, u32[]{:S(2)}) copy-start(bf16[1024,256]{1,0:T(8,128)(2,1)} %refs_3_.1) | copy-start | bytes 1572868
  39.6 7.2 %copy-start.4 = (s32[8]{0:T(128)S(1)}, s32[8]{0:T(128)}, u32[]{:S(2)}) copy-start(s32[8]{0:T(128)} %dynamic-slice_bitcast_fusion.chunks.refs_0_) | copy-start | bytes 100
  39.7 11.7 %collective-permute-start.1 = (bf16[256,128]{1,0:T(8,128)(2,1)S(1)}, bf16[256,128]{1,0:T(8,128)(2,1)S(1)}, u32[]{:S(2)}, u32[]{:S(2)}) collective-permute-start(bf16[256,128]{1,0:T(8,128)(2,1)S(1)} %get-tuple-element.12), channel_id=1, source_target_pairs={{0,464},{1,496},{2,400},{3,432},{4,128},{5,160},{6,192},{7,224},{8... | collective-permute-start | bytes 196616 | tf_op jit(solution)/shard_map/ppermute | solution.py:238
  46.9 74.3 %copy-start.3 = (bf16[128,256]{1,0:T(8,128)(2,1)S(1)}, bf16[128,256]{1,0:T(8,128)(2,1)}, u32[]{:S(2)}) copy-start(bf16[128,256]{1,0:T(8,128)(2,1)} %weight.1) | copy-start | bytes 196612
  100.1 21.1 %all-to-all-start.5 = ((bf16[16,144,128]{2,1,0:T(8,128)(2,1)}), bf16[16,144,128]{2,1,0:T(8,128)(2,1)S(1)}, u32[]{:S(2)}, u32[]{:S(2)}) async-start(bf16[16,144,128]{2,1,0:T(8,128)(2,1)} %gather.1), calls=%async_computation.5 | async-start | bytes 1179648 | tf_op jit(solution)/shard_map/all_to_all | solution.py:200

commit v9 on v7

--- a/solution.py
+++ b/solution.py
@@ -10,6 +10,7 @@
 
 REP = ("zl", "x")
 ROW = ("zh", "y", "c")
+YC = ("y", "c")
 F32 = jnp.float32
 BF16 = jnp.bfloat16
 VMEM = pl.BlockSpec(memory_space=pltpu.VMEM)
@@ -156,14 +157,19 @@
     total = parts[0, 64:80, :].astype(F32)
     for a in range(1, 16):
         total = total + parts[a, 64:80, :].astype(F32)
-    weight_part[...] = jnp.broadcast_to(total.astype(BF16)[None], (32, 16, 128))
+    weight_part[...] = jnp.broadcast_to(total.astype(BF16)[None], (8, 16, 128))
+
+
+def weight_kernel(parts, total):
+    partial = parts[0].astype(F32)
+    for k in range(1, 8):
+        partial = partial + parts[k].astype(F32)
+    total[...] = jnp.broadcast_to(partial[None], (4, 16, 128))
 
 
 def gather_kernel(piece, weight_parts, message):
     message[:, 0:128, :] = jnp.broadcast_to(piece[...][None], (16, 128, 128))
-    total = weight_parts[0].astype(F32)
-    for r in range(1, 32):
-        total = total + weight_parts[r].astype(F32)
+    total = (weight_parts[0] + weight_parts[1]) + (weight_parts[2] + weight_parts[3])
     message[:, 128:144, :] = jnp.broadcast_to(total.astype(BF16)[None], (16, 16, 128))
 
 
@@ -252,9 +258,12 @@
     parts = exchange(message, REP)
 
     piece, weight_part = call(
-        reduce_kernel, "reduce", (shape(128, 128), shape(32, 16, 128)), [VMEM]
+        reduce_kernel, "reduce", (shape(128, 128), shape(8, 16, 128)), [VMEM]
     )(parts)
-    weight_parts = exchange(weight_part, ROW)
+    weight_part = call(weight_kernel, "weight", shape(4, 16, 128, dtype=F32), [VMEM])(
+        exchange(weight_part, YC)
+    )
+    weight_parts = exchange(weight_part, "zh")
     message = call(gather_kernel, "gather", shape(16, 144, 128), [VMEM] * 2)(piece, weight_parts)
     received = exchange(message, REP)
     return call(

time: 122 us -> 124 us (1.016)
  blocking collectives: 65.5 us -> 69 us
  waiting for transfers between devices: 18 us -> 16.3 us
    all_to_all x5 -> x6, blocking collectives: 65.5 us -> 69 us  [exchange(): return lax.all_to_all(block, axes, 0, 0)]
    all_to_all x1, waiting for transfers between devices: 17 us -> 15.3 us  [exchange(): return lax.all_to_all(block, axes, 0, 0)]
where the time goes in v9:
time: 124 us; the launch traced here: 122 us
  blocking collectives  69 us (56%)
  starting transfers between devices  24.8 us (20%)
  waiting for transfers between devices  16.3 us (13%)
  Pallas kernels  10.3 us (8%)
    all_to_all x6, blocking collectives, exchange(): return lax.all_to_all(block, axes, 0, 0)  69 us
    all_to_all x1, waiting for transfers between devices, exchange(): return lax.all_to_all(block, axes, 0, 0)  15.3 us
    ppermute x1, starting transfers between devices, body(): quarter = lax.ppermute(quarter, REP + ROW, PAIRS)  14.5 us
    ppermute x1, starting transfers between devices, body(): column_sum = lax.ppermute(column_sum, REP + ROW, [(d, s) for s, d in PAIRS])  6.19 us
    pallas_call x1, Pallas kernels, body(): call(backward_kernel, 'backward', shape(2, 4, 256, 128), [SMEM, SMEM, HBM...  4.75 us
    all_to_all x1, starting transfers between devices, exchange(): return lax.all_to_all(block, axes, 0, 0)  4.04 us
  transfers between devices with their start and end apart: 3, of which 2 were waited for; matrix products, arithmetic and copies ran while one was open for 0% of the time, Pallas kernels for 6%

profile of v9, /device:TPU:24, one launch (start us, length us, event | category | flops | bytes accessed | tf_op | source)
XLA Modules:
  0.0 122.1 jit_solution(15631653319075030867)
XLA Ops:
  0.6 0.0 copy-start
  0.6 0.0 copy-start.5
  0.7 0.0 copy-start.4
  0.7 0.0 copy-start.1
  0.8 0.8 copy-done
  1.6 14.5 %collective-permute-start = (bf16[256,128]{1,0:T(8,128)(2,1)S(1)}, bf16[256,128]{1,0:T(8,128)(2,1)S(1)}, u32[]{:S(2)}, u32[]{:S(2)}) collective-permute-start(bf16[256,128]{1,0:T(8,128)(2,1)S(1)} %constant_dynamic-slice_fusion), channel_id=1, source_target_pairs={{192,0},{224,1},{128,2},{160,3},{400,4},{432,5},{464,6},{496,7},{3... | collective-permute-start | bytes 196616 | tf_op jit(solution)/shard_map/ppermute | solution.py:234
  16.1 4.7 %backward.1 = bf16[2,4,256,128]{3,2,1,0:T(8,128)(2,1)} custom-call(s32[8]{0:T(128)} %bitcast.6, s32[96]{0:T(128)} %bitcast.8, bf16[96,128,128]{2,1,0:T(8,128)(2,1)} %bitcast.4, bf16[1024,256]{1,0:T(8,128)(2,1)} %refs_2_.1, bf16[128,256]{1,0:T(8,128)(2,1)} %weight.3), custom_call_target="tpu_custom_call" | custom-call | flops 603979776 | bytes 8388608 | tf_op jit(solution)/shard_map/backward/pallas_call | solution.py:215
  20.9 5.2 %all_to_all.35.terms = bf16[2,4,256,128]{3,2,1,0:T(8,128)(2,1)S(1)} all-to-all(bf16[2,4,256,128]{3,2,1,0:T(8,128)(2,1)} %backward.1), channel_id=1, replica_groups=mesh['zl'=4,'x'=4,'zh'=4,'y'=4,'c'=2] {'c'}, dimensions={0} | all-to-all | bytes 1048576 | tf_op jit(solution)/shard_map/all_to_all | solution.py:205
  26.1 0.1 pack.1
  26.2 12.0 %all_to_all.36.received = bf16[4,512,128]{2,1,0:T(8,128)(2,1)S(1)} all-to-all(bf16[4,512,128]{2,1,0:T(8,128)(2,1)S(1)} %pack.1), channel_id=1, replica_groups=mesh['zl'=4,'x'=4,'zh'=4,'y'=4,'c'=2] {'y'}, dimensions={0} | all-to-all | bytes 1048576 | tf_op jit(solution)/shard_map/all_to_all | solution.py:205
  38.2 0.1 split.1
  38.3 6.2 %collective-permute-start.1 = (bf16[256,128]{1,0:T(8,128)(2,1)S(1)}, bf16[256,128]{1,0:T(8,128)(2,1)S(1)}, u32[]{:S(2)}, u32[]{:S(2)}) collective-permute-start(bf16[256,128]{1,0:T(8,128)(2,1)S(1)} %get-tuple-element.12), channel_id=1, source_target_pairs={{0,192},{1,224},{2,128},{3,160},{4,400},{5,432},{6,464},{7,496},{8... | collective-permute-start | bytes 196616 | tf_op jit(solution)/shard_map/ppermute | solution.py:242
  44.5 1.2 dense.1.refs_0_
  45.8 4.2 %all_to_all.37.refs_1_ = bf16[2,4,256,128]{3,2,1,0:T(8,128)(2,1)S(1)} all-to-all(bf16[2,4,256,128]{3,2,1,0:T(8,128)(2,1)S(1)} %get-tuple-element.11), channel_id=1, replica_groups=mesh['zl'=4,'x'=4,'zh'=4,'y'=4,'c'=2] {'c'}, dimensions={0} | all-to-all | bytes 1048576 | tf_op jit(solution)/shard_map/all_to_all | solution.py:205
  49.9 1.5 %forward.1 = bf16[16,80,128]{2,1,0:T(8,128)(2,1)S(1)} custom-call(bf16[1024,2048]{1,0:T(8,128)(2,1)S(1)} %dense.1.refs_0_, bf16[2,4,256,128]{3,2,1,0:T(8,128)(2,1)S(1)} %all_to_all.37.refs_1_, bf16[1024,256]{1,0:T(8,128)(2,1)S(1)} %copy-done.2), custom_call_target="tpu_custom_call" | custom-call | flops 603979776 | bytes 3145728 | tf_op jit(solution)/shard_map/forward/pallas_call | solution.py:248
  51.4 1.1 collective-permute-done.1
  52.5 20.8 %all_to_all.38.parts = bf16[16,96,128]{2,1,0:T(8,128)(2,1)S(1)} all-to-all(bf16[16,96,128]{2,1,0:T(8,128)(2,1)S(1)} %pad_maximum_fusion), channel_id=1, replica_groups=mesh['zl'=4,'x'=4,'zh'=4,'y'=4,'c'=2] {'zl','x'}, dimensions={0} | all-to-all | bytes 786432 | tf_op jit(solution)/shard_map/all_to_all | solution.py:205
  73.3 0.1 reduce.1
  73.4 7.7 %all_to_all.39.parts = bf16[8,16,128]{2,1,0:T(8,128)(2,1)S(1)} all-to-all(bf16[8,16,128]{2,1,0:T(8,128)(2,1)S(1)} %get-tuple-element.14), channel_id=1, replica_groups=mesh['zl'=4,'x'=4,'zh'=4,'y'=4,'c'=2] {'y','c'}, dimensions={0} | all-to-all | bytes 65536 | tf_op jit(solution)/shard_map/all_to_all | solution.py:205
  81.1 19.1 %all_to_all.40.weight_parts = f32[4,16,128]{2,1,0:T(8,128)S(1)} all-to-all(f32[4,16,128]{2,1,0:T(8,128)S(1)} %weight.2), channel_id=1, replica_groups=mesh['zl'=4,'x'=4,'zh'=4,'y'=4,'c'=2] {'zh'}, dimensions={0} | all-to-all | bytes 65536 | tf_op jit(solution)/shard_map/all_to_all | solution.py:205
  100.2 0.9 gather.1
  101.1 4.0 %all-to-all-start.6 = ((bf16[16,144,128]{2,1,0:T(8,128)(2,1)}), bf16[16,144,128]{2,1,0:T(8,128)(2,1)S(1)}, u32[]{:S(2)}, u32[]{:S(2)}) async-start(bf16[16,144,128]{2,1,0:T(8,128)(2,1)} %gather.1), calls=%async_computation.6 | async-start | bytes 1179648 | tf_op jit(solution)/shard_map/all_to_all | solution.py:205
  105.1 15.3 %all-to-all-done.6.received = bf16[16,144,128]{2,1,0:T(8,128)(2,1)S(1)} async-done(((bf16[16,144,128]{2,1,0:T(8,128)(2,1)}), bf16[16,144,128]{2,1,0:T(8,128)(2,1)S(1)}, u32[]{:S(2)}, u32[]{:S(2)}) %all-to-all-start.6) | async-done | bytes 589856 | tf_op jit(solution)/shard_map/all_to_all | solution.py:205
  120.4 1.7 %output.1 = (bf16[1024,256]{1,0:T(8,128)(2,1)}, f32[128,256]{1,0:T(8,128)}, bf16[1024,128]{1,0:T(8,128)(2,1)}) custom-call(s32[4]{0:T(128)S(1)} %fusion.order, bf16[16,144,128]{2,1,0:T(8,128)(2,1)S(1)} %all-to-all-done.6.received, bf16[128,256]{1,0:T(8,128)(2,1)S(1)} %copy-done.3), custom_call_target="tpu_custom_call" | custom-call | bytes 1048576 | tf_op jit(solution)/shard_map/output/pallas_call | solution.py:269
  (12 shorter events, 0.1 us)
Async XLA Ops:
  0.6 1.0 copy-start
  0.6 43.9 %copy-start.5 = (s32[1,1,96]{2,1,0:T(1,128)S(1)}, s32[1,1,96]{2,1,0:T(1,128)}, u32[]{:S(2)}) copy-start(s32[1,1,96]{2,1,0:T(1,128)} %param.9) | copy-start | bytes 1156
  0.7 43.9 %copy-start.4 = (s32[1,1,8]{2,1,0:T(1,128)S(1)}, s32[1,1,8]{2,1,0:T(1,128)}, u32[]{:S(2)}) copy-start(s32[1,1,8]{2,1,0:T(1,128)} %param.8) | copy-start | bytes 100
  0.7 43.9 %copy-start.1 = (bf16[1,1,96,128,128]{4,3,2,1,0:T(8,128)(2,1)S(1)}, bf16[1,1,96,128,128]{4,3,2,1,0:T(8,128)(2,1)}, u32[]{:S(2)}) copy-start(bf16[1,1,96,128,128]{4,3,2,1,0:T(8,128)(2,1)} %param.7) | copy-start | bytes 9437188
  1.6 24.5 %collective-permute-start = (bf16[256,128]{1,0:T(8,128)(2,1)S(1)}, bf16[256,128]{1,0:T(8,128)(2,1)S(1)}, u32[]{:S(2)}, u32[]{:S(2)}) collective-permute-start(bf16[256,128]{1,0:T(8,128)(2,1)S(1)} %constant_dynamic-slice_fusion), channel_id=1, source_target_pairs={{192,0},{224,1},{128,2},{160,3},{400,4},{432,5},{464,6},{496,7},{3... | collective-permute-start | bytes 196616 | tf_op jit(solution)/shard_map/ppermute | solution.py:234
  38.3 11.6 %copy-start.2 = (bf16[1024,256]{1,0:T(8,128)(2,1)S(1)}, bf16[1024,256]{1,0:T(8,128)(2,1)}, u32[]{:S(2)}) copy-start(bf16[1024,256]{1,0:T(8,128)(2,1)} %refs_2_.1) | copy-start | bytes 1572868
  38.3 14.2 %collective-permute-start.1 = (bf16[256,128]{1,0:T(8,128)(2,1)S(1)}, bf16[256,128]{1,0:T(8,128)(2,1)S(1)}, u32[]{:S(2)}, u32[]{:S(2)}) collective-permute-start(bf16[256,128]{1,0:T(8,128)(2,1)S(1)} %get-tuple-element.12), channel_id=1, source_target_pairs={{0,192},{1,224},{2,128},{3,160},{4,400},{5,432},{6,464},{7,496},{8... | collective-permute-start | bytes 196616 | tf_op jit(solution)/shard_map/ppermute | solution.py:242
  49.9 70.5 %copy-start.3 = (bf16[128,256]{1,0:T(8,128)(2,1)S(1)}, bf16[128,256]{1,0:T(8,128)(2,1)}, u32[]{:S(2)}) copy-start(bf16[128,256]{1,0:T(8,128)(2,1)} %weight.3) | copy-start | bytes 196612
  101.1 19.3 %all-to-all-start.6 = ((bf16[16,144,128]{2,1,0:T(8,128)(2,1)}), bf16[16,144,128]{2,1,0:T(8,128)(2,1)S(1)}, u32[]{:S(2)}, u32[]{:S(2)}) async-start(bf16[16,144,128]{2,1,0:T(8,128)(2,1)} %gather.1), calls=%async_computation.6 | async-start | bytes 1179648 | tf_op jit(solution)/shard_map/all_to_all | solution.py:205

commit v10 on v7

--- a/solution.py
+++ b/solution.py
@@ -37,6 +37,11 @@
     return jnp.where(turn < 2, far, 1 - far) * 2 + turn % 2
 
 
+def back_pair(q, zh, k):
+    return q * 32 + zh * 8 + k, (k % 4 * 4 + zh) * 32 + q + k // 4 * 16
+
+
+BACK = [back_pair(q, zh, k) for q in range(16) for zh in range(4) for k in range(8)]
 PAIRS = [pair(q, zh, k) for q in range(16) for zh in range(4) for k in range(8)]
 
 
@@ -144,42 +149,41 @@
 
 
 def reduce_kernel(parts, piece, weight_part):
-    total = parts[0, 0:64, :].astype(F32)
+    total = parts[0].astype(F32)
     for a in range(1, 16):
-        total = total + parts[a, 0:64, :].astype(F32)
-    piece[0:64, :] = total.astype(BF16)
-    for part in range(4):
-        total = parts[part, 80:96, :].astype(F32)
-        for zl in range(1, 4):
-            total = total + parts[zl * 4 + part, 80:96, :].astype(F32)
-        piece[64 + part * 16 : 80 + part * 16, :] = total.astype(BF16)
-    total = parts[0, 64:80, :].astype(F32)
-    for a in range(1, 16):
-        total = total + parts[a, 64:80, :].astype(F32)
-    weight_part[...] = jnp.broadcast_to(total.astype(BF16)[None], (32, 16, 128))
-
-
-def gather_kernel(piece, weight_parts, message):
-    message[:, 0:128, :] = jnp.broadcast_to(piece[...][None], (16, 128, 128))
+        total = total + parts[a].astype(F32)
+    piece[...] = total[0:64].astype(BF16)
+    weight_part[...] = jnp.broadcast_to(total[64:80].astype(BF16)[None], (32, 16, 128))
+
+
+def slice_kernel(place, column, *slices):
+    for k in range(4):
+        row = pl.multiple_of(((place[0] + k) & 3) * 64, 64)
+        slices[k][...] = column[pl.ds(row, 64), :]
+
+
+def gather_kernel(piece, own, first, second, third, weight_parts, message):
+    message[:, 0:64, :] = jnp.broadcast_to(piece[...][None], (16, 64, 128))
+    column = (own[...].astype(F32) + first[...].astype(F32)) + (
+        second[...].astype(F32) + third[...].astype(F32)
+    )
+    message[:, 64:128, :] = jnp.broadcast_to(column.astype(BF16)[None], (16, 64, 128))
     total = weight_parts[0].astype(F32)
     for r in range(1, 32):
         total = total + weight_parts[r].astype(F32)
     message[:, 128:144, :] = jnp.broadcast_to(total.astype(BF16)[None], (16, 16, 128))
 
 
-def output_kernel(order, received, weight, output, weight_grad, feature_grad):
+def output_kernel(received, weight, output, weight_grad, feature_grad):
     parts = received[:, 128:144, :].astype(F32)
     weight_grad[:, 0:128] = parts[:, 0:8, :].reshape(128, 128)
     weight_grad[:, 128:256] = parts[:, 8:16, :].reshape(128, 128)
-    for zq in range(4):
-        aggregate = received[zq * 4 : zq * 4 + 4, 0:64, :].reshape(256, 128)
-        output[zq * 256 : (zq + 1) * 256, :] = jnp.dot(
+    feature_grad[...] = received[:, 64:128, :].reshape(1024, 128)
+    for quarter in range(4):
+        aggregate = received[quarter * 4 : quarter * 4 + 4, 0:64, :].reshape(256, 128)
+        output[quarter * 256 : (quarter + 1) * 256, :] = jnp.dot(
             aggregate, weight[...], preferred_element_type=F32
         ).astype(BF16)
-        row = pl.multiple_of(order[zq] * 256, 256)
-        feature_grad[pl.ds(row, 256), :] = received[
-            :, 64 + zq * 16 : 80 + zq * 16, :
-        ].reshape(256, 128)
 
 
 def call(kernel, name, outs, ins, scratch=(), flops=0, moved=1 << 20, limit=16):
@@ -204,7 +208,7 @@
     row_index = lax.axis_index(ROW)
     scaling = 1.0 / math.sqrt(features.shape[0] * 32)
     counts, cols, tiles = tile_counts[0, 0], tile_columns[0, 0], tile_values[0, 0]
-    order = quarter_of(jnp.arange(4, dtype=jnp.int32), row_index).astype(jnp.int32)
+    place = lax.axis_index("x").astype(jnp.int32).reshape(1)
 
     terms = call(
         backward_kernel,
@@ -233,7 +237,8 @@
     held, column_sum = call(
         split_kernel, "split", (shape(2, 4, 256, 128), shape(256, 128)), [VMEM]
     )(received)
-    column_sum = lax.ppermute(column_sum, REP + ROW, [(d, s) for s, d in PAIRS])
+    column_sum = lax.ppermute(column_sum, REP + ROW, BACK)
+    counts, held = lax.optimization_barrier((counts, held))
     dense = call(dense_kernel, "dense", shape(1024, 2048), [SMEM, SMEM, VMEM])(
         counts, cols, tiles
     )
@@ -248,21 +253,30 @@
         flops=2 * 128 * 1024 * 2304,
         moved=3 << 20,
     )(dense, held, node_grad)
-    message = jnp.concatenate([message, column_sum.reshape(16, 16, 128)], axis=1)
     parts = exchange(message, REP)
+    parts, column_sum = lax.optimization_barrier((parts, column_sum))
 
     piece, weight_part = call(
-        reduce_kernel, "reduce", (shape(128, 128), shape(32, 16, 128)), [VMEM]
+        reduce_kernel, "reduce", (shape(64, 128), shape(32, 16, 128)), [VMEM]
     )(parts)
     weight_parts = exchange(weight_part, ROW)
-    message = call(gather_kernel, "gather", shape(16, 144, 128), [VMEM] * 2)(piece, weight_parts)
+    own, *others = call(slice_kernel, "slice", (shape(64, 128),) * 4, [SMEM, VMEM])(
+        place, column_sum
+    )
+    others = [
+        lax.ppermute(block, "x", [(i, (i + k + 1) % 4) for i in range(4)])
+        for k, block in enumerate(others)
+    ]
+    message = call(gather_kernel, "gather", shape(16, 144, 128), [VMEM] * 6)(
+        piece, own, *others, weight_parts
+    )
     received = exchange(message, REP)
     return call(
         output_kernel,
         "output",
         (shape(1024, 256), shape(128, 256, dtype=F32), shape(1024, 128)),
-        [SMEM, VMEM, VMEM],
-    )(order, received, weight)
+        [VMEM] * 2,
+    )(received, weight)
 
 
 def solution(mesh):

time: 122 us -> 122 us (level)
  starting transfers between devices: 25 us -> 50.4 us
  blocking collectives: 65.5 us -> 44.4 us
  waiting for transfers between devices: 18 us -> 13.3 us
    all_to_all x5 -> x4, blocking collectives: 65.5 us -> 44.4 us  [exchange(): return lax.all_to_all(block, axes, 0, 0)]
    all_to_all x1 -> x2, starting transfers between devices: 4.13 us -> 19.6 us  [exchange(): return lax.all_to_all(block, axes, 0, 0)]
    all_to_all x1 -> x2, waiting for transfers between devices: 17 us -> 4.49 us  [exchange(): return lax.all_to_all(block, axes, 0, 0)]
    ppermute x1 -> x4, starting transfers between devices: 6.38 us -> 16.2 us  [the longest x3 10.2 us: body(): lax.ppermute(block, 'x', [(i, (i + k + 1) % 4) for i in range(4)])]
    ppermute x1 -> x4, waiting for transfers between devices: 1.03 us -> 8.85 us  [the longest x1 5.16 us: body(): column_sum = lax.ppermute(column_sum, REP + ROW, BACK)]
  transfers between devices with their start and end apart: 3 -> 7, of which waited for: 2 -> 4; matrix products, arithmetic and copies ran while one was open for 0% -> 0% of each run, Pallas kernels for 6% -> 4%
where the time goes in v10:
time: 122 us; the launch traced here: 120 us
  starting transfers between devices  50.4 us (41%)
  blocking collectives  44.4 us (36%)
  waiting for transfers between devices  13.3 us (11%)
  Pallas kernels  10.5 us (9%)
    all_to_all x4, blocking collectives, exchange(): return lax.all_to_all(block, axes, 0, 0)  44.4 us
    all_to_all x2, starting transfers between devices, exchange(): return lax.all_to_all(block, axes, 0, 0)  19.6 us
    ppermute x1, starting transfers between devices, body(): quarter = lax.ppermute(quarter, REP + ROW, PAIRS)  14.5 us
    ppermute x3, starting transfers between devices, body(): lax.ppermute(block, 'x', [(i, (i + k + 1) % 4) for i in range(4)])  10.2 us
    ppermute x1, starting transfers between devices, body(): column_sum = lax.ppermute(column_sum, REP + ROW, BACK)  6 us
    ppermute x1, waiting for transfers between devices, body(): column_sum = lax.ppermute(column_sum, REP + ROW, BACK)  5.16 us
    pallas_call x1, Pallas kernels, body(): call(backward_kernel, 'backward', shape(2, 4, 256, 128), [SMEM, SMEM, HBM...  4.89 us
    all_to_all x2, waiting for transfers between devices, exchange(): return lax.all_to_all(block, axes, 0, 0)  4.49 us
  transfers between devices with their start and end apart: 7, of which 4 were waited for; matrix products, arithmetic and copies ran while one was open for 0% of the time, Pallas kernels for 4%

profile of v10, /device:TPU:24, one launch (start us, length us, event | category | flops | bytes accessed | tf_op | source)
XLA Modules:
  0.0 120.5 jit_solution(4536380892360623760)
XLA Ops:
  0.8 0.8 copy-done
  1.6 14.5 %collective-permute-start = (bf16[256,128]{1,0:T(8,128)(2,1)S(1)}, bf16[256,128]{1,0:T(8,128)(2,1)S(1)}, u32[]{:S(2)}, u32[]{:S(2)}) collective-permute-start(bf16[256,128]{1,0:T(8,128)(2,1)S(1)} %constant_dynamic-slice_fusion), channel_id=1, source_target_pairs={{192,0},{224,1},{128,2},{160,3},{400,4},{432,5},{464,6},{496,7},{3... | collective-permute-start | bytes 196616 | tf_op jit(solution)/shard_map/ppermute | solution.py:232
  16.1 4.9 %backward.1 = bf16[2,4,256,128]{3,2,1,0:T(8,128)(2,1)} custom-call(s32[8]{0:T(128)} %bitcast.6, s32[96]{0:T(128)} %bitcast.8, bf16[96,128,128]{2,1,0:T(8,128)(2,1)} %bitcast.4, bf16[1024,256]{1,0:T(8,128)(2,1)} %refs_2_.1, bf16[128,256]{1,0:T(8,128)(2,1)} %weight.1), custom_call_target="tpu_custom_call" | custom-call | flops 603979776 | bytes 8388608 | tf_op jit(solution)/shard_map/backward/pallas_call | solution.py:213
  21.0 5.2 %all_to_all.30.terms = bf16[2,4,256,128]{3,2,1,0:T(8,128)(2,1)S(1)} all-to-all(bf16[2,4,256,128]{3,2,1,0:T(8,128)(2,1)} %backward.1), channel_id=1, replica_groups=mesh['zl'=4,'x'=4,'zh'=4,'y'=4,'c'=2] {'c'}, dimensions={0} | all-to-all | bytes 1048576 | tf_op jit(solution)/shard_map/all_to_all | solution.py:203
  26.3 0.1 pack.1
  26.3 12.0 %all_to_all.31.received = bf16[4,512,128]{2,1,0:T(8,128)(2,1)S(1)} all-to-all(bf16[4,512,128]{2,1,0:T(8,128)(2,1)S(1)} %pack.1), channel_id=1, replica_groups=mesh['zl'=4,'x'=4,'zh'=4,'y'=4,'c'=2] {'y'}, dimensions={0} | all-to-all | bytes 1048576 | tf_op jit(solution)/shard_map/all_to_all | solution.py:203
  38.4 0.1 split.1
  38.5 1.3 %dense.1.refs_0_ = bf16[1024,2048]{1,0:T(8,128)(2,1)S(1)} custom-call(s32[8]{0:T(128)S(1)} %bitcast.7, s32[96]{0:T(128)S(1)} %bitcast.9, bf16[96,128,128]{2,1,0:T(8,128)(2,1)S(1)} %bitcast.5), custom_call_target="tpu_custom_call" | custom-call | bytes 1048576 | tf_op jit(solution)/shard_map/dense/pallas_call | solution.py:242
  39.8 4.2 %all_to_all.32.refs_1_ = bf16[2,4,256,128]{3,2,1,0:T(8,128)(2,1)S(1)} all-to-all(bf16[2,4,256,128]{3,2,1,0:T(8,128)(2,1)S(1)} %get-tuple-element.21), channel_id=1, replica_groups=mesh['zl'=4,'x'=4,'zh'=4,'y'=4,'c'=2] {'c'}, dimensions={0} | all-to-all | bytes 1048576 | tf_op jit(solution)/shard_map/all_to_all | solution.py:203
  44.0 2.2 %forward.1 = bf16[16,80,128]{2,1,0:T(8,128)(2,1)} custom-call(bf16[1024,2048]{1,0:T(8,128)(2,1)S(1)} %dense.1.refs_0_, bf16[2,4,256,128]{3,2,1,0:T(8,128)(2,1)S(1)} %all_to_all.32.refs_1_, bf16[1024,256]{1,0:T(8,128)(2,1)S(1)} %copy-done.2), custom_call_target="tpu_custom_call" | custom-call | flops 603979776 | bytes 3145728 | tf_op jit(solution)/shard_map/forward/pallas_call | solution.py:247
  46.2 6.7 %all-to-all-start.3 = ((bf16[16,80,128]{2,1,0:T(8,128)(2,1)}), bf16[16,80,128]{2,1,0:T(8,128)(2,1)S(1)}, u32[]{:S(2)}, u32[]{:S(2)}) async-start(bf16[16,80,128]{2,1,0:T(8,128)(2,1)} %forward.1), calls=%async_computation.3 | async-start | bytes 655360 | tf_op jit(solution)/shard_map/all_to_all | solution.py:203
  53.0 6.0 %collective-permute-start.1 = (bf16[256,128]{1,0:T(8,128)(2,1)S(1)}, bf16[256,128]{1,0:T(8,128)(2,1)S(1)}, u32[]{:S(2)}, u32[]{:S(2)}) collective-permute-start(bf16[256,128]{1,0:T(8,128)(2,1)S(1)} %get-tuple-element.22), channel_id=1, source_target_pairs={{0,0},{1,128},{2,256},{3,384},{4,16},{5,144},{6,272},{7,400},{8,32... | collective-permute-start | bytes 196616 | tf_op jit(solution)/shard_map/ppermute | solution.py:240
  59.0 5.2 %collective-permute-done.1.column = bf16[256,128]{1,0:T(8,128)(2,1)S(1)} collective-permute-done((bf16[256,128]{1,0:T(8,128)(2,1)S(1)}, bf16[256,128]{1,0:T(8,128)(2,1)S(1)}, u32[]{:S(2)}, u32[]{:S(2)}) %collective-permute-start.1) | collective-permute-done | bytes 65568 | tf_op jit(solution)/shard_map/ppermute | solution.py:240
  64.1 2.7 %all-to-all-done.3.parts = bf16[16,80,128]{2,1,0:T(8,128)(2,1)S(1)} async-done(((bf16[16,80,128]{2,1,0:T(8,128)(2,1)}), bf16[16,80,128]{2,1,0:T(8,128)(2,1)S(1)}, u32[]{:S(2)}, u32[]{:S(2)}) %all-to-all-start.3) | async-done | bytes 327712 | tf_op jit(solution)/shard_map/all_to_all | solution.py:203
  66.9 0.7 reduce.1
  67.5 12.9 %all-to-all-start.4 = ((bf16[32,16,128]{2,1,0:T(8,128)(2,1)}), bf16[32,16,128]{2,1,0:T(8,128)(2,1)S(1)}, u32[]{:S(2)}, u32[]{:S(2)}) async-start(bf16[32,16,128]{2,1,0:T(8,128)(2,1)} %get-tuple-element.30), calls=%async_computation.4 | async-start | bytes 262144 | tf_op jit(solution)/shard_map/all_to_all | solution.py:203
  80.5 2.0 %collective-permute-start.2 = (bf16[64,128]{1,0:T(8,128)(2,1)S(1)}, bf16[64,128]{1,0:T(8,128)(2,1)S(1)}, u32[]{:S(2)}, u32[]{:S(2)}) collective-permute-start(bf16[64,128]{1,0:T(8,128)(2,1)S(1)} %get-tuple-element.27), channel_id=1, source_target_pairs={{0,32},{32,64},{64,96},{96,0},{1,33},{33,65},{65,97},{97,1},{2,34}... | collective-permute-start | bytes 49160 | tf_op jit(solution)/shard_map/ppermute | solution.py:267
  82.5 6.3 %collective-permute-start.3 = (bf16[64,128]{1,0:T(8,128)(2,1)S(1)}, bf16[64,128]{1,0:T(8,128)(2,1)S(1)}, u32[]{:S(2)}, u32[]{:S(2)}) collective-permute-start(bf16[64,128]{1,0:T(8,128)(2,1)S(1)} %get-tuple-element.28), channel_id=1, source_target_pairs={{0,64},{32,96},{64,0},{96,32},{1,65},{33,97},{65,1},{97,33},{2,66}... | collective-permute-start | bytes 49160 | tf_op jit(solution)/shard_map/ppermute | solution.py:267
  88.8 1.9 %collective-permute-start.4 = (bf16[64,128]{1,0:T(8,128)(2,1)S(1)}, bf16[64,128]{1,0:T(8,128)(2,1)S(1)}, u32[]{:S(2)}, u32[]{:S(2)}) collective-permute-start(bf16[64,128]{1,0:T(8,128)(2,1)S(1)} %get-tuple-element.29), channel_id=1, source_target_pairs={{0,96},{32,0},{64,32},{96,64},{1,97},{33,1},{65,33},{97,65},{2,98}... | collective-permute-start | bytes 49160 | tf_op jit(solution)/shard_map/ppermute | solution.py:267
  90.8 3.7 %collective-permute-done.4.third = bf16[64,128]{1,0:T(8,128)(2,1)S(1)} collective-permute-done((bf16[64,128]{1,0:T(8,128)(2,1)S(1)}, bf16[64,128]{1,0:T(8,128)(2,1)S(1)}, u32[]{:S(2)}, u32[]{:S(2)}) %collective-permute-start.4) | collective-permute-done | bytes 16416 | tf_op jit(solution)/shard_map/ppermute | solution.py:267
  94.4 1.8 %all-to-all-done.4.weight_parts = bf16[32,16,128]{2,1,0:T(8,128)(2,1)S(1)} async-done(((bf16[32,16,128]{2,1,0:T(8,128)(2,1)}), bf16[32,16,128]{2,1,0:T(8,128)(2,1)S(1)}, u32[]{:S(2)}, u32[]{:S(2)}) %all-to-all-start.4) | async-done | bytes 131104 | tf_op jit(solution)/shard_map/all_to_all | solution.py:203
  96.2 0.1 gather.1
  96.3 23.0 %all_to_all.33.received = bf16[16,144,128]{2,1,0:T(8,128)(2,1)S(1)} all-to-all(bf16[16,144,128]{2,1,0:T(8,128)(2,1)S(1)} %gather.1), channel_id=1, replica_groups=mesh['zl'=4,'x'=4,'zh'=4,'y'=4,'c'=2] {'zl','x'}, dimensions={0} | all-to-all | bytes 1179648 | tf_op jit(solution)/shard_map/all_to_all | solution.py:203
  119.3 1.1 output.1
  (16 shorter events, 0.1 us)
Async XLA Ops:
  0.6 1.0 copy-start
  0.6 37.8 %copy-start.5 = (s32[1,1,96]{2,1,0:T(1,128)S(1)}, s32[1,1,96]{2,1,0:T(1,128)}, u32[]{:S(2)}) copy-start(s32[1,1,96]{2,1,0:T(1,128)} %param.9) | copy-start | bytes 1156
  0.7 37.8 %copy-start.4 = (s32[1,1,8]{2,1,0:T(1,128)S(1)}, s32[1,1,8]{2,1,0:T(1,128)}, u32[]{:S(2)}) copy-start(s32[1,1,8]{2,1,0:T(1,128)} %param.8) | copy-start | bytes 100
  0.7 37.8 %copy-start.1 = (bf16[1,1,96,128,128]{4,3,2,1,0:T(8,128)(2,1)S(1)}, bf16[1,1,96,128,128]{4,3,2,1,0:T(8,128)(2,1)}, u32[]{:S(2)}) copy-start(bf16[1,1,96,128,128]{4,3,2,1,0:T(8,128)(2,1)} %param.7) | copy-start | bytes 9437188
  1.6 24.7 %collective-permute-start = (bf16[256,128]{1,0:T(8,128)(2,1)S(1)}, bf16[256,128]{1,0:T(8,128)(2,1)S(1)}, u32[]{:S(2)}, u32[]{:S(2)}) collective-permute-start(bf16[256,128]{1,0:T(8,128)(2,1)S(1)} %constant_dynamic-slice_fusion), channel_id=1, source_target_pairs={{192,0},{224,1},{128,2},{160,3},{400,4},{432,5},{464,6},{496,7},{3... | collective-permute-start | bytes 196616 | tf_op jit(solution)/shard_map/ppermute | solution.py:232
  38.5 5.5 %copy-start.2 = (bf16[1024,256]{1,0:T(8,128)(2,1)S(1)}, bf16[1024,256]{1,0:T(8,128)(2,1)}, u32[]{:S(2)}) copy-start(bf16[1024,256]{1,0:T(8,128)(2,1)} %refs_2_.1) | copy-start | bytes 1572868
  44.0 75.3 %copy-start.3 = (bf16[128,256]{1,0:T(8,128)(2,1)S(1)}, bf16[128,256]{1,0:T(8,128)(2,1)}, u32[]{:S(2)}) copy-start(bf16[128,256]{1,0:T(8,128)(2,1)} %weight.1) | copy-start | bytes 196612
  46.2 20.6 %all-to-all-start.3 = ((bf16[16,80,128]{2,1,0:T(8,128)(2,1)}), bf16[16,80,128]{2,1,0:T(8,128)(2,1)S(1)}, u32[]{:S(2)}, u32[]{:S(2)}) async-start(bf16[16,80,128]{2,1,0:T(8,128)(2,1)} %forward.1), calls=%async_computation.3 | async-start | bytes 655360 | tf_op jit(solution)/shard_map/all_to_all | solution.py:203
  53.0 11.2 %collective-permute-start.1 = (bf16[256,128]{1,0:T(8,128)(2,1)S(1)}, bf16[256,128]{1,0:T(8,128)(2,1)S(1)}, u32[]{:S(2)}, u32[]{:S(2)}) collective-permute-start(bf16[256,128]{1,0:T(8,128)(2,1)S(1)} %get-tuple-element.22), channel_id=1, source_target_pairs={{0,0},{1,128},{2,256},{3,384},{4,16},{5,144},{6,272},{7,400},{8,32... | collective-permute-start | bytes 196616 | tf_op jit(solution)/shard_map/ppermute | solution.py:240
  67.5 28.7 %all-to-all-start.4 = ((bf16[32,16,128]{2,1,0:T(8,128)(2,1)}), bf16[32,16,128]{2,1,0:T(8,128)(2,1)S(1)}, u32[]{:S(2)}, u32[]{:S(2)}) async-start(bf16[32,16,128]{2,1,0:T(8,128)(2,1)} %get-tuple-element.30), calls=%async_computation.4 | async-start | bytes 262144 | tf_op jit(solution)/shard_map/all_to_all | solution.py:203
  80.5 10.3 %collective-permute-start.2 = (bf16[64,128]{1,0:T(8,128)(2,1)S(1)}, bf16[64,128]{1,0:T(8,128)(2,1)S(1)}, u32[]{:S(2)}, u32[]{:S(2)}) collective-permute-start(bf16[64,128]{1,0:T(8,128)(2,1)S(1)} %get-tuple-element.27), channel_id=1, source_target_pairs={{0,32},{32,64},{64,96},{96,0},{1,33},{33,65},{65,97},{97,1},{2,34}... | collective-permute-start | bytes 49160 | tf_op jit(solution)/shard_map/ppermute | solution.py:267
  82.5 8.2 %collective-permute-start.3 = (bf16[64,128]{1,0:T(8,128)(2,1)S(1)}, bf16[64,128]{1,0:T(8,128)(2,1)S(1)}, u32[]{:S(2)}, u32[]{:S(2)}) collective-permute-start(bf16[64,128]{1,0:T(8,128)(2,1)S(1)} %get-tuple-element.28), channel_id=1, source_target_pairs={{0,64},{32,96},{64,0},{96,32},{1,65},{33,97},{65,1},{97,33},{2,66}... | collective-permute-start | bytes 49160 | tf_op jit(solution)/shard_map/ppermute | solution.py:267
  88.8 5.6 %collective-permute-start.4 = (bf16[64,128]{1,0:T(8,128)(2,1)S(1)}, bf16[64,128]{1,0:T(8,128)(2,1)S(1)}, u32[]{:S(2)}, u32[]{:S(2)}) collective-permute-start(bf16[64,128]{1,0:T(8,128)(2,1)S(1)} %get-tuple-element.29), channel_id=1, source_target_pairs={{0,96},{32,0},{64,32},{96,64},{1,97},{33,1},{65,33},{97,65},{2,98}... | collective-permute-start | bytes 49160 | tf_op jit(solution)/shard_map/ppermute | solution.py:267

commit v11 on v10

--- a/solution.py
+++ b/solution.py
@@ -38,7 +38,18 @@
 
 
 def back_pair(q, zh, k):
-    return q * 32 + zh * 8 + k, (k % 4 * 4 + zh) * 32 + q + k // 4 * 16
+    half, u = k // 4, k % 2
+    if k // 2 % 2 != farther(q, half):
+        u += 2
+    zl = u if q // 8 else 3 - u
+    x = (q + (2, 1, 0, 3)[(zh - half * 2 - q // 8) % 4]) % 4
+    return q * 32 + zh * 8 + k, (zl * 4 + x) * 32 + q + half * 16
+
+
+def back_quarter(zl, s):
+    u = jnp.where(s % 16 // 8 == 0, 3 - zl, zl)
+    far = farther(s % 16, s // 16)
+    return jnp.where(u < 2, far, 1 - far) * 2 + u % 2
 
 
 BACK = [back_pair(q, zh, k) for q in range(16) for zh in range(4) for k in range(8)]
@@ -174,12 +185,15 @@
     message[:, 128:144, :] = jnp.broadcast_to(total.astype(BF16)[None], (16, 16, 128))
 
 
-def output_kernel(received, weight, output, weight_grad, feature_grad):
+def output_kernel(order, received, weight, output, weight_grad, feature_grad):
     parts = received[:, 128:144, :].astype(F32)
     weight_grad[:, 0:128] = parts[:, 0:8, :].reshape(128, 128)
     weight_grad[:, 128:256] = parts[:, 8:16, :].reshape(128, 128)
-    feature_grad[...] = received[:, 64:128, :].reshape(1024, 128)
     for quarter in range(4):
+        row = pl.multiple_of(order[quarter] * 256, 256)
+        feature_grad[pl.ds(row, 256), :] = received[
+            quarter * 4 : quarter * 4 + 4, 64:128, :
+        ].reshape(256, 128)
         aggregate = received[quarter * 4 : quarter * 4 + 4, 0:64, :].reshape(256, 128)
         output[quarter * 256 : (quarter + 1) * 256, :] = jnp.dot(
             aggregate, weight[...], preferred_element_type=F32
@@ -208,6 +222,7 @@
     row_index = lax.axis_index(ROW)
     scaling = 1.0 / math.sqrt(features.shape[0] * 32)
     counts, cols, tiles = tile_counts[0, 0], tile_columns[0, 0], tile_values[0, 0]
+    order = back_quarter(jnp.arange(4, dtype=jnp.int32), row_index).astype(jnp.int32)
     place = lax.axis_index("x").astype(jnp.int32).reshape(1)
 
     terms = call(
@@ -275,8 +290,8 @@
         output_kernel,
         "output",
         (shape(1024, 256), shape(128, 256, dtype=F32), shape(1024, 128)),
-        [VMEM] * 2,
-    )(received, weight)
+        [SMEM, VMEM, VMEM],
+    )(order, received, weight)
 
 
 def solution(mesh):

time: 122 us -> 123 us (level)
  the two profiles are of different devices: /device:TPU:24 before, /device:TPU:1 now
where the time goes in v11:
time: 123 us
  starting transfers between devices  55.6 us (45%)
  waiting for transfers between devices  29 us (24%)
  blocking collectives  25.1 us (20%)
  Pallas kernels  11.1 us (9%)
    all_to_all x3, starting transfers between devices, exchange(): return lax.all_to_all(block, axes, 0, 0)  25.9 us
    all_to_all x3, blocking collectives, exchange(): return lax.all_to_all(block, axes, 0, 0)  25.1 us
    all_to_all x3, waiting for transfers between devices, exchange(): return lax.all_to_all(block, axes, 0, 0)  23.3 us
    ppermute x1, starting transfers between devices, body(): quarter = lax.ppermute(quarter, REP + ROW, PAIRS)  14.3 us
    ppermute x3, starting transfers between devices, body(): lax.ppermute(block, 'x', [(i, (i + k + 1) % 4) for i in range(4)])  9.73 us
    ppermute x1, starting transfers between devices, body(): column_sum = lax.ppermute(column_sum, REP + ROW, BACK)  5.59 us
    pallas_call x1, Pallas kernels, body(): call(backward_kernel, 'backward', shape(2, 4, 256, 128), [SMEM, SMEM, HBM...  4.49 us
    ppermute x1, waiting for transfers between devices, body(): column_sum = lax.ppermute(column_sum, REP + ROW, BACK)  4.42 us
  transfers between devices with their start and end apart: 8, of which 5 were waited for; matrix products, arithmetic and copies ran while one was open for 0% of the time, Pallas kernels for 4%

profile of v11, /device:TPU:1, one launch (start us, length us, event | category | flops | bytes accessed | tf_op | source)
XLA Modules:
  0.0 122.6 jit_solution(1413142482214782654)
XLA Ops:
  0.8 0.8 copy-done
  1.6 14.3 %collective-permute-start = (bf16[256,128]{1,0:T(8,128)(2,1)S(1)}, bf16[256,128]{1,0:T(8,128)(2,1)S(1)}, u32[]{:S(2)}, u32[]{:S(2)}) collective-permute-start(bf16[256,128]{1,0:T(8,128)(2,1)S(1)} %constant_dynamic-slice_fusion), channel_id=1, source_target_pairs={{192,0},{224,1},{128,2},{160,3},{400,4},{432,5},{464,6},{496,7},{3... | collective-permute-start | bytes 196616 | tf_op jit(solution)/shard_map/ppermute | solution.py:247
  15.9 4.5 %backward.1 = bf16[2,4,256,128]{3,2,1,0:T(8,128)(2,1)} custom-call(s32[8]{0:T(128)} %bitcast.6, s32[96]{0:T(128)} %bitcast.8, bf16[96,128,128]{2,1,0:T(8,128)(2,1)} %bitcast.4, bf16[1024,256]{1,0:T(8,128)(2,1)} %refs_2_.1, bf16[128,256]{1,0:T(8,128)(2,1)} %weight.1), custom_call_target="tpu_custom_call" | custom-call | flops 603979776 | bytes 8388608 | tf_op jit(solution)/shard_map/backward/pallas_call | solution.py:228
  20.4 6.4 %all_to_all.30.terms = bf16[2,4,256,128]{3,2,1,0:T(8,128)(2,1)S(1)} all-to-all(bf16[2,4,256,128]{3,2,1,0:T(8,128)(2,1)} %backward.1), channel_id=1, replica_groups=mesh['zl'=4,'x'=4,'zh'=4,'y'=4,'c'=2] {'c'}, dimensions={0} | all-to-all | bytes 1048576 | tf_op jit(solution)/shard_map/all_to_all | solution.py:217
  26.9 12.6 %all_to_all.31.received = bf16[4,512,128]{2,1,0:T(8,128)(2,1)S(1)} all-to-all(bf16[4,512,128]{2,1,0:T(8,128)(2,1)S(1)} %pack.1), channel_id=1, replica_groups=mesh['zl'=4,'x'=4,'zh'=4,'y'=4,'c'=2] {'y'}, dimensions={0} | all-to-all | bytes 1048576 | tf_op jit(solution)/shard_map/all_to_all | solution.py:217
  39.5 0.1 split.1
  39.6 1.0 dense.1.refs_0_
  40.6 6.1 %all_to_all.32.refs_1_ = bf16[2,4,256,128]{3,2,1,0:T(8,128)(2,1)S(1)} all-to-all(bf16[2,4,256,128]{3,2,1,0:T(8,128)(2,1)S(1)} %get-tuple-element.21), channel_id=1, replica_groups=mesh['zl'=4,'x'=4,'zh'=4,'y'=4,'c'=2] {'c'}, dimensions={0} | all-to-all | bytes 1048576 | tf_op jit(solution)/shard_map/all_to_all | solution.py:217
  46.7 2.2 %forward.1 = bf16[16,80,128]{2,1,0:T(8,128)(2,1)} custom-call(bf16[1024,2048]{1,0:T(8,128)(2,1)S(1)} %dense.1.refs_0_, bf16[2,4,256,128]{3,2,1,0:T(8,128)(2,1)S(1)} %all_to_all.32.refs_1_, bf16[1024,256]{1,0:T(8,128)(2,1)S(1)} %copy-done.2), custom_call_target="tpu_custom_call" | custom-call | flops 603979776 | bytes 3145728 | tf_op jit(solution)/shard_map/forward/pallas_call | solution.py:262
  48.9 6.3 %all-to-all-start.3 = ((bf16[16,80,128]{2,1,0:T(8,128)(2,1)}), bf16[16,80,128]{2,1,0:T(8,128)(2,1)S(1)}, u32[]{:S(2)}, u32[]{:S(2)}) async-start(bf16[16,80,128]{2,1,0:T(8,128)(2,1)} %forward.1), calls=%async_computation.3 | async-start | bytes 655360 | tf_op jit(solution)/shard_map/all_to_all | solution.py:217
  55.3 5.6 %collective-permute-start.1 = (bf16[256,128]{1,0:T(8,128)(2,1)S(1)}, bf16[256,128]{1,0:T(8,128)(2,1)S(1)}, u32[]{:S(2)}, u32[]{:S(2)}) collective-permute-start(bf16[256,128]{1,0:T(8,128)(2,1)S(1)} %get-tuple-element.22), channel_id=1, source_target_pairs={{0,192},{1,64},{2,448},{3,320},{4,400},{5,272},{6,144},{7,16},{8,1... | collective-permute-start | bytes 196616 | tf_op jit(solution)/shard_map/ppermute | solution.py:255
  60.8 4.4 %collective-permute-done.1.column = bf16[256,128]{1,0:T(8,128)(2,1)S(1)} collective-permute-done((bf16[256,128]{1,0:T(8,128)(2,1)S(1)}, bf16[256,128]{1,0:T(8,128)(2,1)S(1)}, u32[]{:S(2)}, u32[]{:S(2)}) %collective-permute-start.1) | collective-permute-done | bytes 65568 | tf_op jit(solution)/shard_map/ppermute | solution.py:255
  65.3 0.9 all-to-all-done.3.parts
  66.2 0.7 reduce.1
  66.9 12.9 %all-to-all-start.4 = ((bf16[32,16,128]{2,1,0:T(8,128)(2,1)}), bf16[32,16,128]{2,1,0:T(8,128)(2,1)S(1)}, u32[]{:S(2)}, u32[]{:S(2)}) async-start(bf16[32,16,128]{2,1,0:T(8,128)(2,1)} %get-tuple-element.30), calls=%async_computation.4 | async-start | bytes 262144 | tf_op jit(solution)/shard_map/all_to_all | solution.py:217
  79.8 1.9 %collective-permute-start.2 = (bf16[64,128]{1,0:T(8,128)(2,1)S(1)}, bf16[64,128]{1,0:T(8,128)(2,1)S(1)}, u32[]{:S(2)}, u32[]{:S(2)}) collective-permute-start(bf16[64,128]{1,0:T(8,128)(2,1)S(1)} %get-tuple-element.27), channel_id=1, source_target_pairs={{0,32},{32,64},{64,96},{96,0},{1,33},{33,65},{65,97},{97,1},{2,34}... | collective-permute-start | bytes 49160 | tf_op jit(solution)/shard_map/ppermute | solution.py:282
  81.8 4.3 %collective-permute-start.3 = (bf16[64,128]{1,0:T(8,128)(2,1)S(1)}, bf16[64,128]{1,0:T(8,128)(2,1)S(1)}, u32[]{:S(2)}, u32[]{:S(2)}) collective-permute-start(bf16[64,128]{1,0:T(8,128)(2,1)S(1)} %get-tuple-element.28), channel_id=1, source_target_pairs={{0,64},{32,96},{64,0},{96,32},{1,65},{33,97},{65,1},{97,33},{2,66}... | collective-permute-start | bytes 49160 | tf_op jit(solution)/shard_map/ppermute | solution.py:282
  86.1 3.5 %collective-permute-start.4 = (bf16[64,128]{1,0:T(8,128)(2,1)S(1)}, bf16[64,128]{1,0:T(8,128)(2,1)S(1)}, u32[]{:S(2)}, u32[]{:S(2)}) collective-permute-start(bf16[64,128]{1,0:T(8,128)(2,1)S(1)} %get-tuple-element.29), channel_id=1, source_target_pairs={{0,96},{32,0},{64,32},{96,64},{1,97},{33,1},{65,33},{97,65},{2,98}... | collective-permute-start | bytes 49160 | tf_op jit(solution)/shard_map/ppermute | solution.py:282
  89.6 1.3 %collective-permute-done.4.third = bf16[64,128]{1,0:T(8,128)(2,1)S(1)} collective-permute-done((bf16[64,128]{1,0:T(8,128)(2,1)S(1)}, bf16[64,128]{1,0:T(8,128)(2,1)S(1)}, u32[]{:S(2)}, u32[]{:S(2)}) %collective-permute-start.4) | collective-permute-done | bytes 16416 | tf_op jit(solution)/shard_map/ppermute | solution.py:282
  90.9 6.2 %all-to-all-done.4.weight_parts = bf16[32,16,128]{2,1,0:T(8,128)(2,1)S(1)} async-done(((bf16[32,16,128]{2,1,0:T(8,128)(2,1)}), bf16[32,16,128]{2,1,0:T(8,128)(2,1)S(1)}, u32[]{:S(2)}, u32[]{:S(2)}) %all-to-all-start.4) | async-done | bytes 131104 | tf_op jit(solution)/shard_map/all_to_all | solution.py:217
  97.1 0.9 gather.1
  98.0 6.7 %all-to-all-start.5 = ((bf16[16,144,128]{2,1,0:T(8,128)(2,1)}), bf16[16,144,128]{2,1,0:T(8,128)(2,1)S(1)}, u32[]{:S(2)}, u32[]{:S(2)}) async-start(bf16[16,144,128]{2,1,0:T(8,128)(2,1)} %gather.1), calls=%async_computation.5 | async-start | bytes 1179648 | tf_op jit(solution)/shard_map/all_to_all | solution.py:217
  104.8 16.1 %all-to-all-done.5.received = bf16[16,144,128]{2,1,0:T(8,128)(2,1)S(1)} async-done(((bf16[16,144,128]{2,1,0:T(8,128)(2,1)}), bf16[16,144,128]{2,1,0:T(8,128)(2,1)S(1)}, u32[]{:S(2)}, u32[]{:S(2)}) %all-to-all-start.5) | async-done | bytes 589856 | tf_op jit(solution)/shard_map/all_to_all | solution.py:217
  120.9 1.7 %output.1 = (bf16[1024,256]{1,0:T(8,128)(2,1)}, f32[128,256]{1,0:T(8,128)}, bf16[1024,128]{1,0:T(8,128)(2,1)}) custom-call(s32[4]{0:T(128)S(1)} %fusion.order, bf16[16,144,128]{2,1,0:T(8,128)(2,1)S(1)} %all-to-all-done.5.received, bf16[128,256]{1,0:T(8,128)(2,1)S(1)} %copy-done.3), custom_call_target="tpu_custom_call" | custom-call | bytes 1048576 | tf_op jit(solution)/shard_map/output/pallas_call | solution.py:289
  (18 shorter events, 0.2 us)
Async XLA Ops:
  0.6 1.0 copy-start
  0.6 38.9 %copy-start.5 = (s32[1,1,96]{2,1,0:T(1,128)S(1)}, s32[1,1,96]{2,1,0:T(1,128)}, u32[]{:S(2)}) copy-start(s32[1,1,96]{2,1,0:T(1,128)} %param.9) | copy-start | bytes 1156
  0.7 38.9 %copy-start.4 = (s32[1,1,8]{2,1,0:T(1,128)S(1)}, s32[1,1,8]{2,1,0:T(1,128)}, u32[]{:S(2)}) copy-start(s32[1,1,8]{2,1,0:T(1,128)} %param.8) | copy-start | bytes 100
  0.7 38.9 %copy-start.1 = (bf16[1,1,96,128,128]{4,3,2,1,0:T(8,128)(2,1)S(1)}, bf16[1,1,96,128,128]{4,3,2,1,0:T(8,128)(2,1)}, u32[]{:S(2)}) copy-start(bf16[1,1,96,128,128]{4,3,2,1,0:T(8,128)(2,1)} %param.7) | copy-start | bytes 9437188
  1.6 25.2 %collective-permute-start = (bf16[256,128]{1,0:T(8,128)(2,1)S(1)}, bf16[256,128]{1,0:T(8,128)(2,1)S(1)}, u32[]{:S(2)}, u32[]{:S(2)}) collective-permute-start(bf16[256,128]{1,0:T(8,128)(2,1)S(1)} %constant_dynamic-slice_fusion), channel_id=1, source_target_pairs={{192,0},{224,1},{128,2},{160,3},{400,4},{432,5},{464,6},{496,7},{3... | collective-permute-start | bytes 196616 | tf_op jit(solution)/shard_map/ppermute | solution.py:247
  39.6 7.1 %copy-start.2 = (bf16[1024,256]{1,0:T(8,128)(2,1)S(1)}, bf16[1024,256]{1,0:T(8,128)(2,1)}, u32[]{:S(2)}) copy-start(bf16[1024,256]{1,0:T(8,128)(2,1)} %refs_2_.1) | copy-start | bytes 1572868
  46.7 74.2 %copy-start.3 = (bf16[128,256]{1,0:T(8,128)(2,1)S(1)}, bf16[128,256]{1,0:T(8,128)(2,1)}, u32[]{:S(2)}) copy-start(bf16[128,256]{1,0:T(8,128)(2,1)} %weight.1) | copy-start | bytes 196612
  48.9 17.3 %all-to-all-start.3 = ((bf16[16,80,128]{2,1,0:T(8,128)(2,1)}), bf16[16,80,128]{2,1,0:T(8,128)(2,1)S(1)}, u32[]{:S(2)}, u32[]{:S(2)}) async-start(bf16[16,80,128]{2,1,0:T(8,128)(2,1)} %forward.1), calls=%async_computation.3 | async-start | bytes 655360 | tf_op jit(solution)/shard_map/all_to_all | solution.py:217
  55.3 10.0 %collective-permute-start.1 = (bf16[256,128]{1,0:T(8,128)(2,1)S(1)}, bf16[256,128]{1,0:T(8,128)(2,1)S(1)}, u32[]{:S(2)}, u32[]{:S(2)}) collective-permute-start(bf16[256,128]{1,0:T(8,128)(2,1)S(1)} %get-tuple-element.22), channel_id=1, source_target_pairs={{0,192},{1,64},{2,448},{3,320},{4,400},{5,272},{6,144},{7,16},{8,1... | collective-permute-start | bytes 196616 | tf_op jit(solution)/shard_map/ppermute | solution.py:255
  66.9 30.2 %all-to-all-start.4 = ((bf16[32,16,128]{2,1,0:T(8,128)(2,1)}), bf16[32,16,128]{2,1,0:T(8,128)(2,1)S(1)}, u32[]{:S(2)}, u32[]{:S(2)}) async-start(bf16[32,16,128]{2,1,0:T(8,128)(2,1)} %get-tuple-element.30), calls=%async_computation.4 | async-start | bytes 262144 | tf_op jit(solution)/shard_map/all_to_all | solution.py:217
  79.8 9.8 %collective-permute-start.2 = (bf16[64,128]{1,0:T(8,128)(2,1)S(1)}, bf16[64,128]{1,0:T(8,128)(2,1)S(1)}, u32[]{:S(2)}, u32[]{:S(2)}) collective-permute-start(bf16[64,128]{1,0:T(8,128)(2,1)S(1)} %get-tuple-element.27), channel_id=1, source_target_pairs={{0,32},{32,64},{64,96},{96,0},{1,33},{33,65},{65,97},{97,1},{2,34}... | collective-permute-start | bytes 49160 | tf_op jit(solution)/shard_map/ppermute | solution.py:282
  81.8 7.8 %collective-permute-start.3 = (bf16[64,128]{1,0:T(8,128)(2,1)S(1)}, bf16[64,128]{1,0:T(8,128)(2,1)S(1)}, u32[]{:S(2)}, u32[]{:S(2)}) collective-permute-start(bf16[64,128]{1,0:T(8,128)(2,1)S(1)} %get-tuple-element.28), channel_id=1, source_target_pairs={{0,64},{32,96},{64,0},{96,32},{1,65},{33,97},{65,1},{97,33},{2,66}... | collective-permute-start | bytes 49160 | tf_op jit(solution)/shard_map/ppermute | solution.py:282
  86.1 4.8 %collective-permute-start.4 = (bf16[64,128]{1,0:T(8,128)(2,1)S(1)}, bf16[64,128]{1,0:T(8,128)(2,1)S(1)}, u32[]{:S(2)}, u32[]{:S(2)}) collective-permute-start(bf16[64,128]{1,0:T(8,128)(2,1)S(1)} %get-tuple-element.29), channel_id=1, source_target_pairs={{0,96},{32,0},{64,32},{96,64},{1,97},{33,1},{65,33},{97,65},{2,98}... | collective-permute-start | bytes 49160 | tf_op jit(solution)/shard_map/ppermute | solution.py:282
  98.0 22.9 %all-to-all-start.5 = ((bf16[16,144,128]{2,1,0:T(8,128)(2,1)}), bf16[16,144,128]{2,1,0:T(8,128)(2,1)S(1)}, u32[]{:S(2)}, u32[]{:S(2)}) async-start(bf16[16,144,128]{2,1,0:T(8,128)(2,1)} %gather.1), calls=%async_computation.5 | async-start | bytes 1179648 | tf_op jit(solution)/shard_map/all_to_all | solution.py:217

commit v12 on v7

--- a/solution.py
+++ b/solution.py
@@ -32,9 +32,9 @@
 
 
 def quarter_of(a, s):
-    turn = (a - s) % 4
-    far = farther(s % 16, s // 16)
-    return jnp.where(turn < 2, far, 1 - far) * 2 + turn % 2
+    turn = (a - s) & 3
+    far = farther(s & 15, s >> 4)
+    return (far ^ turn >> 1) * 2 + (turn & 1)
 
 
 PAIRS = [pair(q, zh, k) for q in range(16) for zh in range(4) for k in range(8)]
@@ -44,7 +44,7 @@
     return jax.ShapeDtypeStruct(dims, dtype)
 
 
-def fill(counts, cols, tiles, dense):
+def fill(counts, cols, tiles, dense, loads=()):
     def clear(b, carry):
         dense[pl.ds(pl.multiple_of(b * 128, 128), 128), :] = jnp.zeros((128, 2048), BF16)
         return carry
@@ -53,6 +53,8 @@
     yield
     start = jnp.int32(0)
     for b in range(8):
+        if loads:
+            loads[b].wait()
         count = counts[b]
 
         def place(i, carry, b=b, start=start):
@@ -86,15 +88,13 @@
     loads = tile_copies(tiles_hbm, tiles, sems)
     for copy in copies + loads:
         copy.start()
-    filling = fill(counts, cols, tiles, dense)
+    filling = fill(counts, cols, tiles, dense, loads)
     next(filling)
     copies[0].wait()
     copies[1].wait()
     grad_t[...] = lax.dot_general(
         weight[...], node_grad[...], (((1,), (1,)), ((), ())), preferred_element_type=F32
     ).astype(BF16)
-    for copy in loads:
-        copy.wait()
     next(filling)
     for k in range(8):
         term = jnp.dot(
@@ -143,7 +143,7 @@
     ).astype(BF16)
 
 
-def reduce_kernel(parts, piece, weight_part):
+def reduce_kernel(shard, parts, piece, weight_part):
     total = parts[0, 0:64, :].astype(F32)
     for a in range(1, 16):
         total = total + parts[a, 0:64, :].astype(F32)
@@ -152,7 +152,8 @@
         total = parts[part, 80:96, :].astype(F32)
         for zl in range(1, 4):
             total = total + parts[zl * 4 + part, 80:96, :].astype(F32)
-        piece[64 + part * 16 : 80 + part * 16, :] = total.astype(BF16)
+        row = pl.multiple_of(64 + quarter_of(part, shard[0]) * 16, 16)
+        piece[pl.ds(row, 16), :] = total.astype(BF16)
     total = parts[0, 64:80, :].astype(F32)
     for a in range(1, 16):
         total = total + parts[a, 64:80, :].astype(F32)
@@ -167,7 +168,7 @@
     message[:, 128:144, :] = jnp.broadcast_to(total.astype(BF16)[None], (16, 16, 128))
 
 
-def output_kernel(order, received, weight, output, weight_grad, feature_grad):
+def output_kernel(received, weight, output, weight_grad, feature_grad):
     parts = received[:, 128:144, :].astype(F32)
     weight_grad[:, 0:128] = parts[:, 0:8, :].reshape(128, 128)
     weight_grad[:, 128:256] = parts[:, 8:16, :].reshape(128, 128)
@@ -176,8 +177,7 @@
         output[zq * 256 : (zq + 1) * 256, :] = jnp.dot(
             aggregate, weight[...], preferred_element_type=F32
         ).astype(BF16)
-        row = pl.multiple_of(order[zq] * 256, 256)
-        feature_grad[pl.ds(row, 256), :] = received[
+        feature_grad[zq * 256 : (zq + 1) * 256, :] = received[
             :, 64 + zq * 16 : 80 + zq * 16, :
         ].reshape(256, 128)
 
@@ -204,7 +204,7 @@
     row_index = lax.axis_index(ROW)
     scaling = 1.0 / math.sqrt(features.shape[0] * 32)
     counts, cols, tiles = tile_counts[0, 0], tile_columns[0, 0], tile_values[0, 0]
-    order = quarter_of(jnp.arange(4, dtype=jnp.int32), row_index).astype(jnp.int32)
+    shard = row_index.astype(jnp.int32).reshape(1)
 
     terms = call(
         backward_kernel,
@@ -252,8 +252,8 @@
     parts = exchange(message, REP)
 
     piece, weight_part = call(
-        reduce_kernel, "reduce", (shape(128, 128), shape(32, 16, 128)), [VMEM]
-    )(parts)
+        reduce_kernel, "reduce", (shape(128, 128), shape(32, 16, 128)), [SMEM, VMEM]
+    )(shard, parts)
     weight_parts = exchange(weight_part, ROW)
     message = call(gather_kernel, "gather", shape(16, 144, 128), [VMEM] * 2)(piece, weight_parts)
     received = exchange(message, REP)
@@ -261,8 +261,8 @@
         output_kernel,
         "output",
         (shape(1024, 256), shape(128, 256, dtype=F32), shape(1024, 128)),
-        [SMEM, VMEM, VMEM],
-    )(order, received, weight)
+        [VMEM, VMEM],
+    )(received, weight)
 
 
 def solution(mesh):

time: 122 us -> 122 us (level)
  blocking collectives: 65.5 us -> 88.6 us
  waiting for transfers between devices: 18 us -> 0.95 us
  starting transfers between devices: 25 us -> 20.7 us
  Pallas kernels: 10.1 us -> 8.41 us
    all_to_all x5 -> x6, blocking collectives: 65.5 us -> 88.6 us  [exchange(): return lax.all_to_all(block, axes, 0, 0)]
    all_to_all x1 -> x0, waiting for transfers between devices: 17 us -> none  [exchange(): return lax.all_to_all(block, axes, 0, 0)]
    all_to_all x1 -> x0, starting transfers between devices: 4.13 us -> none  [exchange(): return lax.all_to_all(block, axes, 0, 0)]
  transfers between devices with their start and end apart: 3 -> 2, of which waited for: 2 -> 1; matrix products, arithmetic and copies ran while one was open for 0% -> 0% of each run, Pallas kernels for 6% -> 6%
where the time goes in v12:
time: 122 us; the launch traced here: 120 us
  blocking collectives  88.6 us (73%)
  starting transfers between devices  20.7 us (17%)
  Pallas kernels  8.41 us (7%)
    all_to_all x6, blocking collectives, exchange(): return lax.all_to_all(block, axes, 0, 0)  88.6 us
    ppermute x1, starting transfers between devices, body(): quarter = lax.ppermute(quarter, REP + ROW, PAIRS)  14.5 us
    ppermute x1, starting transfers between devices, body(): column_sum = lax.ppermute(column_sum, REP + ROW, [(d, s) for s, d in PAIRS])  6.15 us
    pallas_call x1, Pallas kernels, body(): call(backward_kernel, 'backward', shape(2, 4, 256, 128), [SMEM, SMEM, HBM...  4.42 us
  transfers between devices with their start and end apart: 2, of which 1 were waited for; matrix products, arithmetic and copies ran while one was open for 0% of the time, Pallas kernels for 6%

profile of v12, /device:TPU:24, one launch (start us, length us, event | category | flops | bytes accessed | tf_op | source)
XLA Modules:
  0.0 120.4 jit_solution(13315079234282258996)
XLA Ops:
  0.6 0.0 copy-start
  0.6 0.0 copy-start.5
  0.7 0.0 copy-start.4
  0.7 0.0 copy-start.1
  0.7 0.9 copy-done
  1.6 14.5 %collective-permute-start = (bf16[256,128]{1,0:T(8,128)(2,1)S(1)}, bf16[256,128]{1,0:T(8,128)(2,1)S(1)}, u32[]{:S(2)}, u32[]{:S(2)}) collective-permute-start(bf16[256,128]{1,0:T(8,128)(2,1)S(1)} %constant_dynamic-slice_fusion), channel_id=1, source_target_pairs={{192,0},{224,1},{128,2},{160,3},{400,4},{432,5},{464,6},{496,7},{3... | collective-permute-start | bytes 196616 | tf_op jit(solution)/shard_map/ppermute | solution.py:228
  16.1 4.4 %backward.1 = bf16[2,4,256,128]{3,2,1,0:T(8,128)(2,1)} custom-call(s32[8]{0:T(128)} %bitcast.7, s32[96]{0:T(128)} %bitcast.9, bf16[96,128,128]{2,1,0:T(8,128)(2,1)} %bitcast.5, bf16[1024,256]{1,0:T(8,128)(2,1)} %refs_2_.1, bf16[128,256]{1,0:T(8,128)(2,1)} %weight.1), custom_call_target="tpu_custom_call" | custom-call | flops 603979776 | bytes 8388608 | tf_op jit(solution)/shard_map/backward/pallas_call | solution.py:209
  20.6 5.2 %all_to_all.30.terms = bf16[2,4,256,128]{3,2,1,0:T(8,128)(2,1)S(1)} all-to-all(bf16[2,4,256,128]{3,2,1,0:T(8,128)(2,1)} %backward.1), channel_id=1, replica_groups=mesh['zl'=4,'x'=4,'zh'=4,'y'=4,'c'=2] {'c'}, dimensions={0} | all-to-all | bytes 1048576 | tf_op jit(solution)/shard_map/all_to_all | solution.py:199
  25.8 0.0 collective-permute-done.quarter
  25.8 0.1 pack.1
  25.9 12.0 %all_to_all.31.received = bf16[4,512,128]{2,1,0:T(8,128)(2,1)S(1)} all-to-all(bf16[4,512,128]{2,1,0:T(8,128)(2,1)S(1)} %pack.1), channel_id=1, replica_groups=mesh['zl'=4,'x'=4,'zh'=4,'y'=4,'c'=2] {'y'}, dimensions={0} | all-to-all | bytes 1048576 | tf_op jit(solution)/shard_map/all_to_all | solution.py:199
  37.9 0.1 split.1
  38.0 0.0 copy-start.2
  38.0 6.1 %collective-permute-start.1 = (bf16[256,128]{1,0:T(8,128)(2,1)S(1)}, bf16[256,128]{1,0:T(8,128)(2,1)S(1)}, u32[]{:S(2)}, u32[]{:S(2)}) collective-permute-start(bf16[256,128]{1,0:T(8,128)(2,1)S(1)} %get-tuple-element.12), channel_id=1, source_target_pairs={{0,192},{1,224},{2,128},{3,160},{4,400},{5,432},{6,464},{7,496},{8... | collective-permute-start | bytes 196616 | tf_op jit(solution)/shard_map/ppermute | solution.py:236
  44.2 1.0 dense.1.refs_0_
  45.2 4.5 %all_to_all.32.refs_1_ = bf16[2,4,256,128]{3,2,1,0:T(8,128)(2,1)S(1)} all-to-all(bf16[2,4,256,128]{3,2,1,0:T(8,128)(2,1)S(1)} %get-tuple-element.11), channel_id=1, replica_groups=mesh['zl'=4,'x'=4,'zh'=4,'y'=4,'c'=2] {'c'}, dimensions={0} | all-to-all | bytes 1048576 | tf_op jit(solution)/shard_map/all_to_all | solution.py:199
  49.7 1.5 %forward.1 = bf16[16,80,128]{2,1,0:T(8,128)(2,1)S(1)} custom-call(bf16[1024,2048]{1,0:T(8,128)(2,1)S(1)} %dense.1.refs_0_, bf16[2,4,256,128]{3,2,1,0:T(8,128)(2,1)S(1)} %all_to_all.32.refs_1_, bf16[1024,256]{1,0:T(8,128)(2,1)S(1)} %copy-done.2), custom_call_target="tpu_custom_call" | custom-call | flops 603979776 | bytes 3145728 | tf_op jit(solution)/shard_map/forward/pallas_call | solution.py:242
  51.2 0.9 collective-permute-done.1
  52.2 20.9 %all_to_all.33.parts = bf16[16,96,128]{2,1,0:T(8,128)(2,1)S(1)} all-to-all(bf16[16,96,128]{2,1,0:T(8,128)(2,1)S(1)} %pad_maximum_fusion), channel_id=1, replica_groups=mesh['zl'=4,'x'=4,'zh'=4,'y'=4,'c'=2] {'zl','x'}, dimensions={0} | all-to-all | bytes 786432 | tf_op jit(solution)/shard_map/all_to_all | solution.py:199
  73.0 0.1 reduce.1
  73.1 23.5 %all_to_all.34.weight_parts = bf16[32,16,128]{2,1,0:T(8,128)(2,1)S(1)} all-to-all(bf16[32,16,128]{2,1,0:T(8,128)(2,1)S(1)} %get-tuple-element.14), channel_id=1, replica_groups=mesh['zl'=4,'x'=4,'zh'=4,'y'=4,'c'=2] {'zh','y','c'}, dimensions={0} | all-to-all | bytes 262144 | tf_op jit(solution)/shard_map/all_to_all | solution.py:199
  96.6 0.1 gather.1
  96.7 22.5 %all_to_all.35.received = bf16[16,144,128]{2,1,0:T(8,128)(2,1)S(1)} all-to-all(bf16[16,144,128]{2,1,0:T(8,128)(2,1)S(1)} %gather.1), channel_id=1, replica_groups=mesh['zl'=4,'x'=4,'zh'=4,'y'=4,'c'=2] {'zl','x'}, dimensions={0} | all-to-all | bytes 1179648 | tf_op jit(solution)/shard_map/all_to_all | solution.py:199
  119.3 1.1 output.1
  (8 shorter events, 0.0 us)
Async XLA Ops:
  0.6 1.0 copy-start
  0.6 43.5 %copy-start.5 = (s32[1,1,96]{2,1,0:T(1,128)S(1)}, s32[1,1,96]{2,1,0:T(1,128)}, u32[]{:S(2)}) copy-start(s32[1,1,96]{2,1,0:T(1,128)} %param.9) | copy-start | bytes 1156
  0.7 43.5 %copy-start.4 = (s32[1,1,8]{2,1,0:T(1,128)S(1)}, s32[1,1,8]{2,1,0:T(1,128)}, u32[]{:S(2)}) copy-start(s32[1,1,8]{2,1,0:T(1,128)} %param.8) | copy-start | bytes 100
  0.7 43.5 %copy-start.1 = (bf16[1,1,96,128,128]{4,3,2,1,0:T(8,128)(2,1)S(1)}, bf16[1,1,96,128,128]{4,3,2,1,0:T(8,128)(2,1)}, u32[]{:S(2)}) copy-start(bf16[1,1,96,128,128]{4,3,2,1,0:T(8,128)(2,1)} %param.7) | copy-start | bytes 9437188
  1.6 24.2 %collective-permute-start = (bf16[256,128]{1,0:T(8,128)(2,1)S(1)}, bf16[256,128]{1,0:T(8,128)(2,1)S(1)}, u32[]{:S(2)}, u32[]{:S(2)}) collective-permute-start(bf16[256,128]{1,0:T(8,128)(2,1)S(1)} %constant_dynamic-slice_fusion), channel_id=1, source_target_pairs={{192,0},{224,1},{128,2},{160,3},{400,4},{432,5},{464,6},{496,7},{3... | collective-permute-start | bytes 196616 | tf_op jit(solution)/shard_map/ppermute | solution.py:228
  38.0 11.7 %copy-start.2 = (bf16[1024,256]{1,0:T(8,128)(2,1)S(1)}, bf16[1024,256]{1,0:T(8,128)(2,1)}, u32[]{:S(2)}) copy-start(bf16[1024,256]{1,0:T(8,128)(2,1)} %refs_2_.1) | copy-start | bytes 1572868
  38.0 14.1 %collective-permute-start.1 = (bf16[256,128]{1,0:T(8,128)(2,1)S(1)}, bf16[256,128]{1,0:T(8,128)(2,1)S(1)}, u32[]{:S(2)}, u32[]{:S(2)}) collective-permute-start(bf16[256,128]{1,0:T(8,128)(2,1)S(1)} %get-tuple-element.12), channel_id=1, source_target_pairs={{0,192},{1,224},{2,128},{3,160},{4,400},{5,432},{6,464},{7,496},{8... | collective-permute-start | bytes 196616 | tf_op jit(solution)/shard_map/ppermute | solution.py:236
  49.7 69.6 %copy-start.3 = (bf16[128,256]{1,0:T(8,128)(2,1)S(1)}, bf16[128,256]{1,0:T(8,128)(2,1)}, u32[]{:S(2)}) copy-start(bf16[128,256]{1,0:T(8,128)(2,1)} %weight.1) | copy-start | bytes 196612

commit v13 on v12

--- a/solution.py
+++ b/solution.py
@@ -118,12 +118,9 @@
         held[c] = received[:, 0:256, :]
 
 
-def dense_kernel(counts, cols, tiles, dense):
+def forward_kernel(scaling, counts, cols, tiles, held, node_grad, message, dense, total):
     for _ in fill(counts, cols, tiles, dense):
         pass
-
-
-def forward_kernel(scaling, dense, held, node_grad, message, total):
     for k in range(8):
         term = jnp.dot(
             dense[:, k * 256 : (k + 1) * 256], held[k % 2, k // 2], preferred_element_type=F32
@@ -234,20 +231,16 @@
         split_kernel, "split", (shape(2, 4, 256, 128), shape(256, 128)), [VMEM]
     )(received)
     column_sum = lax.ppermute(column_sum, REP + ROW, [(d, s) for s, d in PAIRS])
-    dense = call(dense_kernel, "dense", shape(1024, 2048), [SMEM, SMEM, VMEM])(
-        counts, cols, tiles
-    )
-    held, dense = lax.optimization_barrier((held, dense))
     held = exchange(held, "c")
     message = call(
         lambda *refs: forward_kernel(scaling, *refs),
         "forward",
         shape(16, 80, 128),
-        [VMEM] * 3,
-        [pltpu.VMEM((1024, 128), F32)],
+        [SMEM, SMEM] + [VMEM] * 3,
+        [pltpu.VMEM((1024, 2048), BF16), pltpu.VMEM((1024, 128), F32)],
         flops=2 * 128 * 1024 * 2304,
         moved=3 << 20,
-    )(dense, held, node_grad)
+    )(counts, cols, tile_values[0, 0], held, node_grad)
     message = jnp.concatenate([message, column_sum.reshape(16, 16, 128)], axis=1)
     parts = exchange(message, REP)
 

time: 122 us -> 122 us (level)
  no operation moved by 1% of the time
where the time goes in v13:
time: 122 us; the launch traced here: 120 us
  blocking collectives  88.5 us (73%)
  starting transfers between devices  20.4 us (17%)
  Pallas kernels  8.35 us (7%)
  waiting for transfers between devices  1.28 us (1%)
    all_to_all x6, blocking collectives, exchange(): return lax.all_to_all(block, axes, 0, 0)  88.5 us
    ppermute x1, starting transfers between devices, body(): quarter = lax.ppermute(quarter, REP + ROW, PAIRS)  14.4 us
    ppermute x1, starting transfers between devices, body(): column_sum = lax.ppermute(column_sum, REP + ROW, [(d, s) for s, d in PAIRS])  6.04 us
    pallas_call x1, Pallas kernels, body(): call(backward_kernel, 'backward', shape(2, 4, 256, 128), [SMEM, SMEM, HBM...  4.4 us
    pallas_call x1, Pallas kernels, body(): call(lambda *refs: forward_kernel(scaling, *refs), 'forward', shape(16, 8...  2.5 us
  transfers between devices with their start and end apart: 2, of which 1 were waited for; matrix products, arithmetic and copies ran while one was open for 0% of the time, Pallas kernels for 6%

profile of v13, /device:TPU:24, one launch (start us, length us, event | category | flops | bytes accessed | tf_op | source)
XLA Modules:
  0.0 120.3 jit_solution(11208419145803795009)
XLA Ops:
  0.6 0.0 copy-start
  0.7 0.9 copy-done
  1.6 14.4 %collective-permute-start = (bf16[256,128]{1,0:T(8,128)(2,1)S(1)}, bf16[256,128]{1,0:T(8,128)(2,1)S(1)}, u32[]{:S(2)}, u32[]{:S(2)}) collective-permute-start(bf16[256,128]{1,0:T(8,128)(2,1)S(1)} %constant_dynamic-slice_fusion), channel_id=1, source_target_pairs={{192,0},{224,1},{128,2},{160,3},{400,4},{432,5},{464,6},{496,7},{3... | collective-permute-start | bytes 196616 | tf_op jit(solution)/shard_map/ppermute | solution.py:225
  16.0 4.4 %backward.1 = bf16[2,4,256,128]{3,2,1,0:T(8,128)(2,1)} custom-call(s32[8]{0:T(128)} %bitcast.7, s32[96]{0:T(128)} %bitcast.9, bf16[96,128,128]{2,1,0:T(8,128)(2,1)} %bitcast.5, bf16[1024,256]{1,0:T(8,128)(2,1)} %refs_4_.1, bf16[128,256]{1,0:T(8,128)(2,1)} %weight.1), custom_call_target="tpu_custom_call" | custom-call | flops 603979776 | bytes 8388608 | tf_op jit(solution)/shard_map/backward/pallas_call | solution.py:206
  20.4 0.0 copy-start.1
  20.4 0.0 copy-start.2
  20.4 0.0 copy-start.4
  20.4 0.0 copy-start.5
  20.4 5.5 %all_to_all.30.terms = bf16[2,4,256,128]{3,2,1,0:T(8,128)(2,1)S(1)} all-to-all(bf16[2,4,256,128]{3,2,1,0:T(8,128)(2,1)} %backward.1), channel_id=1, replica_groups=mesh['zl'=4,'x'=4,'zh'=4,'y'=4,'c'=2] {'c'}, dimensions={0} | all-to-all | bytes 1048576 | tf_op jit(solution)/shard_map/all_to_all | solution.py:196
  25.9 0.0 collective-permute-done.quarter
  25.9 0.1 pack.1
  26.0 12.0 %all_to_all.31.received = bf16[4,512,128]{2,1,0:T(8,128)(2,1)S(1)} all-to-all(bf16[4,512,128]{2,1,0:T(8,128)(2,1)S(1)} %pack.1), channel_id=1, replica_groups=mesh['zl'=4,'x'=4,'zh'=4,'y'=4,'c'=2] {'y'}, dimensions={0} | all-to-all | bytes 1048576 | tf_op jit(solution)/shard_map/all_to_all | solution.py:196
  38.0 0.1 split.1
  38.1 6.0 %collective-permute-start.1 = (bf16[256,128]{1,0:T(8,128)(2,1)S(1)}, bf16[256,128]{1,0:T(8,128)(2,1)S(1)}, u32[]{:S(2)}, u32[]{:S(2)}) collective-permute-start(bf16[256,128]{1,0:T(8,128)(2,1)S(1)} %get-tuple-element.8), channel_id=1, source_target_pairs={{0,192},{1,224},{2,128},{3,160},{4,400},{5,432},{6,464},{7,496},{8... | collective-permute-start | bytes 196616 | tf_op jit(solution)/shard_map/ppermute | solution.py:233
  44.2 4.2 %all_to_all.32.refs_3_ = bf16[2,4,256,128]{3,2,1,0:T(8,128)(2,1)S(1)} all-to-all(bf16[2,4,256,128]{3,2,1,0:T(8,128)(2,1)S(1)} %get-tuple-element.7), channel_id=1, replica_groups=mesh['zl'=4,'x'=4,'zh'=4,'y'=4,'c'=2] {'c'}, dimensions={0} | all-to-all | bytes 1048576 | tf_op jit(solution)/shard_map/all_to_all | solution.py:196
  48.3 2.5 %forward.1 = bf16[16,80,128]{2,1,0:T(8,128)(2,1)S(1)} custom-call(s32[8]{0:T(128)S(1)} %bitcast.8, s32[96]{0:T(128)S(1)} %bitcast.10, bf16[96,128,128]{2,1,0:T(8,128)(2,1)S(1)} %bitcast.6, bf16[2,4,256,128]{3,2,1,0:T(8,128)(2,1)S(1)} %all_to_all.32.refs_3_, bf16[1024,256]{1,0:T(8,128)(2,1)S(1)} %copy-done.2), custom_call_target="tpu_custom_call" | custom-call | flops 603979776 | bytes 3145728 | tf_op jit(solution)/shard_map/forward/pallas_call | solution.py:235
  50.9 0.0 copy-start.3
  50.9 1.3 %collective-permute-done.1 = bf16[256,128]{1,0:T(8,128)(2,1)S(1)} collective-permute-done((bf16[256,128]{1,0:T(8,128)(2,1)S(1)}, bf16[256,128]{1,0:T(8,128)(2,1)S(1)}, u32[]{:S(2)}, u32[]{:S(2)}) %collective-permute-start.1) | collective-permute-done | bytes 65568 | tf_op jit(solution)/shard_map/ppermute | solution.py:233
  52.2 20.9 %all_to_all.33.parts = bf16[16,96,128]{2,1,0:T(8,128)(2,1)S(1)} all-to-all(bf16[16,96,128]{2,1,0:T(8,128)(2,1)S(1)} %pad_maximum_fusion), channel_id=1, replica_groups=mesh['zl'=4,'x'=4,'zh'=4,'y'=4,'c'=2] {'zl','x'}, dimensions={0} | all-to-all | bytes 786432 | tf_op jit(solution)/shard_map/all_to_all | solution.py:196
  73.1 0.1 reduce.1
  73.2 23.4 %all_to_all.34.weight_parts = bf16[32,16,128]{2,1,0:T(8,128)(2,1)S(1)} all-to-all(bf16[32,16,128]{2,1,0:T(8,128)(2,1)S(1)} %get-tuple-element.10), channel_id=1, replica_groups=mesh['zl'=4,'x'=4,'zh'=4,'y'=4,'c'=2] {'zh','y','c'}, dimensions={0} | all-to-all | bytes 262144 | tf_op jit(solution)/shard_map/all_to_all | solution.py:196
  96.6 0.1 gather.1
  96.7 22.5 %all_to_all.35.received = bf16[16,144,128]{2,1,0:T(8,128)(2,1)S(1)} all-to-all(bf16[16,144,128]{2,1,0:T(8,128)(2,1)S(1)} %gather.1), channel_id=1, replica_groups=mesh['zl'=4,'x'=4,'zh'=4,'y'=4,'c'=2] {'zl','x'}, dimensions={0} | all-to-all | bytes 1179648 | tf_op jit(solution)/shard_map/all_to_all | solution.py:196
  119.2 1.1 output.1
  (7 shorter events, 0.0 us)
Async XLA Ops:
  0.6 1.0 copy-start
  1.6 24.4 %collective-permute-start = (bf16[256,128]{1,0:T(8,128)(2,1)S(1)}, bf16[256,128]{1,0:T(8,128)(2,1)S(1)}, u32[]{:S(2)}, u32[]{:S(2)}) collective-permute-start(bf16[256,128]{1,0:T(8,128)(2,1)S(1)} %constant_dynamic-slice_fusion), channel_id=1, source_target_pairs={{192,0},{224,1},{128,2},{160,3},{400,4},{432,5},{464,6},{496,7},{3... | collective-permute-start | bytes 196616 | tf_op jit(solution)/shard_map/ppermute | solution.py:225
  20.4 27.9 %copy-start.1 = (bf16[1,1,96,128,128]{4,3,2,1,0:T(8,128)(2,1)S(1)}, bf16[1,1,96,128,128]{4,3,2,1,0:T(8,128)(2,1)}, u32[]{:S(2)}) copy-start(bf16[1,1,96,128,128]{4,3,2,1,0:T(8,128)(2,1)} %param.7) | copy-start | bytes 9437188
  20.4 27.9 %copy-start.2 = (bf16[1024,256]{1,0:T(8,128)(2,1)S(1)}, bf16[1024,256]{1,0:T(8,128)(2,1)}, u32[]{:S(2)}) copy-start(bf16[1024,256]{1,0:T(8,128)(2,1)} %refs_4_.1) | copy-start | bytes 1572868
  20.4 27.9 %copy-start.4 = (s32[1,1,8]{2,1,0:T(1,128)S(1)}, s32[1,1,8]{2,1,0:T(1,128)}, u32[]{:S(2)}) copy-start(s32[1,1,8]{2,1,0:T(1,128)} %param.8) | copy-start | bytes 100
  20.4 27.9 %copy-start.5 = (s32[1,1,96]{2,1,0:T(1,128)S(1)}, s32[1,1,96]{2,1,0:T(1,128)}, u32[]{:S(2)}) copy-start(s32[1,1,96]{2,1,0:T(1,128)} %param.9) | copy-start | bytes 1156
  38.1 14.0 %collective-permute-start.1 = (bf16[256,128]{1,0:T(8,128)(2,1)S(1)}, bf16[256,128]{1,0:T(8,128)(2,1)S(1)}, u32[]{:S(2)}, u32[]{:S(2)}) collective-permute-start(bf16[256,128]{1,0:T(8,128)(2,1)S(1)} %get-tuple-element.8), channel_id=1, source_target_pairs={{0,192},{1,224},{2,128},{3,160},{4,400},{5,432},{6,464},{7,496},{8... | collective-permute-start | bytes 196616 | tf_op jit(solution)/shard_map/ppermute | solution.py:233
  50.9 68.3 %copy-start.3 = (bf16[128,256]{1,0:T(8,128)(2,1)S(1)}, bf16[128,256]{1,0:T(8,128)(2,1)}, u32[]{:S(2)}) copy-start(bf16[128,256]{1,0:T(8,128)(2,1)} %weight.1) | copy-start | bytes 196612
